TPU v7x, 32 devices: a whole 2x2x4 slice. The times are simulated.
32 devices in a mesh: gx: 8 (over y, x, core), gy: 4 (over z).
Axes of the slice: x: 2, y: 2, z: 4, core: 2. Of those that a mesh axis runs over, the one named last changes fastest.
Arguments:
- leaf_maps: float32 [8, 4, 1024, 1024], P('gx', 'gy'), may hold values from -8 to 40, as said below
- edge_data: float32 [8, 4, 512, 1024], P('gx', 'gy'), may hold values from -6 to 6
Outputs:
- potential: float32 [8, 4, 1024, 1024], P('gx', 'gy')
- flux: float32 [8, 4, 1024, 1024], P('gx', 'gy')
Inputs may be any that keep to these rules, and one draw needn't show every extreme that they name: `leaf_maps`: each leaf's map is exactly symmetric and positive definite.
All inputs are finite; a program needn't handle non-finite values.
Results may differ from a plain program's by a relative error of at most 0.0003.
Values sent between devices are 32-bit elements; how exact they have to be, the bound alone decides.
No kernel may reach another device: no remote copies, remote signals or barrier semaphores. Data moves between devices by JAX's collectives and lax.ppermute only.
A program may use at most 128 MiB of HBM per device.

v0:
```python
import functools

import jax
import jax.numpy as jnp
from jax import lax
from jax.experimental import pallas as pl
from jax.experimental.pallas import tpu as pltpu
from jax.sharding import PartitionSpec as P

HIGHEST = lax.Precision.HIGHEST
F32 = jnp.float32
BF16 = jnp.bfloat16
LANES = 128
PANEL = 8
TURN = 4


def exchange(block, axis):
    half = lax.axis_size(axis) // 2
    return lax.ppermute(block, axis, [(i, i ^ half) for i in range(2 * half)])


def side(axis):
    return (lax.axis_index(axis) >= lax.axis_size(axis) // 2).astype(jnp.int32)


def edges():
    c, r = side("gx"), side("gy")
    return 1 - c, c, 3 - r, 2 + r


def contract(left, right, dims):
    return lax.dot_general(left, right, ((dims[:1], dims[1:]), ((), ())), precision=HIGHEST, preferred_element_type=F32)


def full_nn(left, right):
    return contract(left, right, (1, 0))


def full_nt(left, right):
    return contract(left, right, (1, 1))


def full_tn(left, right):
    return contract(left, right, (0, 0))


def split(values):
    high = values.astype(BF16)
    return high, (values - high.astype(F32)).astype(BF16)


def half_dot(left, right):
    return jnp.dot(left, right, preferred_element_type=F32)


def triple(left, right):
    (lh, ll), (rh, rl) = left, right
    return half_dot(lh, rh) + (half_dot(lh, rl) + half_dot(ll, rh))


def tree(terms):
    while len(terms) > 1:
        terms = [a + b for a, b in zip(terms[::2], terms[1::2])]
    return terms[0]


def entry(i, j):
    return (i, j) if i >= j else (j, i)


def invert_panel(s):
    s = dict(s)
    for k in range(PANEL):
        inverse = 1.0 / s[k, k]
        rest = [i for i in range(PANEL) if i != k]
        column = {i: s[entry(i, k)] for i in rest}
        scaled = {i: column[i] * inverse for i in rest}
        for i in rest:
            for j in rest:
                if j <= i:
                    s[i, j] = s[i, j] - scaled[i] * column[j]
        for i in rest:
            s[entry(i, k)] = scaled[i]
        s[k, k] = -inverse
    return {key: -value for key, value in s.items()}


def invert_tile(tile):
    shape = (PANEL, LANES)
    lane = lax.broadcasted_iota(jnp.int32, shape, 1)
    sub = lax.broadcasted_iota(jnp.int32, shape, 0)
    count = LANES // PANEL

    def turn(_, rows):
        rows = list(rows)
        for q in range(TURN):
            start = PANEL * q
            panel = rows[q]
            columns = [jnp.broadcast_to(panel[:, start + j : start + j + 1], shape) for j in range(PANEL)]
            s = {(i, j): jnp.broadcast_to(columns[j][i : i + 1, :], shape) for i in range(PANEL) for j in range(i + 1)}
            inverse = invert_panel(s)
            inside = (lane >= start) & (lane < start + PANEL)
            unit = jnp.where(inside, jnp.where(lane - start == sub, 1.0, 0.0), panel)
            wide = [jnp.broadcast_to(unit[j : j + 1, :], shape) for j in range(PANEL)]
            swept = [tree([inverse[entry(i, j)] * wide[j] for j in range(PANEL)]) for i in range(PANEL)]
            new = swept[0]
            for i in range(1, PANEL):
                new = jnp.where(sub == i, swept[i], new)
            for p in [*range(q + 1, count), *range(q)]:
                row = rows[p]
                terms = [jnp.broadcast_to(row[:, start + j : start + j + 1], shape) * swept[j] for j in range(PANEL)]
                rows[p] = jnp.where(inside, 0.0, row) - tree(terms)
            rows[q] = new
        return tuple(pltpu.roll(row, LANES - PANEL * TURN, 1) for row in rows[TURN:] + rows[:TURN])

    rows = tuple(tile[PANEL * i : PANEL * (i + 1), :] for i in range(count))
    return jnp.concatenate(lax.fori_loop(0, count // TURN, turn, rows), 0)


def invert(matrix):
    size = matrix.shape[0]
    if size == LANES:
        return invert_tile(matrix)
    half = size // 2
    first, cross, last = matrix[:half, :half], matrix[:half, half:], matrix[half:, half:]
    head = invert(first)
    reach = full_nn(head, cross)
    tail = invert(last - full_tn(cross, reach))
    return join(head, reach, tail)


def join(head, reach, tail):
    corner = full_nn(reach, tail)
    top = jnp.concatenate([head + full_nt(corner, reach), -corner], 1)
    return jnp.concatenate([top, jnp.concatenate([-corner.T, tail], 1)], 0)


def unpack(packed):
    h = packed.shape[1] // 2
    low = jnp.concatenate([packed[h:, :h], packed[h:, h:]], 0)
    return jnp.concatenate(
        [jnp.concatenate([packed[:h, :h], low.T], 1), jnp.concatenate([low, packed[:h, h:]], 1)], 0
    )


def quarters(leaf, n, a, b):
    h = n // 2

    def block(row, rows, col):
        return leaf.at[pl.ds(pl.multiple_of(a * n + row, h // 2), rows), pl.ds(pl.multiple_of(b * n + col, h), h)]

    return block


def fetch(moves, sems):
    copies = [pltpu.make_async_copy(a, b, sems.at[k]) for k, (a, b) in enumerate(moves)]
    for copy in copies:
        copy.start()
    for copy in copies:
        copy.wait()


def symmetric(leaf, e, out, base):
    n = out.shape[1]
    h = n // 2
    block = quarters(leaf, n, e, e)
    return [
        (block(0, h, 0), out.at[pl.ds(base, h), pl.ds(0, h)]),
        (block(h, h, h), out.at[pl.ds(base, h), pl.ds(h, h)]),
        (block(h, h // 2, 0), out.at[pl.ds(base + h, h // 2), pl.ds(0, h)]),
        (block(h + h // 2, h // 2, 0), out.at[pl.ds(base + h, h // 2), pl.ds(h, h)]),
    ]


def joined_kernel(leaf, out, sems):
    fetch(symmetric(leaf, edges()[0], out, 0), sems)


def crossing_kernel(leaf, out, sems):
    n = out.shape[1]
    i, _, y, _ = edges()
    whole = leaf.at[pl.ds(pl.multiple_of(y * n, n), n), pl.ds(pl.multiple_of(i * n, n), n)]
    fetch([(whole, out.at[pl.ds(0, n)])] + symmetric(leaf, y, out, n), sems)


def passing_kernel(middle, middle_z, out):
    n = out.shape[1]
    out[:n] = middle[:n]
    out[n : 2 * n] = middle_z[:n]
    out[2 * n :] = middle[n:] + middle_z[n:]


def sum_kernel(own, other, out):
    out[...] = own[...] + other[...]


def outer_rows(leaf, edge, rows, sems):
    n = rows.shape[0]
    _, x, _, d = edges()
    own = pl.ds(pl.multiple_of(edge * n, n), n)
    return [
        pltpu.make_async_copy(leaf.at[own, pl.ds(pl.multiple_of(e * n, n), n)], rows.at[:, pl.ds(p * n, n)], sems.at[p])
        for p, e in enumerate((x, d))
    ]


def side_kernel(base, leaf, data, out, rows, held, sems):
    copies = outer_rows(leaf, edges()[0], rows, sems)
    copies.append(pltpu.make_async_copy(data.at[:, pl.ds(base, held.shape[1])], held, sems.at[2]))
    for copy in copies:
        copy.start()
    for copy in copies:
        copy.wait()
    out[...] = triple(split(rows[...]), split(held[...]))


def known_kernel(leaf, data, flux, high, low, potential, data_high, data_low, sems):
    step = pl.program_id(0)
    n = leaf.shape[0]
    i, x, y, d = edges()
    copies = [
        pltpu.make_async_copy(data.at[pl.ds(p * n, n), :], potential.at[pl.ds(pl.multiple_of(e * n, n), n), :], sems.at[p])
        for p, e in enumerate((x, d))
    ]

    @pl.when(step == 0)
    def _():
        for copy in copies:
            copy.start()
        data_high[...], data_low[...] = split(data[...])

    cols = lambda e: leaf[:, pl.ds(pl.multiple_of(e * n, n), n)]
    unknown = split(jnp.concatenate([cols(i), cols(y)], 1))
    high[...], low[...] = unknown
    outer = split(jnp.concatenate([cols(x), cols(d)], 1))
    flux[...] = triple(outer, (data_high[...], data_low[...]))

    @pl.when(step == pl.num_programs(0) - 1)
    def _():
        for copy in copies:
            copy.wait()


def first_kernel(joined, joined_far, middle, inverse, across, half):
    n = inverse.shape[0]
    h = n // 2
    solved = invert(unpack(joined[...] + joined_far[...]))
    inverse[...] = solved
    across[...] = full_nt(solved, middle[:n])

    def fill(diagonal, low):
        half[:h] = diagonal
        half[h:] = low

    @pl.when(side("gx") == 0)
    def _():
        fill(solved[:h, :h], solved[h : h + h // 2, :h])

    @pl.when(side("gx") == 1)
    def _():
        fill(solved[h:, h:], solved[h + h // 2 :, :h])


def middle_kernel(base, offset, widths, leaf, data, own, far, across, inverse, *rest):
    outs, (start, rows, held, sems) = rest[:-4], rest[-4:]
    width = sum(widths)
    copies = outer_rows(leaf, edges()[2], rows, sems)
    copies.append(pltpu.make_async_copy(data.at[:, pl.ds(base, width)], held, sems.at[2]))
    for copy in copies:
        copy.start()
    right = split(own[:, offset : offset + width] + far[:, offset : offset + width])
    start[...] = -triple(split(inverse[...]), right)
    out = triple(split(across[...].T), right)
    for copy in copies:
        copy.wait()
    out = triple(split(rows[...]), split(held[...])) - out
    done = 0
    for ref, part in zip(outs, widths):
        ref[...] = out[:, done : done + part]
        done += part


def build_kernel(middle, middle_z, passed, inverse, half_z, half_x, across, across_far, own, off, far, other):
    n = inverse.shape[0]
    h = n // 2

    def fill(one, two):
        low = jnp.concatenate([one[h:], two[h:]], 0)
        other[:h, :h] = one[:h]
        other[h:, h:] = two[:h]
        other[h:, :h] = low
        other[:h, h:] = low.T

    @pl.when(side("gx") == 0)
    def _():
        fill(half_z, half_x)

    @pl.when(side("gx") == 1)
    def _():
        fill(half_x, half_z)

    q_far = full_nt(inverse[...], passed[:n])
    across_far[...] = q_far
    q_own = across[...]
    p_own = full_nt(other[...], middle_z[:n])
    p_far = full_nt(other[...], passed[n : 2 * n])
    own[...] = unpack(middle[n:] + middle_z[n:]) - (full_nn(middle[:n], q_own) + full_nn(middle_z[:n], p_own))
    off[...] = -(full_nn(middle[:n], q_far) + full_nn(middle_z[:n], p_far))
    far[...] = unpack(passed[2 * n :]) - (full_nn(passed[:n], q_far) + full_nn(passed[n : 2 * n], p_far))


def open_half(matrix, head, reach, rest):
    h = matrix.shape[0] // 2
    solved = invert(matrix[:h, :h])
    head[...] = solved
    reach[...] = full_nn(solved, matrix[:h, h:])
    rest[...] = matrix[h:, h:] - full_tn(matrix[:h, h:], reach[...])


def head_kernel(matrix, head, reach, rest):
    open_half(matrix, head, reach, rest)


def turn_kernel(head, reach, rest, off, far, done, wide, left):
    done[...] = join(head[...], reach[...], invert(rest[...]))
    wide[...] = full_nn(done[...], off[...])
    left[...] = far[...] - full_tn(off[...], wide[...])


def tail_kernel(head, reach, rest, done, wide, out):
    out[...] = join(done[...], wide[...], join(head[...], reach[...], invert(rest[...])))


def beside(parts):
    return jnp.concatenate([part[...] for part in parts], 1)


def last_kernel(count, base, offset, inverse2, across, across_far, high, low, *rest):
    w_own, w_far, start = rest[:count], rest[count : 2 * count], rest[2 * count : 3 * count]
    _, _, flux, potential, solved, known, sems = rest[3 * count :]
    n = across.shape[0]
    width = solved.shape[1]
    i, _, y, _ = edges()
    cols = pl.ds(base, width)
    load = pltpu.make_async_copy(flux.at[:, cols], known, sems.at[2])
    load.start()
    top = triple(split(inverse2[...]), split(jnp.concatenate([beside(w_own), beside(w_far)], 0)))
    left = split(jnp.concatenate([across[...], across_far[...]], 1))
    solved[:n] = beside(start)[:, offset : offset + width] + triple(left, split(top))
    solved[n:] = -top[:n]
    copies = [
        pltpu.make_async_copy(
            solved.at[pl.ds(p * n, n), :], potential.at[pl.ds(pl.multiple_of(e * n, n), n), cols], sems.at[p]
        )
        for p, e in enumerate((i, y))
    ]
    for copy in copies:
        copy.start()
    load.wait()
    known[...] += triple((high[...], low[...]), split(solved[...]))
    store = pltpu.make_async_copy(known, flux.at[:, cols], sems.at[2])
    store.start()
    for copy in copies + [store]:
        copy.wait()


def array(*shape, dtype=F32):
    return jax.ShapeDtypeStruct(shape, dtype)


ANY = pl.BlockSpec(memory_space=pl.ANY)
HBM = pl.BlockSpec(memory_space=pltpu.HBM)
WHOLE = pl.BlockSpec(memory_space=pltpu.VMEM)
MIB = 1 << 20


COSTS = {
    "crossing": 0.1,
    "joined": 0.1,
    "side": 1.0,
    "first": 11.0,
    "middle": 1.3,
    "passing": 0.1,
    "known": 6.0,
    "build": 3.0,
    "head": 5.4,
    "turn": 6.5,
    "tail": 6.6,
    "total": 0.1,
    "last": 5.0,
}


class Chain:
    def __init__(self):
        self.mark = None

    def __call__(self, name, kernel, outs, *args, ins=None, out_specs=None, scratch=(), aliases=None, limit=24, **kwargs):
        cost = COSTS[name]
        ins = ins or [WHOLE] * len(args)
        out_specs = out_specs or [WHOLE] * len(outs)
        marks = [] if self.mark is None else [self.mark]

        def body(*refs):
            inner = refs[: len(args)] + refs[len(args) + len(marks) :]
            kernel(*inner[: len(args) + len(outs)], *inner[len(args) + len(outs) + 1 :])

        *given, self.mark = pl.pallas_call(
            body,
            out_shape=list(outs) + [array(8, LANES)],
            in_specs=list(ins) + [HBM] * len(marks),
            out_specs=list(out_specs) + [HBM],
            scratch_shapes=list(scratch),
            input_output_aliases=aliases or {},
            compiler_params=pltpu.CompilerParams(vmem_limit_bytes=limit * MIB),
            cost_estimate=pl.CostEstimate(flops=int(cost * 1e9), bytes_accessed=int(cost * 3e6), transcendentals=0),
            name=name,
            **kwargs,
        )(*args, *marks)
        return given[0] if len(given) == 1 else given


def per_device(leaf_maps, edge_data):
    leaf = leaf_maps[0, 0]
    data = edge_data[0, 0]
    full, count = leaf.shape[0], data.shape[1]
    n = full // 4
    h = n // 2
    packed = 3 * n // 4
    dma = pltpu.SemaphoreType.DMA
    call = Chain()
    unit = count // 8
    widths = [2 * unit, 3 * unit, 2 * unit, unit]
    bases = [0, 2 * unit, 5 * unit, 7 * unit]
    cut = 5 * unit

    middle = call("crossing", crossing_kernel, [array(n + packed, n)], leaf, ins=[ANY], scratch=[dma((5,))])
    middle_z = exchange(middle, "gy")
    joined = call("joined", joined_kernel, [array(packed, n)], leaf, ins=[ANY], scratch=[dma((4,))])
    joined_far = exchange(joined, "gx")

    def sides(base, width):
        own = call(
            "side",
            functools.partial(side_kernel, base),
            [array(n, width)],
            leaf,
            data,
            ins=[ANY] * 2,
            scratch=[pltpu.VMEM((n, 2 * n), F32), pltpu.VMEM((2 * n, width), F32), dma((3,))],
        )
        return own, exchange(own, "gx")

    def middles(parts, offset, own, far):
        base, width = bases[parts[0]], sum(widths[k] for k in parts)
        given = call(
            "middle",
            functools.partial(middle_kernel, base, base - offset, [widths[k] for k in parts]),
            [array(n, widths[k]) for k in parts] + [array(n, width)],
            leaf,
            data,
            own,
            far,
            across,
            inverse1,
            ins=[ANY] * 2 + [WHOLE] * 4,
            scratch=[pltpu.VMEM((n, 2 * n), F32), pltpu.VMEM((2 * n, width), F32), dma((3,))],
        )
        return given[:-1], given[-1]

    def total(own, other):
        return call("total", sum_kernel, [array(*own.shape)], own, other)

    own_a, far_a = sides(0, cut)
    inverse1, across, half = call(
        "first", first_kernel, [array(n, n)] * 2 + [array(packed, h)], joined, joined_far, middle
    )
    half_z = exchange(half, "gy")
    (v0,), start0 = middles([0], 0, own_a, far_a)
    z0 = exchange(v0, "gy")
    passing = call("passing", passing_kernel, [array(2 * n + packed, n)], middle, middle_z)
    passed = exchange(passing, "gx")
    known, high, low, potential = call(
        "known",
        known_kernel,
        [
            array(full, count),
            array(full, 2 * n, dtype=BF16),
            array(full, 2 * n, dtype=BF16),
            array(full, count),
        ],
        leaf,
        data,
        ins=[pl.BlockSpec((n, full), lambda s: (s, 0)), pl.BlockSpec((2 * n, count), lambda s: (0, 0))],
        out_specs=[
            pl.BlockSpec((n, count), lambda s: (s, 0)),
            pl.BlockSpec((n, 2 * n), lambda s: (s, 0)),
            pl.BlockSpec((n, 2 * n), lambda s: (s, 0)),
            ANY,
        ],
        scratch=[pltpu.VMEM((2 * n, count), BF16), pltpu.VMEM((2 * n, count), BF16), dma((2,))],
        grid=(4,),
    )
    half_x = exchange(half_z, "gx")
    (v1,), start1 = middles([1], 0, own_a, far_a)
    z1 = exchange(v1, "gy")
    own_b, far_b = sides(cut, count - cut)
    across_far, s_own, s_off, s_far = call(
        "build",
        build_kernel,
        [array(n, n)] * 4,
        middle,
        middle_z,
        passed,
        inverse1,
        half_z,
        half_x,
        across,
        scratch=[pltpu.VMEM((n, n), F32)],
    )
    head, reach, rest = call("head", head_kernel, [array(h, h)] * 3, s_own)
    w0 = total(v0, z0)
    w0_far = exchange(w0, "gx")
    (v2, v3), start2 = middles([2, 3], cut, own_b, far_b)
    z2, z3 = exchange(v2, "gy"), exchange(v3, "gy")
    done, wide, left = call("turn", turn_kernel, [array(n, n)] * 3, head, reach, rest, s_off, s_far)
    w1 = total(v1, z1)
    w1_far = exchange(w1, "gx")
    head, reach, rest = call("head", head_kernel, [array(h, h)] * 3, left)
    inverse2 = call("tail", tail_kernel, [array(2 * n, 2 * n)], head, reach, rest, done, wide)
    w2 = total(v2, z2)
    w2_far = exchange(w2, "gx")
    w3 = total(v3, z3)
    w3_far = exchange(w3, "gx")

    flux = known
    groups = [
        ([0, 1], [w0, w1], [w0_far, w1_far], [start0, start1]),
        ([2], [w2], [w2_far], [start2]),
        ([3], [w3], [w3_far], [start2]),
    ]
    for parts, own, far, start in groups:
        base, width = bases[parts[0]], sum(widths[k] for k in parts)
        pieces = (*own, *far, *start)
        offset = widths[2] if parts == [3] else 0
        flux, potential = call(
            "last",
            functools.partial(last_kernel, len(parts), base, offset),
            [array(full, count), array(full, count)],
            inverse2,
            across,
            across_far,
            high,
            low,
            *pieces,
            flux,
            potential,
            ins=[WHOLE] * (5 + len(pieces)) + [ANY] * 2,
            out_specs=[ANY] * 2,
            scratch=[pltpu.VMEM((2 * n, width), F32), pltpu.VMEM((full, width), F32), dma((3,))],
            aliases={5 + len(pieces): 0, 6 + len(pieces): 1},
        )
    return potential[None, None], flux[None, None]


def solution(mesh):
    spec = P("gx", "gy", None, None)
    return jax.shard_map(per_device, mesh=mesh, in_specs=(spec, spec), out_specs=(spec, spec), check_vma=False)
```

profile of v0, /device:TPU:0, one launch (start us, length us, event | category | flops | bytes accessed | tf_op | source)
XLA Modules:
  0.0 111.2 jit_solution(16622857168286007213)
XLA Ops:
  0.6 0.0 copy-start
  0.6 2.2 %copy-done = f32[1,1,1024,1024]{3,2,1,0:T(8,128)S(1)} copy-done((f32[1,1,1024,1024]{3,2,1,0:T(8,128)S(1)}, f32[1,1,1024,1024]{3,2,1,0:T(8,128)}, u32[]{:S(2)}) %copy-start) | copy-done | bytes 4194328
  2.8 0.0 copy-start.2
  2.8 0.1 crossing.1
  2.9 0.1 joined.1
  3.0 3.0 %collective-permute-start.2 = (f32[192,256]{1,0:T(8,128)S(1)}, f32[192,256]{1,0:T(8,128)S(1)}, u32[]{:S(2)}, u32[]{:S(2)}) collective-permute-start(f32[192,256]{1,0:T(8,128)S(1)} %get-tuple-element.70.refs_0_), channel_id=1, source_target_pairs={{0,16},{4,20},{8,24},{12,28},{16,0},{20,4},{24,8},{28,12},{1,17},{... | collective-permute-start | bytes 589832 | tf_op jit(solution)/shard_map/ppermute | solution.py:20
  6.1 0.0 copy-done.2
  6.1 1.1 side.2
  7.1 1.4 %collective-permute-start.1 = (f32[256,640]{1,0:T(8,128)S(1)}, f32[256,640]{1,0:T(8,128)S(1)}, u32[]{:S(2)}, u32[]{:S(2)}) collective-permute-start(f32[256,640]{1,0:T(8,128)S(1)} %get-tuple-element.69.refs_2_), channel_id=1, source_target_pairs={{0,16},{4,20},{8,24},{12,28},{16,0},{20,4},{24,8},{28,12},{1,17},{... | collective-permute-start | bytes 1966088 | tf_op jit(solution)/shard_map/ppermute | solution.py:20
  8.5 2.6 %collective-permute-start = (f32[448,256]{1,0:T(8,128)S(1)}, f32[448,256]{1,0:T(8,128)S(1)}, u32[]{:S(2)}, u32[]{:S(2)}) collective-permute-start(f32[448,256]{1,0:T(8,128)S(1)} %get-tuple-element.66.refs_2_.refs_0_), channel_id=1, source_target_pairs={{0,2},{1,3},{2,0},{3,1},{4,6},{5,7},{6,4},{7,5},{8,10},{9,11},{10,... | collective-permute-start | bytes 1376264 | tf_op jit(solution)/shard_map/ppermute | solution.py:20
  11.1 0.7 collective-permute-done.2.refs_1_
  11.8 0.0 copy-start.1
  11.8 11.3 %first.1 = (f32[256,256]{1,0:T(8,128)S(1)}, f32[256,256]{1,0:T(8,128)S(1)}, f32[192,128]{1,0:T(8,128)S(1)}, f32[8,128]{1,0:T(8,128)S(1)}) custom-call(f32[192,256]{1,0:T(8,128)S(1)} %get-tuple-element.70.refs_0_, f32[192,256]{1,0:T(8,128)S(1)} %collective-permute-done.2.refs_1_, f32[448,256]{1,0:T(8,128)S(1)} %get-tuple-element.66.refs_2_.refs_0_, ...), custom_call_target="tpu_custom_call" | custom-call | flops 11000000512 | bytes 33000000 | tf_op jit(solution)/shard_map/first/pallas_call | solution.py:409
  23.2 3.2 %collective-permute-start.4 = (f32[192,128]{1,0:T(8,128)S(1)}, f32[192,128]{1,0:T(8,128)S(1)}, u32[]{:S(2)}, u32[]{:S(2)}) collective-permute-start(f32[192,128]{1,0:T(8,128)S(1)} %get-tuple-element.77), channel_id=1, source_target_pairs={{0,2},{1,3},{2,0},{3,1},{4,6},{5,7},{6,4},{7,5},{8,10},{9,11},{10,... | collective-permute-start | bytes 294920 | tf_op jit(solution)/shard_map/ppermute | solution.py:20
  26.3 9.1 %collective-permute-done.4.refs_4_ = f32[192,128]{1,0:T(8,128)S(1)} collective-permute-done((f32[192,128]{1,0:T(8,128)S(1)}, f32[192,128]{1,0:T(8,128)S(1)}, u32[]{:S(2)}, u32[]{:S(2)}) %collective-permute-start.4) | collective-permute-done | bytes 98336 | tf_op jit(solution)/shard_map/ppermute | solution.py:20
  35.4 0.5 collective-permute-start.5
  35.9 0.0 collective-permute-done.1.refs_3_
  35.9 0.0 copy-done.1
  35.9 1.3 %middle.3 = (f32[256,256]{1,0:T(8,128)S(1)}, f32[256,256]{1,0:T(8,128)S(1)}, f32[8,128]{1,0:T(8,128)S(1)}) custom-call(f32[1024,1024]{1,0:T(8,128)S(1)} %bitcast.7, f32[512,1024]{1,0:T(8,128)S(1)} %bitcast.13, f32[256,640]{1,0:T(8,128)S(1)} %get-tuple-element.69.refs_2_, f32[256,640]{1,0:T(8,128)S(1)} %collective-permute-done.1.refs_3_, ...), custom_call_target="tpu_custom_call" | custom-call | flops 1300000000 | bytes 3900000 | tf_op jit(solution)/shard_map/middle/pallas_call | solution.py:409
  37.2 0.0 collective-permute-done.refs_1_
  37.2 0.1 passing.1
  37.3 1.6 %collective-permute-start.3 = (f32[704,256]{1,0:T(8,128)S(1)}, f32[704,256]{1,0:T(8,128)S(1)}, u32[]{:S(2)}, u32[]{:S(2)}) collective-permute-start(f32[704,256]{1,0:T(8,128)S(1)} %get-tuple-element.76), channel_id=1, source_target_pairs={{0,16},{4,20},{8,24},{12,28},{16,0},{20,4},{24,8},{28,12},{1,17},{... | collective-permute-start | bytes 2162696 | tf_op jit(solution)/shard_map/ppermute | solution.py:20
  38.9 0.0 collective-permute-start.7
  38.9 5.9 %known.1 = (f32[1024,1024]{1,0:T(8,128)}, bf16[1024,512]{1,0:T(8,128)(2,1)S(1)}, bf16[1024,512]{1,0:T(8,128)(2,1)S(1)}, f32[1024,1024]{1,0:T(8,128)}, f32[8,128]{1,0:T(8,128)S(1)}) custom-call(f32[1024,1024]{1,0:T(8,128)S(1)} %bitcast.8, f32[512,1024]{1,0:T(8,128)S(1)} %bitcast.14, f32[8,128]{1,0:T(8,128)S(1)} %get-tuple-element.78.refs_2_), custom_call_target="tpu_custom_call" | custom-call | flops 6000000000 | bytes 18000000 | tf_op jit(solution)/shard_map/known/pallas_call | solution.py:409
  44.8 1.4 %middle.4 = (f32[256,384]{1,0:T(8,128)S(1)}, f32[256,384]{1,0:T(8,128)S(1)}, f32[8,128]{1,0:T(8,128)S(1)}) custom-call(f32[1024,1024]{1,0:T(8,128)S(1)} %bitcast.9, f32[512,1024]{1,0:T(8,128)S(1)} %bitcast.15, f32[256,640]{1,0:T(8,128)S(1)} %get-tuple-element.69.refs_2_, f32[256,640]{1,0:T(8,128)S(1)} %collective-permute-done.1.refs_3_, ...), custom_call_target="tpu_custom_call" | custom-call | flops 1300000000 | bytes 3900000 | tf_op jit(solution)/shard_map/middle/pallas_call | solution.py:409
  46.2 0.8 side.3
  47.0 0.5 collective-permute-start.6
  47.5 2.9 %collective-permute-start.8 = (f32[256,384]{1,0:T(8,128)S(1)}, f32[256,384]{1,0:T(8,128)S(1)}, u32[]{:S(2)}, u32[]{:S(2)}) collective-permute-start(f32[256,384]{1,0:T(8,128)S(1)} %get-tuple-element.95.refs_0_), channel_id=1, source_target_pairs={{0,2},{1,3},{2,0},{3,1},{4,6},{5,7},{6,4},{7,5},{8,10},{9,11},{10,... | collective-permute-start | bytes 1179656 | tf_op jit(solution)/shard_map/ppermute | solution.py:20
  50.4 0.0 collective-permute-done.5.refs_5_
  50.4 6.1 %collective-permute-done.3.refs_2_ = f32[704,256]{1,0:T(8,128)S(1)} collective-permute-done((f32[704,256]{1,0:T(8,128)S(1)}, f32[704,256]{1,0:T(8,128)S(1)}, u32[]{:S(2)}, u32[]{:S(2)}) %collective-permute-start.3) | collective-permute-done | bytes 720928 | tf_op jit(solution)/shard_map/ppermute | solution.py:20
  56.5 2.9 %build.1 = (f32[256,256]{1,0:T(8,128)S(1)}, f32[256,256]{1,0:T(8,128)S(1)}, f32[256,256]{1,0:T(8,128)S(1)}, f32[256,256]{1,0:T(8,128)S(1)}, f32[8,128]{1,0:T(8,128)S(1)}) custom-call(f32[448,256]{1,0:T(8,128)S(1)} %get-tuple-element.66.refs_2_.refs_0_, f32[448,256]{1,0:T(8,128)S(1)} %collective-permute-done.refs_1_, ...), custom_call_target="tpu_custom_call" | custom-call | flops 3000000000 | bytes 9000000 | tf_op jit(solution)/shard_map/build/pallas_call | solution.py:409
  59.4 5.4 %head.2 = (f32[128,128]{1,0:T(8,128)S(1)}, f32[128,128]{1,0:T(8,128)S(1)}, f32[128,128]{1,0:T(8,128)S(1)}, f32[8,128]{1,0:T(8,128)S(1)}) custom-call(f32[256,256]{1,0:T(8,128)S(1)} %get-tuple-element.82.refs_0_, f32[8,128]{1,0:T(8,128)S(1)} %get-tuple-element.83.refs_1_), custom_call_target="tpu_custom_call" | custom-call | flops 5400000000 | bytes 16200000 | tf_op jit(solution)/shard_map/head/pallas_call | solution.py:409
  64.8 0.0 collective-permute-done.7.refs_1_
  64.9 0.0 collective-permute-done.6.refs_3_
  64.9 1.4 %middle.5 = (f32[256,256]{1,0:T(8,128)S(1)}, f32[256,128]{1,0:T(8,128)S(1)}, f32[256,384]{1,0:T(8,128)S(1)}, f32[8,128]{1,0:T(8,128)S(1)}) custom-call(f32[1024,1024]{1,0:T(8,128)S(1)} %bitcast.11, f32[512,1024]{1,0:T(8,128)S(1)} %bitcast.17, f32[256,384]{1,0:T(8,128)S(1)} %get-tuple-element.89.refs_2_, f32[256,384]{1,0:T(8,128)S(1)} %collective-permute-done.6.refs_3_, ...), custom_call_target="tpu_custom_call" | custom-call | flops 1300000000 | bytes 3900000 | tf_op jit(solution)/shard_map/middle/pallas_call | solution.py:409
  66.3 0.1 collective-permute-start.10
  66.3 2.9 %collective-permute-start.9 = (f32[256,128]{1,0:T(8,128)S(1)}, f32[256,128]{1,0:T(8,128)S(1)}, u32[]{:S(2)}, u32[]{:S(2)}) collective-permute-start(f32[256,128]{1,0:T(8,128)S(1)} %get-tuple-element.108.refs_0_), channel_id=1, source_target_pairs={{0,2},{1,3},{2,0},{3,1},{4,6},{5,7},{6,4},{7,5},{8,10},{9,11},{10,... | collective-permute-start | bytes 393224 | tf_op jit(solution)/shard_map/ppermute | solution.py:20
  69.3 6.5 %turn.1 = (f32[256,256]{1,0:T(8,128)S(1)}, f32[256,256]{1,0:T(8,128)S(1)}, f32[256,256]{1,0:T(8,128)S(1)}, f32[8,128]{1,0:T(8,128)S(1)}) custom-call(f32[128,128]{1,0:T(8,128)S(1)} %get-tuple-element.84.refs_0_, f32[128,128]{1,0:T(8,128)S(1)} %get-tuple-element.85.refs_1_, f32[128,128]{1,0:T(8,128)S(1)} %get-tuple-element.86.refs_2_, ...), custom_call_target="tpu_custom_call" | custom-call | flops 6499999744 | bytes 19500000 | tf_op jit(solution)/shard_map/turn/pallas_call | solution.py:409
  75.7 3.3 %collective-permute-done.8.refs_1_ = f32[256,384]{1,0:T(8,128)S(1)} collective-permute-done((f32[256,384]{1,0:T(8,128)S(1)}, f32[256,384]{1,0:T(8,128)S(1)}, u32[]{:S(2)}, u32[]{:S(2)}) %collective-permute-start.8) | collective-permute-done | bytes 393248 | tf_op jit(solution)/shard_map/ppermute | solution.py:20
  79.0 0.1 total.5
  79.1 0.4 collective-permute-start.14
  79.5 1.7 %collective-permute-start.13 = (f32[256,256]{1,0:T(8,128)S(1)}, f32[256,256]{1,0:T(8,128)S(1)}, u32[]{:S(2)}, u32[]{:S(2)}) collective-permute-start(f32[256,256]{1,0:T(8,128)S(1)} %get-tuple-element.115.refs_5_), channel_id=1, source_target_pairs={{0,16},{4,20},{8,24},{12,28},{16,0},{20,4},{24,8},{28,12},{1,17},{... | collective-permute-start | bytes 786440 | tf_op jit(solution)/shard_map/ppermute | solution.py:20
  81.2 5.4 %head.3 = (f32[128,128]{1,0:T(8,128)S(1)}, f32[128,128]{1,0:T(8,128)S(1)}, f32[128,128]{1,0:T(8,128)S(1)}, f32[8,128]{1,0:T(8,128)S(1)}) custom-call(f32[256,256]{1,0:T(8,128)S(1)} %get-tuple-element.94.refs_0_, f32[8,128]{1,0:T(8,128)S(1)} %get-tuple-element.97.refs_1_), custom_call_target="tpu_custom_call" | custom-call | flops 5400000000 | bytes 16200000 | tf_op jit(solution)/shard_map/head/pallas_call | solution.py:409
  86.6 6.7 %tail.1 = (f32[512,512]{1,0:T(8,128)S(1)}, f32[8,128]{1,0:T(8,128)S(1)}) custom-call(f32[128,128]{1,0:T(8,128)S(1)} %get-tuple-element.98.refs_0_, f32[128,128]{1,0:T(8,128)S(1)} %get-tuple-element.99.refs_1_, f32[128,128]{1,0:T(8,128)S(1)} %get-tuple-element.100.refs_2_, f32[256,256]{1,0:T(8,128)S(1)} %get-tuple-element.101.refs_3_, ...), custom_call_target="tpu_custom_call" | custom-call | flops 6600000000 | bytes 19800000 | tf_op jit(solution)/shard_map/tail/pallas_call | solution.py:409
  93.2 0.0 collective-permute-done.10.refs_1_
  93.3 0.4 collective-permute-start.12
  93.7 0.0 collective-permute-done.9.refs_1_
  93.7 1.8 %collective-permute-start.11 = (f32[256,128]{1,0:T(8,128)S(1)}, f32[256,128]{1,0:T(8,128)S(1)}, u32[]{:S(2)}, u32[]{:S(2)}) collective-permute-start(f32[256,128]{1,0:T(8,128)S(1)} %get-tuple-element.112.refs_5_), channel_id=1, source_target_pairs={{0,16},{4,20},{8,24},{12,28},{16,0},{20,4},{24,8},{28,12},{1,17},{... | collective-permute-start | bytes 393224 | tf_op jit(solution)/shard_map/ppermute | solution.py:20
  95.5 0.0 collective-permute-done.13.refs_7_
  95.5 0.0 collective-permute-done.14.refs_8_
  95.5 6.9 %last.3 = (f32[1024,1024]{1,0:T(8,128)}, f32[1024,1024]{1,0:T(8,128)}, f32[8,128]{1,0:T(8,128)S(1)}) custom-call(f32[512,512]{1,0:T(8,128)S(1)} %get-tuple-element.104.refs_0_, f32[256,256]{1,0:T(8,128)S(1)} %get-tuple-element.72.refs_4_.refs_6_.refs_1_, f32[256,256]{1,0:T(8,128)S(1)} %get-tuple-element.105.refs_2_, ...), custom_call_target="tpu_custom_call", output_to_operand_aliasing={{0}: (11, {}), {1}: (12, {})} | custom-call | flops 5000000000 | bytes 15000000 | tf_op jit(solution)/shard_map/last/pallas_call | solution.py:409
  102.4 0.0 collective-permute-done.12.refs_6_
  102.4 4.6 %last.4 = (f32[1024,1024]{1,0:T(8,128)}, f32[1024,1024]{1,0:T(8,128)}, f32[8,128]{1,0:T(8,128)S(1)}) custom-call(f32[512,512]{1,0:T(8,128)S(1)} %get-tuple-element.104.refs_0_, f32[256,256]{1,0:T(8,128)S(1)} %get-tuple-element.72.refs_4_.refs_6_.refs_1_, f32[256,256]{1,0:T(8,128)S(1)} %get-tuple-element.105.refs_2_, ...), custom_call_target="tpu_custom_call", output_to_operand_aliasing={{0}: (8, {}), {1}: (9, {})} | custom-call | flops 5000000000 | bytes 15000000 | tf_op jit(solution)/shard_map/last/pallas_call | solution.py:409
  107.0 0.0 collective-permute-done.11.refs_6_
  107.0 4.1 %last.5 = (f32[1024,1024]{1,0:T(8,128)}, f32[1024,1024]{1,0:T(8,128)}, f32[8,128]{1,0:T(8,128)}) custom-call(f32[512,512]{1,0:T(8,128)S(1)} %get-tuple-element.104.refs_0_, f32[256,256]{1,0:T(8,128)S(1)} %get-tuple-element.72.refs_4_.refs_6_.refs_1_, f32[256,256]{1,0:T(8,128)S(1)} %get-tuple-element.105.refs_2_, ...), custom_call_target="tpu_custom_call", output_to_operand_aliasing={{0}: (8, {}), {1}: (9, {})} | custom-call | flops 5000000000 | bytes 15000000 | tf_op jit(solution)/shard_map/last/pallas_call | solution.py:409
  (3 shorter events, 0.1 us)
Async XLA Ops:
  0.6 2.2 %copy-start = (f32[1,1,1024,1024]{3,2,1,0:T(8,128)S(1)}, f32[1,1,1024,1024]{3,2,1,0:T(8,128)}, u32[]{:S(2)}) copy-start(f32[1,1,1024,1024]{3,2,1,0:T(8,128)} %param.2) | copy-start | bytes 12582916
  2.8 3.3 %copy-start.2 = (f32[1,1,512,1024]{3,2,1,0:T(8,128)S(1)}, f32[1,1,512,1024]{3,2,1,0:T(8,128)}, u32[]{:S(2)}) copy-start(f32[1,1,512,1024]{3,2,1,0:T(8,128)} %param.3) | copy-start | bytes 6291460
  3.0 8.8 %collective-permute-start.2 = (f32[192,256]{1,0:T(8,128)S(1)}, f32[192,256]{1,0:T(8,128)S(1)}, u32[]{:S(2)}, u32[]{:S(2)}) collective-permute-start(f32[192,256]{1,0:T(8,128)S(1)} %get-tuple-element.70.refs_0_), channel_id=1, source_target_pairs={{0,16},{4,20},{8,24},{12,28},{16,0},{20,4},{24,8},{28,12},{1,17},{... | collective-permute-start | bytes 589832 | tf_op jit(solution)/shard_map/ppermute | solution.py:20
  7.1 28.8 %collective-permute-start.1 = (f32[256,640]{1,0:T(8,128)S(1)}, f32[256,640]{1,0:T(8,128)S(1)}, u32[]{:S(2)}, u32[]{:S(2)}) collective-permute-start(f32[256,640]{1,0:T(8,128)S(1)} %get-tuple-element.69.refs_2_), channel_id=1, source_target_pairs={{0,16},{4,20},{8,24},{12,28},{16,0},{20,4},{24,8},{28,12},{1,17},{... | collective-permute-start | bytes 1966088 | tf_op jit(solution)/shard_map/ppermute | solution.py:20
  8.5 28.7 %collective-permute-start = (f32[448,256]{1,0:T(8,128)S(1)}, f32[448,256]{1,0:T(8,128)S(1)}, u32[]{:S(2)}, u32[]{:S(2)}) collective-permute-start(f32[448,256]{1,0:T(8,128)S(1)} %get-tuple-element.66.refs_2_.refs_0_), channel_id=1, source_target_pairs={{0,2},{1,3},{2,0},{3,1},{4,6},{5,7},{6,4},{7,5},{8,10},{9,11},{10,... | collective-permute-start | bytes 1376264 | tf_op jit(solution)/shard_map/ppermute | solution.py:20
  11.8 24.1 %copy-start.1 = (f32[1,1,1024,1024]{3,2,1,0:T(8,128)S(1)}, f32[1,1,1024,1024]{3,2,1,0:T(8,128)}, u32[]{:S(2)}) copy-start(f32[1,1,1024,1024]{3,2,1,0:T(8,128)} %param.2) | copy-start | bytes 12582916
  23.2 12.3 %collective-permute-start.4 = (f32[192,128]{1,0:T(8,128)S(1)}, f32[192,128]{1,0:T(8,128)S(1)}, u32[]{:S(2)}, u32[]{:S(2)}) collective-permute-start(f32[192,128]{1,0:T(8,128)S(1)} %get-tuple-element.77), channel_id=1, source_target_pairs={{0,2},{1,3},{2,0},{3,1},{4,6},{5,7},{6,4},{7,5},{8,10},{9,11},{10,... | collective-permute-start | bytes 294920 | tf_op jit(solution)/shard_map/ppermute | solution.py:20
  35.4 15.0 %collective-permute-start.5 = (f32[192,128]{1,0:T(8,128)S(1)}, f32[192,128]{1,0:T(8,128)S(1)}, u32[]{:S(2)}, u32[]{:S(2)}) collective-permute-start(f32[192,128]{1,0:T(8,128)S(1)} %collective-permute-done.4.refs_4_), channel_id=1, source_target_pairs={{0,16},{4,20},{8,24},{12,28},{16,0},{20,4},{24,8},{28,12},{1,17},{... | collective-permute-start | bytes 294920 | tf_op jit(solution)/shard_map/ppermute | solution.py:20
  37.3 19.2 %collective-permute-start.3 = (f32[704,256]{1,0:T(8,128)S(1)}, f32[704,256]{1,0:T(8,128)S(1)}, u32[]{:S(2)}, u32[]{:S(2)}) collective-permute-start(f32[704,256]{1,0:T(8,128)S(1)} %get-tuple-element.76), channel_id=1, source_target_pairs={{0,16},{4,20},{8,24},{12,28},{16,0},{20,4},{24,8},{28,12},{1,17},{... | collective-permute-start | bytes 2162696 | tf_op jit(solution)/shard_map/ppermute | solution.py:20
  38.9 25.9 %collective-permute-start.7 = (f32[256,256]{1,0:T(8,128)S(1)}, f32[256,256]{1,0:T(8,128)S(1)}, u32[]{:S(2)}, u32[]{:S(2)}) collective-permute-start(f32[256,256]{1,0:T(8,128)S(1)} %get-tuple-element.90.refs_0_), channel_id=1, source_target_pairs={{0,2},{1,3},{2,0},{3,1},{4,6},{5,7},{6,4},{7,5},{8,10},{9,11},{10,... | collective-permute-start | bytes 786440 | tf_op jit(solution)/shard_map/ppermute | solution.py:20
  47.0 17.9 %collective-permute-start.6 = (f32[256,384]{1,0:T(8,128)S(1)}, f32[256,384]{1,0:T(8,128)S(1)}, u32[]{:S(2)}, u32[]{:S(2)}) collective-permute-start(f32[256,384]{1,0:T(8,128)S(1)} %get-tuple-element.89.refs_2_), channel_id=1, source_target_pairs={{0,16},{4,20},{8,24},{12,28},{16,0},{20,4},{24,8},{28,12},{1,17},{... | collective-permute-start | bytes 1179656 | tf_op jit(solution)/shard_map/ppermute | solution.py:20
  47.5 31.5 %collective-permute-start.8 = (f32[256,384]{1,0:T(8,128)S(1)}, f32[256,384]{1,0:T(8,128)S(1)}, u32[]{:S(2)}, u32[]{:S(2)}) collective-permute-start(f32[256,384]{1,0:T(8,128)S(1)} %get-tuple-element.95.refs_0_), channel_id=1, source_target_pairs={{0,2},{1,3},{2,0},{3,1},{4,6},{5,7},{6,4},{7,5},{8,10},{9,11},{10,... | collective-permute-start | bytes 1179656 | tf_op jit(solution)/shard_map/ppermute | solution.py:20
  66.3 27.0 %collective-permute-start.10 = (f32[256,256]{1,0:T(8,128)S(1)}, f32[256,256]{1,0:T(8,128)S(1)}, u32[]{:S(2)}, u32[]{:S(2)}) collective-permute-start(f32[256,256]{1,0:T(8,128)S(1)} %get-tuple-element.109.refs_0_), channel_id=1, source_target_pairs={{0,2},{1,3},{2,0},{3,1},{4,6},{5,7},{6,4},{7,5},{8,10},{9,11},{10,... | collective-permute-start | bytes 786440 | tf_op jit(solution)/shard_map/ppermute | solution.py:20
  66.3 27.3 %collective-permute-start.9 = (f32[256,128]{1,0:T(8,128)S(1)}, f32[256,128]{1,0:T(8,128)S(1)}, u32[]{:S(2)}, u32[]{:S(2)}) collective-permute-start(f32[256,128]{1,0:T(8,128)S(1)} %get-tuple-element.108.refs_0_), channel_id=1, source_target_pairs={{0,2},{1,3},{2,0},{3,1},{4,6},{5,7},{6,4},{7,5},{8,10},{9,11},{10,... | collective-permute-start | bytes 393224 | tf_op jit(solution)/shard_map/ppermute | solution.py:20
  79.1 16.4 %collective-permute-start.14 = (f32[256,384]{1,0:T(8,128)S(1)}, f32[256,384]{1,0:T(8,128)S(1)}, u32[]{:S(2)}, u32[]{:S(2)}) collective-permute-start(f32[256,384]{1,0:T(8,128)S(1)} %get-tuple-element.116.refs_6_), channel_id=1, source_target_pairs={{0,16},{4,20},{8,24},{12,28},{16,0},{20,4},{24,8},{28,12},{1,17},{... | collective-permute-start | bytes 1179656 | tf_op jit(solution)/shard_map/ppermute | solution.py:20
  79.5 16.0 %collective-permute-start.13 = (f32[256,256]{1,0:T(8,128)S(1)}, f32[256,256]{1,0:T(8,128)S(1)}, u32[]{:S(2)}, u32[]{:S(2)}) collective-permute-start(f32[256,256]{1,0:T(8,128)S(1)} %get-tuple-element.115.refs_5_), channel_id=1, source_target_pairs={{0,16},{4,20},{8,24},{12,28},{16,0},{20,4},{24,8},{28,12},{1,17},{... | collective-permute-start | bytes 786440 | tf_op jit(solution)/shard_map/ppermute | solution.py:20
  93.3 9.1 %collective-permute-start.12 = (f32[256,256]{1,0:T(8,128)S(1)}, f32[256,256]{1,0:T(8,128)S(1)}, u32[]{:S(2)}, u32[]{:S(2)}) collective-permute-start(f32[256,256]{1,0:T(8,128)S(1)} %get-tuple-element.114.refs_5_), channel_id=1, source_target_pairs={{0,16},{4,20},{8,24},{12,28},{16,0},{20,4},{24,8},{28,12},{1,17},{... | collective-permute-start | bytes 786440 | tf_op jit(solution)/shard_map/ppermute | solution.py:20
  93.7 13.3 %collective-permute-start.11 = (f32[256,128]{1,0:T(8,128)S(1)}, f32[256,128]{1,0:T(8,128)S(1)}, u32[]{:S(2)}, u32[]{:S(2)}) collective-permute-start(f32[256,128]{1,0:T(8,128)S(1)} %get-tuple-element.112.refs_5_), channel_id=1, source_target_pairs={{0,16},{4,20},{8,24},{12,28},{16,0},{20,4},{24,8},{28,12},{1,17},{... | collective-permute-start | bytes 393224 | tf_op jit(solution)/shard_map/ppermute | solution.py:20
where the time goes:
time: 111 us
  Pallas kernels  65.9 us (59%)
  starting transfers between devices  22.9 us (21%)
  waiting for transfers between devices  19.2 us (17%)
  local copies, waits for them, and re-layouts  2.19 us (2%)
    pallas_call x22, Pallas kernels, __call__(): pl.pallas_call(body, out_shape=list(outs) + [array(8, LANES)], in_specs=l...  65.9 us
    ppermute x15, starting transfers between devices, exchange(): return lax.ppermute(block, axis, [(i, i ^ half) for i in range(2 * half)])  22.9 us
    ppermute x15, waiting for transfers between devices, exchange(): return lax.ppermute(block, axis, [(i, i ^ half) for i in range(2 * half)])  19.2 us
  transfers between devices with their start and end apart: 15, of which 4 were waited for; matrix products, arithmetic and copies ran while one was open for 0% of the time, Pallas kernels for 55%

commit v1 on v0

--- a/solution.py
+++ b/solution.py
@@ -12,7 +12,7 @@
 BF16 = jnp.bfloat16
 LANES = 128
 PANEL = 8
-TURN = 4
+TURN = 8
 
 
 def exchange(block, axis):
@@ -57,6 +57,18 @@
 def triple(left, right):
     (lh, ll), (rh, rl) = left, right
     return half_dot(lh, rh) + (half_dot(lh, rl) + half_dot(ll, rh))
+
+
+def near_nn(left, right):
+    return triple(split(left), split(right))
+
+
+def near_nt(left, right):
+    return near_nn(left, right.T)
+
+
+def near_tn(left, right):
+    return near_nn(left.T, right)
 
 
 def tree(terms):
@@ -136,6 +148,12 @@
     return jnp.concatenate([top, jnp.concatenate([-corner.T, tail], 1)], 0)
 
 
+def near_join(head, reach, tail):
+    corner = near_nn(reach, tail)
+    top = jnp.concatenate([head + near_nt(corner, reach), -corner], 1)
+    return jnp.concatenate([top, jnp.concatenate([-corner.T, tail], 1)], 0)
+
+
 def unpack(packed):
     h = packed.shape[1] // 2
     low = jnp.concatenate([packed[h:, :h], packed[h:, h:]], 0)
@@ -173,26 +191,24 @@
     ]
 
 
-def joined_kernel(leaf, out, sems):
-    fetch(symmetric(leaf, edges()[0], out, 0), sems)
-
-
-def crossing_kernel(leaf, out, sems):
-    n = out.shape[1]
-    i, _, y, _ = edges()
-    whole = leaf.at[pl.ds(pl.multiple_of(y * n, n), n), pl.ds(pl.multiple_of(i * n, n), n)]
-    fetch([(whole, out.at[pl.ds(0, n)])] + symmetric(leaf, y, out, n), sems)
-
-
 def passing_kernel(middle, middle_z, out):
     n = out.shape[1]
-    out[:n] = middle[:n]
-    out[n : 2 * n] = middle_z[:n]
-    out[2 * n :] = middle[n:] + middle_z[n:]
+    out[:n] = middle_z[:n]
+    out[n:] = middle[n:] + middle_z[n:]
+
+
+def relay_kernel(given, out):
+    out[...] = given[...]
 
 
 def sum_kernel(own, other, out):
     out[...] = own[...] + other[...]
+
+
+def append_kernel(before, own, other, out):
+    width = before.shape[1]
+    out[:, :width] = before[...]
+    out[:, width:] = own[...] + other[...]
 
 
 def outer_rows(leaf, edge, rows, sems):
@@ -206,16 +222,32 @@
 
 
 def side_kernel(base, leaf, data, out, rows, held, sems):
-    copies = outer_rows(leaf, edges()[0], rows, sems)
-    copies.append(pltpu.make_async_copy(data.at[:, pl.ds(base, held.shape[1])], held, sems.at[2]))
+    n, width = rows.shape[0], held.shape[1]
+    i, _, y, _ = edges()
+    copies = outer_rows(leaf, i, rows, sems)
+    copies.append(pltpu.make_async_copy(data.at[:, pl.ds(base, width)], held, sems.at[2]))
     for copy in copies:
         copy.start()
+    if out.shape[1] > width:
+        whole = leaf.at[pl.ds(pl.multiple_of(y * n, n), n), pl.ds(pl.multiple_of(i * n, n), n)]
+        fetch([(whole, out.at[:, pl.ds(width, n)])], sems.at[pl.ds(3, 1)])
     for copy in copies:
         copy.wait()
-    out[...] = triple(split(rows[...]), split(held[...]))
-
-
-def known_kernel(leaf, data, flux, high, low, potential, data_high, data_low, sems):
+    out[:, :width] = triple(split(rows[...]), split(held[...]))
+
+
+def joined_kernel(leaf, out, sems):
+    fetch(symmetric(leaf, edges()[0], out, 0), sems)
+
+
+def crossing_kernel(leaf, out, sems):
+    n = out.shape[1]
+    i, _, y, _ = edges()
+    whole = leaf.at[pl.ds(pl.multiple_of(y * n, n), n), pl.ds(pl.multiple_of(i * n, n), n)]
+    fetch([(whole, out.at[pl.ds(0, n)])] + symmetric(leaf, y, out, n), sems)
+
+
+def known_kernel(leaf, data, flux, high, low, potential, _, data_high, data_low, sems):
     step = pl.program_id(0)
     n = leaf.shape[0]
     i, x, y, d = edges()
@@ -247,7 +279,7 @@
     h = n // 2
     solved = invert(unpack(joined[...] + joined_far[...]))
     inverse[...] = solved
-    across[...] = full_nt(solved, middle[:n])
+    across[...] = near_nt(solved, middle[:n])
 
     def fill(diagonal, low):
         half[:h] = diagonal
@@ -281,7 +313,7 @@
         done += part
 
 
-def build_kernel(middle, middle_z, passed, inverse, half_z, half_x, across, across_far, own, off, far, other):
+def build_kernel(middle, middle_z, passed, side_far, inverse, half_z, half_x, across, across_far, own, off, far, other):
     n = inverse.shape[0]
     h = n // 2
 
@@ -300,14 +332,15 @@
     def _():
         fill(half_x, half_z)
 
-    q_far = full_nt(inverse[...], passed[:n])
+    cross = side_far[:, -n:]
+    q_far = near_nt(inverse[...], cross)
+    q_own = across[...]
     across_far[...] = q_far
-    q_own = across[...]
-    p_own = full_nt(other[...], middle_z[:n])
-    p_far = full_nt(other[...], passed[n : 2 * n])
-    own[...] = unpack(middle[n:] + middle_z[n:]) - (full_nn(middle[:n], q_own) + full_nn(middle_z[:n], p_own))
-    off[...] = -(full_nn(middle[:n], q_far) + full_nn(middle_z[:n], p_far))
-    far[...] = unpack(passed[2 * n :]) - (full_nn(passed[:n], q_far) + full_nn(passed[n : 2 * n], p_far))
+    p_own = near_nt(other[...], middle_z[:n])
+    p_far = near_nt(other[...], passed[:n])
+    own[...] = unpack(middle[n:] + middle_z[n:]) - (near_nn(middle[:n], q_own) + near_nn(middle_z[:n], p_own))
+    off[...] = -(near_nn(middle[:n], q_far) + near_nn(middle_z[:n], p_far))
+    far[...] = unpack(passed[n:]) - (near_nn(cross, q_far) + near_nn(passed[:n], p_far))
 
 
 def open_half(matrix, head, reach, rest):
@@ -324,44 +357,46 @@
 
 def turn_kernel(head, reach, rest, off, far, done, wide, left):
     done[...] = join(head[...], reach[...], invert(rest[...]))
-    wide[...] = full_nn(done[...], off[...])
-    left[...] = far[...] - full_tn(off[...], wide[...])
-
-
-def tail_kernel(head, reach, rest, done, wide, out):
-    out[...] = join(done[...], wide[...], join(head[...], reach[...], invert(rest[...])))
-
-
-def beside(parts):
-    return jnp.concatenate([part[...] for part in parts], 1)
-
-
-def last_kernel(count, base, offset, inverse2, across, across_far, high, low, *rest):
-    w_own, w_far, start = rest[:count], rest[count : 2 * count], rest[2 * count : 3 * count]
-    _, _, flux, potential, solved, known, sems = rest[3 * count :]
-    n = across.shape[0]
-    width = solved.shape[1]
+    wide[...] = near_nn(done[...], off[...])
+    left[...] = far[...] - near_tn(off[...], wide[...])
+
+
+def tail_kernel(head, reach, rest, done, wide, across, across_far, high, low):
+    n = done.shape[0]
+    solved = near_join(done[...], wide[...], join(head[...], reach[...], invert(rest[...])))
+    inward = triple(split(jnp.concatenate([across[...], across_far[...]], 1)), split(solved))
+    high[...], low[...] = split(jnp.concatenate([inward, -solved[:n]], 0))
+
+
+def last_kernel(count, base, solve_high, solve_low, high, low, known, *rest):
+    w_own, w_far, starts = rest[:count], rest[count : 2 * count], rest[2 * count : -7]
+    flux, potential, solved, made, sems = rest[-5:]
+    n, width = w_own[0].shape[0], solved.shape[1]
     i, _, y, _ = edges()
     cols = pl.ds(base, width)
-    load = pltpu.make_async_copy(flux.at[:, cols], known, sems.at[2])
-    load.start()
-    top = triple(split(inverse2[...]), split(jnp.concatenate([beside(w_own), beside(w_far)], 0)))
-    left = split(jnp.concatenate([across[...], across_far[...]], 1))
-    solved[:n] = beside(start)[:, offset : offset + width] + triple(left, split(top))
-    solved[n:] = -top[:n]
-    copies = [
-        pltpu.make_async_copy(
-            solved.at[pl.ds(p * n, n), :], potential.at[pl.ds(pl.multiple_of(e * n, n), n), cols], sems.at[p]
-        )
-        for p, e in enumerate((i, y))
-    ]
+    done = 0
+    for own, far in zip(w_own, w_far):
+        part = slice(done, done + own.shape[1])
+        inner = triple((solve_high[...], solve_low[...]), split(jnp.concatenate([own[...], far[...]], 0)))
+        solved[:, part] = inner
+        done = part.stop
+    done = 0
+    for start in starts:
+        part = slice(done, done + start.shape[1])
+        solved[:n, part] += start[...]
+        done = part.stop
+    right = split(solved[...])
+    copies = []
+    for k in range(4):
+        rows = pl.ds(k * n, n)
+        made[rows] = known[rows, base : base + width] + triple((high[rows], low[rows]), right)
+        copies.append(pltpu.make_async_copy(made.at[rows], flux.at[rows, cols], sems.at[k]))
+        copies[-1].start()
+    for p, e in enumerate((i, y)):
+        rows = pl.ds(pl.multiple_of(e * n, n), n)
+        copies.append(pltpu.make_async_copy(solved.at[pl.ds(p * n, n), :], potential.at[rows, cols], sems.at[4 + p]))
+        copies[-1].start()
     for copy in copies:
-        copy.start()
-    load.wait()
-    known[...] += triple((high[...], low[...]), split(solved[...]))
-    store = pltpu.make_async_copy(known, flux.at[:, cols], sems.at[2])
-    store.start()
-    for copy in copies + [store]:
         copy.wait()
 
 
@@ -373,22 +408,16 @@
 HBM = pl.BlockSpec(memory_space=pltpu.HBM)
 WHOLE = pl.BlockSpec(memory_space=pltpu.VMEM)
 MIB = 1 << 20
+EARLY = 58
 
 
 COSTS = {
-    "crossing": 0.1,
-    "joined": 0.1,
-    "side": 1.0,
-    "first": 11.0,
-    "middle": 1.3,
-    "passing": 0.1,
-    "known": 6.0,
-    "build": 3.0,
-    "head": 5.4,
-    "turn": 6.5,
-    "tail": 6.6,
-    "total": 0.1,
-    "last": 5.0,
+    "passing": 8.0,
+    "relay": 8.0,
+    "build": 0.7,
+    "opening": 1.2,
+    "copy": 0.05,
+    "closing": 2.0,
 }
 
 
@@ -397,7 +426,7 @@
         self.mark = None
 
     def __call__(self, name, kernel, outs, *args, ins=None, out_specs=None, scratch=(), aliases=None, limit=24, **kwargs):
-        cost = COSTS[name]
+        cost = COSTS.get(name, 0.005)
         ins = ins or [WHOLE] * len(args)
         out_specs = out_specs or [WHOLE] * len(outs)
         marks = [] if self.mark is None else [self.mark]
@@ -431,24 +460,26 @@
     dma = pltpu.SemaphoreType.DMA
     call = Chain()
     unit = count // 8
-    widths = [2 * unit, 3 * unit, 2 * unit, unit]
-    bases = [0, 2 * unit, 5 * unit, 7 * unit]
-    cut = 5 * unit
-
-    middle = call("crossing", crossing_kernel, [array(n + packed, n)], leaf, ins=[ANY], scratch=[dma((5,))])
+    widths = [2 * unit, 2 * unit, 2 * unit, unit, unit]
+    bases = [0, 2 * unit, 4 * unit, 6 * unit, 7 * unit]
+
+    middle = call(
+        "crossing", crossing_kernel, [array(n + packed, n)], leaf, limit=EARLY, ins=[HBM], scratch=[dma((5,))]
+    )
     middle_z = exchange(middle, "gy")
-    joined = call("joined", joined_kernel, [array(packed, n)], leaf, ins=[ANY], scratch=[dma((4,))])
+    joined = call("joined", joined_kernel, [array(packed, n)], leaf, limit=EARLY, ins=[HBM], scratch=[dma((4,))])
     joined_far = exchange(joined, "gx")
 
-    def sides(base, width):
+    def sides(base, width, extra=0, limit=24):
         own = call(
             "side",
             functools.partial(side_kernel, base),
-            [array(n, width)],
+            [array(n, width + extra)],
             leaf,
             data,
-            ins=[ANY] * 2,
-            scratch=[pltpu.VMEM((n, 2 * n), F32), pltpu.VMEM((2 * n, width), F32), dma((3,))],
+            limit=limit,
+            ins=[HBM] * 2,
+            scratch=[pltpu.VMEM((n, 2 * n), F32), pltpu.VMEM((2 * n, width), F32), dma((4,))],
         )
         return own, exchange(own, "gx")
 
@@ -469,25 +500,36 @@
         )
         return given[:-1], given[-1]
 
-    def total(own, other):
-        return call("total", sum_kernel, [array(*own.shape)], own, other)
-
-    own_a, far_a = sides(0, cut)
+    def total(own, far, name="total"):
+        w = call(name, sum_kernel, [array(*own.shape)], own, far)
+        return w, exchange(w, "gx")
+
+    def copy(given, name="copy"):
+        return call(name, relay_kernel, [array(*given.shape)], given)
+
+    own_a, far_a = sides(0, 4 * unit, n, EARLY)
     inverse1, across, half = call(
         "first", first_kernel, [array(n, n)] * 2 + [array(packed, h)], joined, joined_far, middle
     )
     half_z = exchange(half, "gy")
+    passing = call("passing", passing_kernel, [array(n + packed, n)], middle, middle_z)
+    passed = exchange(passing, "gx")
     (v0,), start0 = middles([0], 0, own_a, far_a)
     z0 = exchange(v0, "gy")
-    passing = call("passing", passing_kernel, [array(2 * n + packed, n)], middle, middle_z)
-    passed = exchange(passing, "gx")
-    known, high, low, potential = call(
+    half_z = copy(half_z, "relay")
+    half_x = exchange(half_z, "gx")
+    (v1,), start1 = middles([1], 0, own_a, far_a)
+    z1 = exchange(v1, "gy")
+    own_b, far_b = sides(bases[2], widths[2])
+    own_c, far_c = sides(bases[3], 2 * unit)
+    known, high, low, potential, flux = call(
         "known",
         known_kernel,
         [
             array(full, count),
             array(full, 2 * n, dtype=BF16),
             array(full, 2 * n, dtype=BF16),
+            array(full, count),
             array(full, count),
         ],
         leaf,
@@ -498,14 +540,11 @@
             pl.BlockSpec((n, 2 * n), lambda s: (s, 0)),
             pl.BlockSpec((n, 2 * n), lambda s: (s, 0)),
             ANY,
+            ANY,
         ],
         scratch=[pltpu.VMEM((2 * n, count), BF16), pltpu.VMEM((2 * n, count), BF16), dma((2,))],
         grid=(4,),
     )
-    half_x = exchange(half_z, "gx")
-    (v1,), start1 = middles([1], 0, own_a, far_a)
-    z1 = exchange(v1, "gy")
-    own_b, far_b = sides(cut, count - cut)
     across_far, s_own, s_off, s_far = call(
         "build",
         build_kernel,
@@ -513,6 +552,7 @@
         middle,
         middle_z,
         passed,
+        far_a,
         inverse1,
         half_z,
         half_x,
@@ -520,48 +560,51 @@
         scratch=[pltpu.VMEM((n, n), F32)],
     )
     head, reach, rest = call("head", head_kernel, [array(h, h)] * 3, s_own)
-    w0 = total(v0, z0)
-    w0_far = exchange(w0, "gx")
-    (v2, v3), start2 = middles([2, 3], cut, own_b, far_b)
-    z2, z3 = exchange(v2, "gy"), exchange(v3, "gy")
+    w0 = call("opening", sum_kernel, [array(*v0.shape)], v0, z0)
+    (v2,), start2 = middles([2], bases[2], own_b, far_b)
+    z2 = exchange(v2, "gy")
     done, wide, left = call("turn", turn_kernel, [array(n, n)] * 3, head, reach, rest, s_off, s_far)
-    w1 = total(v1, z1)
+    w1 = call("append", append_kernel, [array(n, 4 * unit)], w0, v1, z1)
     w1_far = exchange(w1, "gx")
+    (v3, v4), start3 = middles([3, 4], bases[3], own_c, far_c)
+    z3 = exchange(v3, "gy")
     head, reach, rest = call("head", head_kernel, [array(h, h)] * 3, left)
-    inverse2 = call("tail", tail_kernel, [array(2 * n, 2 * n)], head, reach, rest, done, wide)
-    w2 = total(v2, z2)
-    w2_far = exchange(w2, "gx")
-    w3 = total(v3, z3)
-    w3_far = exchange(w3, "gx")
-
-    flux = known
-    groups = [
-        ([0, 1], [w0, w1], [w0_far, w1_far], [start0, start1]),
-        ([2], [w2], [w2_far], [start2]),
-        ([3], [w3], [w3_far], [start2]),
-    ]
-    for parts, own, far, start in groups:
-        base, width = bases[parts[0]], sum(widths[k] for k in parts)
-        pieces = (*own, *far, *start)
-        offset = widths[2] if parts == [3] else 0
-        flux, potential = call(
+    w2, w2_far = total(v2, z2)
+    v4 = copy(v4)
+    z4 = exchange(v4, "gy")
+    inverse2 = call(
+        "tail", tail_kernel, [array(2 * n, 2 * n, dtype=BF16)] * 2, head, reach, rest, done, wide, across, across_far
+    )
+    w3, w3_far = total(v3, z3)
+    w4, w4_far = total(v4, z4, "closing")
+
+    def last(base, own, far, starts, held):
+        width = sum(part.shape[1] for part in own)
+        fixed = 5 + 2 * len(own) + len(starts)
+        return call(
             "last",
-            functools.partial(last_kernel, len(parts), base, offset),
+            functools.partial(last_kernel, len(own), base),
             [array(full, count), array(full, count)],
-            inverse2,
-            across,
-            across_far,
+            *inverse2,
             high,
             low,
-            *pieces,
-            flux,
-            potential,
-            ins=[WHOLE] * (5 + len(pieces)) + [ANY] * 2,
+            known,
+            *own,
+            *far,
+            *starts,
+            *held[1:],
+            *held[:1],
+            ins=[WHOLE] * fixed + [ANY] * len(held),
             out_specs=[ANY] * 2,
-            scratch=[pltpu.VMEM((2 * n, width), F32), pltpu.VMEM((full, width), F32), dma((3,))],
-            aliases={5 + len(pieces): 0, 6 + len(pieces): 1},
+            scratch=[pltpu.VMEM((2 * n, width), F32), pltpu.VMEM((full, width), F32), dma((6,))],
+            aliases={fixed: 1, fixed + 1: 0},
         )
-    return potential[None, None], flux[None, None]
+
+    held = last(0, [w1], [w1_far], [start0, start1], [flux, potential])
+    held = last(bases[2], [w2], [w2_far], [start2], held)
+    w3_far = copy(w3_far)
+    held = last(bases[3], [w3, w4], [w3_far, w4_far], [start3], held)
+    return held[1][None, None], held[0][None, None]
 
 
 def solution(mesh):

time: 111 us -> 95.8 us (0.86)
  waiting for transfers between devices: 19.2 us -> 6.32 us
  Pallas kernels: 65.9 us -> 62.8 us
  starting transfers between devices: 22.9 us -> 24.6 us
  local copies, waits for them, and re-layouts: 2.19 us -> 0.7 us
    ppermute x15 -> x17, waiting for transfers between devices: 19.2 us -> 6.32 us  [exchange(): return lax.ppermute(block, axis, [(i, i ^ half) for i in range(2 * half)])]
    pallas_call x22 -> x28, Pallas kernels: 65.9 us -> 62.8 us  [__call__(): pl.pallas_call(body, out_shape=list(outs) + [array(8, LANES)], in_specs=l...]
    ppermute x15 -> x17, starting transfers between devices: 22.9 us -> 24.6 us  [exchange(): return lax.ppermute(block, axis, [(i, i ^ half) for i in range(2 * half)])]
    unnamed x6 -> x12, local copies, waits for them, and re-layouts: 2.19 us -> 0.7 us
  transfers between devices with their start and end apart: 15 -> 17, of which waited for: 4 -> 3; matrix products, arithmetic and copies ran while one was open for 0% -> 0% of each run, Pallas kernels for 55% -> 61%
where the time goes in v1:
time: 95.8 us; the launch traced here: 95.6 us
  Pallas kernels  62.8 us (66%)
  starting transfers between devices  24.6 us (26%)
  waiting for transfers between devices  6.32 us (7%)
  between operations  1.11 us (1%)
    pallas_call x28, Pallas kernels, __call__(): pl.pallas_call(body, out_shape=list(outs) + [array(8, LANES)], in_specs=l...  62.8 us
    ppermute x17, starting transfers between devices, exchange(): return lax.ppermute(block, axis, [(i, i ^ half) for i in range(2 * half)])  24.6 us
    ppermute x17, waiting for transfers between devices, exchange(): return lax.ppermute(block, axis, [(i, i ^ half) for i in range(2 * half)])  6.32 us
  transfers between devices with their start and end apart: 17, of which 3 were waited for; matrix products, arithmetic and copies ran while one was open for 0% of the time, Pallas kernels for 61%

profile of v1, /device:TPU:0, one launch (start us, length us, event | category | flops | bytes accessed | tf_op | source)
XLA Modules:
  0.0 95.6 jit_solution(4909330254752543810)
XLA Ops:
  0.6 1.8 %crossing.1 = (f32[448,256]{1,0:T(8,128)}, f32[8,128]{1,0:T(8,128)}) custom-call(f32[1024,1024]{1,0:T(8,128)} %bitcast.4), custom_call_target="tpu_custom_call" | custom-call | flops 5000000 | bytes 15000 | tf_op jit(solution)/shard_map/crossing/pallas_call | solution.py:438
  2.4 4.1 %collective-permute-start = (f32[448,256]{1,0:T(8,128)}, f32[448,256]{1,0:T(8,128)S(1)}, u32[]{:S(2)}, u32[]{:S(2)}) collective-permute-start(f32[448,256]{1,0:T(8,128)} %get-tuple-element.81.refs_2_.refs_0_), channel_id=1, source_target_pairs={{0,2},{1,3},{2,0},{3,1},{4,6},{5,7},{6,4},{7,5},{8,10},{9,11},{10,... | collective-permute-start | bytes 1376264 | tf_op jit(solution)/shard_map/ppermute | solution.py:20
  6.5 1.6 %joined.1 = (f32[192,256]{1,0:T(8,128)}, f32[8,128]{1,0:T(8,128)}) custom-call(f32[1024,1024]{1,0:T(8,128)} %bitcast.5, f32[8,128]{1,0:T(8,128)} %get-tuple-element.82.refs_1_), custom_call_target="tpu_custom_call" | custom-call | flops 5000000 | bytes 15000 | tf_op jit(solution)/shard_map/joined/pallas_call | solution.py:438
  8.1 0.0 copy-start.3
  8.1 0.0 copy-start.4
  8.2 1.6 %collective-permute-start.1 = (f32[192,256]{1,0:T(8,128)}, f32[192,256]{1,0:T(8,128)S(1)}, u32[]{:S(2)}, u32[]{:S(2)}) collective-permute-start(f32[192,256]{1,0:T(8,128)} %get-tuple-element.83.refs_0_), channel_id=1, source_target_pairs={{0,16},{4,20},{8,24},{12,28},{16,0},{20,4},{24,8},{28,12},{1,17},{... | collective-permute-start | bytes 589832 | tf_op jit(solution)/shard_map/ppermute | solution.py:20
  9.7 2.9 %side.3 = (f32[256,768]{1,0:T(8,128)}, f32[8,128]{1,0:T(8,128)}) custom-call(f32[1024,1024]{1,0:T(8,128)} %bitcast.6, f32[512,1024]{1,0:T(8,128)} %bitcast.14, f32[8,128]{1,0:T(8,128)} %get-tuple-element.84.refs_2_), custom_call_target="tpu_custom_call" | custom-call | flops 5000000 | bytes 15000 | tf_op jit(solution)/shard_map/side/pallas_call | solution.py:438
  12.7 0.6 collective-permute-start.3
  13.3 1.6 %collective-permute-done.1.refs_1_ = f32[192,256]{1,0:T(8,128)S(1)} collective-permute-done((f32[192,256]{1,0:T(8,128)}, f32[192,256]{1,0:T(8,128)S(1)}, u32[]{:S(2)}, u32[]{:S(2)}) %collective-permute-start.1) | collective-permute-done | bytes 196640 | tf_op jit(solution)/shard_map/ppermute | solution.py:20
  14.8 0.0 copy-done.3
  14.9 0.0 copy-done.4
  14.9 0.0 copy-start.5
  14.9 0.7 copy-done.5
  15.5 10.7 %first.1 = (f32[256,256]{1,0:T(8,128)S(1)}, f32[256,256]{1,0:T(8,128)S(1)}, f32[192,128]{1,0:T(8,128)S(1)}, f32[8,128]{1,0:T(8,128)S(1)}) custom-call(f32[192,256]{1,0:T(8,128)S(1)} %copy-done.4, f32[192,256]{1,0:T(8,128)S(1)} %collective-permute-done.1.refs_1_, f32[448,256]{1,0:T(8,128)S(1)} %copy-done.3, f32[8,128]{1,0:T(8,128)S(1)} %copy-done.5), custom_call_target="tpu_custom_call" | custom-call | flops 5000000 | bytes 15000 | tf_op jit(solution)/shard_map/first/pallas_call | solution.py:438
  26.2 0.4 collective-permute-start.4
  26.7 0.4 collective-permute-done.refs_1_
  27.1 0.0 copy-start
  27.1 0.0 copy-start.1
  27.1 2.0 %collective-permute-start.2 = (f32[448,256]{1,0:T(8,128)S(1)}, f32[448,256]{1,0:T(8,128)S(1)}, u32[]{:S(2)}, u32[]{:S(2)}) collective-permute-start(f32[448,256]{1,0:T(8,128)S(1)} %get-tuple-element.87), channel_id=1, source_target_pairs={{0,16},{4,20},{8,24},{12,28},{16,0},{20,4},{24,8},{28,12},{1,17},{... | collective-permute-start | bytes 1376264 | tf_op jit(solution)/shard_map/ppermute | solution.py:20
  29.2 4.3 %collective-permute-done.3.refs_3_ = f32[256,768]{1,0:T(8,128)S(1)} collective-permute-done((f32[256,768]{1,0:T(8,128)}, f32[256,768]{1,0:T(8,128)S(1)}, u32[]{:S(2)}, u32[]{:S(2)}) %collective-permute-start.3) | collective-permute-done | bytes 786464 | tf_op jit(solution)/shard_map/ppermute | solution.py:20
  33.4 0.0 copy-done
  33.4 0.0 copy-done.1
  33.5 0.0 copy-done.2
  33.5 1.3 %middle.4 = (f32[256,256]{1,0:T(8,128)S(1)}, f32[256,256]{1,0:T(8,128)S(1)}, f32[8,128]{1,0:T(8,128)S(1)}) custom-call(f32[1024,1024]{1,0:T(8,128)S(1)} %bitcast.7, f32[512,1024]{1,0:T(8,128)S(1)} %bitcast.15, f32[256,768]{1,0:T(8,128)S(1)} %copy-done.2, f32[256,768]{1,0:T(8,128)S(1)} %collective-permute-done.3.refs_3_, ...), custom_call_target="tpu_custom_call" | custom-call | flops 5000000 | bytes 15000 | tf_op jit(solution)/shard_map/middle/pallas_call | solution.py:438
  34.8 0.3 collective-permute-start.7
  35.1 0.0 collective-permute-done.4.refs_0_
  35.1 0.9 collective-permute-start.5
  36.0 1.3 %middle.5 = (f32[256,256]{1,0:T(8,128)S(1)}, f32[256,256]{1,0:T(8,128)S(1)}, f32[8,128]{1,0:T(8,128)S(1)}) custom-call(f32[1024,1024]{1,0:T(8,128)S(1)} %bitcast.8, f32[512,1024]{1,0:T(8,128)S(1)} %bitcast.16, f32[256,768]{1,0:T(8,128)S(1)} %copy-done.2, f32[256,768]{1,0:T(8,128)S(1)} %collective-permute-done.3.refs_3_, ...), custom_call_target="tpu_custom_call" | custom-call | flops 5000000 | bytes 15000 | tf_op jit(solution)/shard_map/middle/pallas_call | solution.py:438
  37.3 0.6 side.4
  37.9 1.2 %collective-permute-start.6 = (f32[256,256]{1,0:T(8,128)S(1)}, f32[256,256]{1,0:T(8,128)S(1)}, u32[]{:S(2)}, u32[]{:S(2)}) collective-permute-start(f32[256,256]{1,0:T(8,128)S(1)} %get-tuple-element.107.refs_2_), channel_id=1, source_target_pairs={{0,16},{4,20},{8,24},{12,28},{16,0},{20,4},{24,8},{28,12},{1,17},{... | collective-permute-start | bytes 786440 | tf_op jit(solution)/shard_map/ppermute | solution.py:20
  39.1 2.6 %collective-permute-start.9 = (f32[256,256]{1,0:T(8,128)S(1)}, f32[256,256]{1,0:T(8,128)S(1)}, u32[]{:S(2)}, u32[]{:S(2)}) collective-permute-start(f32[256,256]{1,0:T(8,128)S(1)} %get-tuple-element.115.refs_1_), channel_id=1, source_target_pairs={{0,2},{1,3},{2,0},{3,1},{4,6},{5,7},{6,4},{7,5},{8,10},{9,11},{10,... | collective-permute-start | bytes 786440 | tf_op jit(solution)/shard_map/ppermute | solution.py:20
  41.8 0.5 side.5
  42.3 4.9 %known.1 = (f32[1024,1024]{1,0:T(8,128)S(1)}, bf16[1024,512]{1,0:T(8,128)(2,1)S(1)}, bf16[1024,512]{1,0:T(8,128)(2,1)S(1)}, f32[1024,1024]{1,0:T(8,128)}, f32[1024,1024]{1,0:T(8,128)}, /*index=5*/f32[8,128]{1,0:T(8,128)S(1)}) custom-call(f32[1024,1024]{1,0:T(8,128)S(1)} %bitcast.11, f32[512,1024]{1,0:T(8,128)S(1)} %bitcast.19, ...), custom_call_target="tpu_custom_call" | custom-call | flops 5000000 | bytes 15000 | tf_op jit(solution)/shard_map/known/pallas_call | solution.py:438
  47.3 0.0 collective-permute-done.5.refs_6_
  47.3 0.7 collective-permute-start.8
  48.0 0.0 collective-permute-done.2.refs_2_
  48.0 1.4 %build.1 = (f32[256,256]{1,0:T(8,128)S(1)}, f32[256,256]{1,0:T(8,128)S(1)}, f32[256,256]{1,0:T(8,128)S(1)}, f32[256,256]{1,0:T(8,128)S(1)}, f32[8,128]{1,0:T(8,128)S(1)}) custom-call(f32[448,256]{1,0:T(8,128)S(1)} %copy-done.3, f32[448,256]{1,0:T(8,128)S(1)} %collective-permute-done.refs_1_, f32[448,256]{1,0:T(8,128)S(1)} %collective-permute-done.2.refs_2_, ...), custom_call_target="tpu_custom_call" | custom-call | flops 700000000 | bytes 2100000 | tf_op jit(solution)/shard_map/build/pallas_call | solution.py:438
  49.4 5.3 %head.2 = (f32[128,128]{1,0:T(8,128)S(1)}, f32[128,128]{1,0:T(8,128)S(1)}, f32[128,128]{1,0:T(8,128)S(1)}, f32[8,128]{1,0:T(8,128)S(1)}) custom-call(f32[256,256]{1,0:T(8,128)S(1)} %get-tuple-element.100.refs_0_, f32[8,128]{1,0:T(8,128)S(1)} %get-tuple-element.101.refs_1_), custom_call_target="tpu_custom_call" | custom-call | flops 5000000 | bytes 15000 | tf_op jit(solution)/shard_map/head/pallas_call | solution.py:438
  54.7 0.0 collective-permute-done.7.refs_1_
  54.8 0.0 collective-permute-done.6.refs_3_
  54.8 1.3 %middle.6 = (f32[256,256]{1,0:T(8,128)S(1)}, f32[256,256]{1,0:T(8,128)S(1)}, f32[8,128]{1,0:T(8,128)S(1)}) custom-call(f32[1024,1024]{1,0:T(8,128)S(1)} %bitcast.12, f32[512,1024]{1,0:T(8,128)S(1)} %bitcast.20, f32[256,256]{1,0:T(8,128)S(1)} %get-tuple-element.107.refs_2_, f32[256,256]{1,0:T(8,128)S(1)} %collective-permute-done.6.refs_3_, ...), custom_call_target="tpu_custom_call" | custom-call | flops 5000000 | bytes 15000 | tf_op jit(solution)/shard_map/middle/pallas_call | solution.py:438
  56.1 0.5 collective-permute-start.10
  56.6 5.8 %turn.1 = (f32[256,256]{1,0:T(8,128)S(1)}, f32[256,256]{1,0:T(8,128)S(1)}, f32[256,256]{1,0:T(8,128)S(1)}, f32[8,128]{1,0:T(8,128)S(1)}) custom-call(f32[128,128]{1,0:T(8,128)S(1)} %get-tuple-element.102.refs_0_, f32[128,128]{1,0:T(8,128)S(1)} %get-tuple-element.103.refs_1_, f32[128,128]{1,0:T(8,128)S(1)} %get-tuple-element.104.refs_2_, ...), custom_call_target="tpu_custom_call" | custom-call | flops 5000000 | bytes 15000 | tf_op jit(solution)/shard_map/turn/pallas_call | solution.py:438
  62.4 0.0 collective-permute-done.9.refs_2_
  62.5 4.3 %collective-permute-start.15 = (f32[256,512]{1,0:T(8,128)S(1)}, f32[256,512]{1,0:T(8,128)S(1)}, u32[]{:S(2)}, u32[]{:S(2)}) collective-permute-start(f32[256,512]{1,0:T(8,128)S(1)} %get-tuple-element.143.refs_5_), channel_id=1, source_target_pairs={{0,16},{4,20},{8,24},{12,28},{16,0},{20,4},{24,8},{28,12},{1,17},{... | collective-permute-start | bytes 1572872 | tf_op jit(solution)/shard_map/ppermute | solution.py:20
  66.8 0.0 collective-permute-done.8.refs_3_
  66.8 1.3 %middle.7 = (f32[256,128]{1,0:T(8,128)S(1)}, f32[256,128]{1,0:T(8,128)S(1)}, f32[256,256]{1,0:T(8,128)S(1)}, f32[8,128]{1,0:T(8,128)S(1)}) custom-call(f32[1024,1024]{1,0:T(8,128)S(1)} %bitcast.13, f32[512,1024]{1,0:T(8,128)S(1)} %bitcast.21, f32[256,256]{1,0:T(8,128)S(1)} %get-tuple-element.113.refs_2_, f32[256,256]{1,0:T(8,128)S(1)} %collective-permute-done.8.refs_3_, ...), custom_call_target="tpu_custom_call" | custom-call | flops 5000000 | bytes 15000 | tf_op jit(solution)/shard_map/middle/pallas_call | solution.py:438
  68.1 0.1 collective-permute-start.11
  68.1 5.1 %head.3 = (f32[128,128]{1,0:T(8,128)S(1)}, f32[128,128]{1,0:T(8,128)S(1)}, f32[128,128]{1,0:T(8,128)S(1)}, f32[8,128]{1,0:T(8,128)S(1)}) custom-call(f32[256,256]{1,0:T(8,128)S(1)} %get-tuple-element.112.refs_0_, f32[8,128]{1,0:T(8,128)S(1)} %get-tuple-element.118.refs_1_), custom_call_target="tpu_custom_call" | custom-call | flops 5000000 | bytes 15000 | tf_op jit(solution)/shard_map/head/pallas_call | solution.py:438
  73.3 0.0 collective-permute-done.10.refs_1_
  73.3 3.0 %collective-permute-start.12 = (f32[256,128]{1,0:T(8,128)S(1)}, f32[256,128]{1,0:T(8,128)S(1)}, u32[]{:S(2)}, u32[]{:S(2)}) collective-permute-start(f32[256,128]{1,0:T(8,128)S(1)} %get-tuple-element.138.refs_0_), channel_id=1, source_target_pairs={{0,2},{1,3},{2,0},{3,1},{4,6},{5,7},{6,4},{7,5},{8,10},{9,11},{10,... | collective-permute-start | bytes 393224 | tf_op jit(solution)/shard_map/ppermute | solution.py:20
  76.3 0.0 collective-permute-start.14
  76.4 6.6 %tail.1 = (bf16[512,512]{1,0:T(8,128)(2,1)S(1)}, bf16[512,512]{1,0:T(8,128)(2,1)S(1)}, f32[8,128]{1,0:T(8,128)S(1)}) custom-call(f32[128,128]{1,0:T(8,128)S(1)} %get-tuple-element.119.refs_0_, f32[128,128]{1,0:T(8,128)S(1)} %get-tuple-element.120.refs_1_, f32[128,128]{1,0:T(8,128)S(1)} %get-tuple-element.121.refs_2_, ...), custom_call_target="tpu_custom_call" | custom-call | flops 5000000 | bytes 15000 | tf_op jit(solution)/shard_map/tail/pallas_call | solution.py:438
  83.0 0.0 collective-permute-done.11.refs_1_
  83.0 2.0 %collective-permute-start.13 = (f32[256,128]{1,0:T(8,128)S(1)}, f32[256,128]{1,0:T(8,128)S(1)}, u32[]{:S(2)}, u32[]{:S(2)}) collective-permute-start(f32[256,128]{1,0:T(8,128)S(1)} %get-tuple-element.137.refs_5_), channel_id=1, source_target_pairs={{0,16},{4,20},{8,24},{12,28},{16,0},{20,4},{24,8},{28,12},{1,17},{... | collective-permute-start | bytes 393224 | tf_op jit(solution)/shard_map/ppermute | solution.py:20
  85.1 0.0 collective-permute-done.12.refs_1_
  85.1 0.1 collective-permute-start.16
  85.2 0.0 collective-permute-done.15.refs_6_
  85.2 3.9 %last.3 = (f32[1024,1024]{1,0:T(8,128)}, f32[1024,1024]{1,0:T(8,128)}, f32[8,128]{1,0:T(8,128)S(1)}) custom-call(bf16[512,512]{1,0:T(8,128)(2,1)S(1)} %get-tuple-element.130.refs_0_, bf16[512,512]{1,0:T(8,128)(2,1)S(1)} %get-tuple-element.131.refs_1_, ...), custom_call_target="tpu_custom_call", output_to_operand_aliasing={{1}: (9, {}), {0}: (10, {})} | custom-call | flops 5000000 | bytes 15000 | tf_op jit(solution)/shard_map/last/pallas_call | solution.py:438
  89.2 0.0 collective-permute-done.14.refs_6_
  89.2 3.2 %last.4 = (f32[1024,1024]{1,0:T(8,128)}, f32[1024,1024]{1,0:T(8,128)}, f32[8,128]{1,0:T(8,128)S(1)}) custom-call(bf16[512,512]{1,0:T(8,128)(2,1)S(1)} %get-tuple-element.130.refs_0_, bf16[512,512]{1,0:T(8,128)(2,1)S(1)} %get-tuple-element.131.refs_1_, ...), custom_call_target="tpu_custom_call", output_to_operand_aliasing={{1}: (8, {}), {0}: (9, {})} | custom-call | flops 5000000 | bytes 15000 | tf_op jit(solution)/shard_map/last/pallas_call | solution.py:438
  92.4 0.0 collective-permute-done.13.refs_0_
  92.4 0.0 collective-permute-done.16.refs_8_
  92.5 3.0 %last.5 = (f32[1024,1024]{1,0:T(8,128)}, f32[1024,1024]{1,0:T(8,128)}, f32[8,128]{1,0:T(8,128)}) custom-call(bf16[512,512]{1,0:T(8,128)(2,1)S(1)} %get-tuple-element.130.refs_0_, bf16[512,512]{1,0:T(8,128)(2,1)S(1)} %get-tuple-element.131.refs_1_, bf16[1024,512]{1,0:T(8,128)(2,1)S(1)} %get-tuple-element.132.refs_2_, ...), custom_call_target="tpu_custom_call", output_to_operand_aliasing={{1}: (10, {}), {0}: (11, {})} | custom-call | flops 5000000 | bytes 15000 | tf_op jit(solution)/shard_map/last/pallas_call | solution.py:438
  (10 shorter events, 0.2 us)
Async XLA Ops:
  2.4 24.7 %collective-permute-start = (f32[448,256]{1,0:T(8,128)}, f32[448,256]{1,0:T(8,128)S(1)}, u32[]{:S(2)}, u32[]{:S(2)}) collective-permute-start(f32[448,256]{1,0:T(8,128)} %get-tuple-element.81.refs_2_.refs_0_), channel_id=1, source_target_pairs={{0,2},{1,3},{2,0},{3,1},{4,6},{5,7},{6,4},{7,5},{8,10},{9,11},{10,... | collective-permute-start | bytes 1376264 | tf_op jit(solution)/shard_map/ppermute | solution.py:20
  8.1 6.7 %copy-start.3 = (f32[448,256]{1,0:T(8,128)S(1)}, f32[448,256]{1,0:T(8,128)}, u32[]{:S(2)}) copy-start(f32[448,256]{1,0:T(8,128)} %get-tuple-element.81.refs_2_.refs_0_) | copy-start | bytes 1376260
  8.1 6.7 %copy-start.4 = (f32[192,256]{1,0:T(8,128)S(1)}, f32[192,256]{1,0:T(8,128)}, u32[]{:S(2)}) copy-start(f32[192,256]{1,0:T(8,128)} %get-tuple-element.83.refs_0_) | copy-start | bytes 589828
  8.2 6.7 %collective-permute-start.1 = (f32[192,256]{1,0:T(8,128)}, f32[192,256]{1,0:T(8,128)S(1)}, u32[]{:S(2)}, u32[]{:S(2)}) collective-permute-start(f32[192,256]{1,0:T(8,128)} %get-tuple-element.83.refs_0_), channel_id=1, source_target_pairs={{0,16},{4,20},{8,24},{12,28},{16,0},{20,4},{24,8},{28,12},{1,17},{... | collective-permute-start | bytes 589832 | tf_op jit(solution)/shard_map/ppermute | solution.py:20
  12.7 20.8 %collective-permute-start.3 = (f32[256,768]{1,0:T(8,128)}, f32[256,768]{1,0:T(8,128)S(1)}, u32[]{:S(2)}, u32[]{:S(2)}) collective-permute-start(f32[256,768]{1,0:T(8,128)} %get-tuple-element.88.refs_2_), channel_id=1, source_target_pairs={{0,16},{4,20},{8,24},{12,28},{16,0},{20,4},{24,8},{28,12},{1,17},{... | collective-permute-start | bytes 2359304 | tf_op jit(solution)/shard_map/ppermute | solution.py:20
  14.9 0.7 copy-start.5
  26.2 8.9 %collective-permute-start.4 = (f32[192,128]{1,0:T(8,128)S(1)}, f32[192,128]{1,0:T(8,128)S(1)}, u32[]{:S(2)}, u32[]{:S(2)}) collective-permute-start(f32[192,128]{1,0:T(8,128)S(1)} %get-tuple-element.90), channel_id=1, source_target_pairs={{0,2},{1,3},{2,0},{3,1},{4,6},{5,7},{6,4},{7,5},{8,10},{9,11},{10,... | collective-permute-start | bytes 294920 | tf_op jit(solution)/shard_map/ppermute | solution.py:20
  27.1 6.4 %copy-start = (f32[1,1,1024,1024]{3,2,1,0:T(8,128)S(1)}, f32[1,1,1024,1024]{3,2,1,0:T(8,128)}, u32[]{:S(2)}) copy-start(f32[1,1,1024,1024]{3,2,1,0:T(8,128)} %param.2) | copy-start | bytes 12582916
  27.1 6.4 %copy-start.1 = (f32[1,1,512,1024]{3,2,1,0:T(8,128)S(1)}, f32[1,1,512,1024]{3,2,1,0:T(8,128)}, u32[]{:S(2)}) copy-start(f32[1,1,512,1024]{3,2,1,0:T(8,128)} %param.3) | copy-start | bytes 6291460
  27.1 6.4 %copy-start.2 = (f32[256,768]{1,0:T(8,128)S(1)}, f32[256,768]{1,0:T(8,128)}, u32[]{:S(2)}) copy-start(f32[256,768]{1,0:T(8,128)} %get-tuple-element.88.refs_2_) | copy-start | bytes 2359300
  27.1 20.8 %collective-permute-start.2 = (f32[448,256]{1,0:T(8,128)S(1)}, f32[448,256]{1,0:T(8,128)S(1)}, u32[]{:S(2)}, u32[]{:S(2)}) collective-permute-start(f32[448,256]{1,0:T(8,128)S(1)} %get-tuple-element.87), channel_id=1, source_target_pairs={{0,16},{4,20},{8,24},{12,28},{16,0},{20,4},{24,8},{28,12},{1,17},{... | collective-permute-start | bytes 1376264 | tf_op jit(solution)/shard_map/ppermute | solution.py:20
  34.8 20.0 %collective-permute-start.7 = (f32[256,256]{1,0:T(8,128)S(1)}, f32[256,256]{1,0:T(8,128)S(1)}, u32[]{:S(2)}, u32[]{:S(2)}) collective-permute-start(f32[256,256]{1,0:T(8,128)S(1)} %get-tuple-element.108.refs_0_), channel_id=1, source_target_pairs={{0,2},{1,3},{2,0},{3,1},{4,6},{5,7},{6,4},{7,5},{8,10},{9,11},{10,... | collective-permute-start | bytes 786440 | tf_op jit(solution)/shard_map/ppermute | solution.py:20
  35.1 12.2 %collective-permute-start.5 = (f32[192,128]{1,0:T(8,128)S(1)}, f32[192,128]{1,0:T(8,128)S(1)}, u32[]{:S(2)}, u32[]{:S(2)}) collective-permute-start(f32[192,128]{1,0:T(8,128)S(1)} %get-tuple-element.94.refs_5_), channel_id=1, source_target_pairs={{0,16},{4,20},{8,24},{12,28},{16,0},{20,4},{24,8},{28,12},{1,17},{... | collective-permute-start | bytes 294920 | tf_op jit(solution)/shard_map/ppermute | solution.py:20
  37.9 16.9 %collective-permute-start.6 = (f32[256,256]{1,0:T(8,128)S(1)}, f32[256,256]{1,0:T(8,128)S(1)}, u32[]{:S(2)}, u32[]{:S(2)}) collective-permute-start(f32[256,256]{1,0:T(8,128)S(1)} %get-tuple-element.107.refs_2_), channel_id=1, source_target_pairs={{0,16},{4,20},{8,24},{12,28},{16,0},{20,4},{24,8},{28,12},{1,17},{... | collective-permute-start | bytes 786440 | tf_op jit(solution)/shard_map/ppermute | solution.py:20
  39.1 23.3 %collective-permute-start.9 = (f32[256,256]{1,0:T(8,128)S(1)}, f32[256,256]{1,0:T(8,128)S(1)}, u32[]{:S(2)}, u32[]{:S(2)}) collective-permute-start(f32[256,256]{1,0:T(8,128)S(1)} %get-tuple-element.115.refs_1_), channel_id=1, source_target_pairs={{0,2},{1,3},{2,0},{3,1},{4,6},{5,7},{6,4},{7,5},{8,10},{9,11},{10,... | collective-permute-start | bytes 786440 | tf_op jit(solution)/shard_map/ppermute | solution.py:20
  47.3 19.5 %collective-permute-start.8 = (f32[256,256]{1,0:T(8,128)S(1)}, f32[256,256]{1,0:T(8,128)S(1)}, u32[]{:S(2)}, u32[]{:S(2)}) collective-permute-start(f32[256,256]{1,0:T(8,128)S(1)} %get-tuple-element.113.refs_2_), channel_id=1, source_target_pairs={{0,16},{4,20},{8,24},{12,28},{16,0},{20,4},{24,8},{28,12},{1,17},{... | collective-permute-start | bytes 786440 | tf_op jit(solution)/shard_map/ppermute | solution.py:20
  56.1 17.2 %collective-permute-start.10 = (f32[256,256]{1,0:T(8,128)S(1)}, f32[256,256]{1,0:T(8,128)S(1)}, u32[]{:S(2)}, u32[]{:S(2)}) collective-permute-start(f32[256,256]{1,0:T(8,128)S(1)} %get-tuple-element.126.refs_0_), channel_id=1, source_target_pairs={{0,2},{1,3},{2,0},{3,1},{4,6},{5,7},{6,4},{7,5},{8,10},{9,11},{10,... | collective-permute-start | bytes 786440 | tf_op jit(solution)/shard_map/ppermute | solution.py:20
  62.5 22.8 %collective-permute-start.15 = (f32[256,512]{1,0:T(8,128)S(1)}, f32[256,512]{1,0:T(8,128)S(1)}, u32[]{:S(2)}, u32[]{:S(2)}) collective-permute-start(f32[256,512]{1,0:T(8,128)S(1)} %get-tuple-element.143.refs_5_), channel_id=1, source_target_pairs={{0,16},{4,20},{8,24},{12,28},{16,0},{20,4},{24,8},{28,12},{1,17},{... | collective-permute-start | bytes 1572872 | tf_op jit(solution)/shard_map/ppermute | solution.py:20
  68.1 15.0 %collective-permute-start.11 = (f32[256,128]{1,0:T(8,128)S(1)}, f32[256,128]{1,0:T(8,128)S(1)}, u32[]{:S(2)}, u32[]{:S(2)}) collective-permute-start(f32[256,128]{1,0:T(8,128)S(1)} %get-tuple-element.135.refs_0_), channel_id=1, source_target_pairs={{0,2},{1,3},{2,0},{3,1},{4,6},{5,7},{6,4},{7,5},{8,10},{9,11},{10,... | collective-permute-start | bytes 393224 | tf_op jit(solution)/shard_map/ppermute | solution.py:20
  73.3 11.8 %collective-permute-start.12 = (f32[256,128]{1,0:T(8,128)S(1)}, f32[256,128]{1,0:T(8,128)S(1)}, u32[]{:S(2)}, u32[]{:S(2)}) collective-permute-start(f32[256,128]{1,0:T(8,128)S(1)} %get-tuple-element.138.refs_0_), channel_id=1, source_target_pairs={{0,2},{1,3},{2,0},{3,1},{4,6},{5,7},{6,4},{7,5},{8,10},{9,11},{10,... | collective-permute-start | bytes 393224 | tf_op jit(solution)/shard_map/ppermute | solution.py:20
  76.3 12.9 %collective-permute-start.14 = (f32[256,256]{1,0:T(8,128)S(1)}, f32[256,256]{1,0:T(8,128)S(1)}, u32[]{:S(2)}, u32[]{:S(2)}) collective-permute-start(f32[256,256]{1,0:T(8,128)S(1)} %get-tuple-element.141.refs_5_), channel_id=1, source_target_pairs={{0,16},{4,20},{8,24},{12,28},{16,0},{20,4},{24,8},{28,12},{1,17},{... | collective-permute-start | bytes 786440 | tf_op jit(solution)/shard_map/ppermute | solution.py:20
  83.0 9.4 %collective-permute-start.13 = (f32[256,128]{1,0:T(8,128)S(1)}, f32[256,128]{1,0:T(8,128)S(1)}, u32[]{:S(2)}, u32[]{:S(2)}) collective-permute-start(f32[256,128]{1,0:T(8,128)S(1)} %get-tuple-element.137.refs_5_), channel_id=1, source_target_pairs={{0,16},{4,20},{8,24},{12,28},{16,0},{20,4},{24,8},{28,12},{1,17},{... | collective-permute-start | bytes 393224 | tf_op jit(solution)/shard_map/ppermute | solution.py:20
  85.1 7.3 %collective-permute-start.16 = (f32[256,128]{1,0:T(8,128)S(1)}, f32[256,128]{1,0:T(8,128)S(1)}, u32[]{:S(2)}, u32[]{:S(2)}) collective-permute-start(f32[256,128]{1,0:T(8,128)S(1)} %get-tuple-element.140.refs_6_), channel_id=1, source_target_pairs={{0,16},{4,20},{8,24},{12,28},{16,0},{20,4},{24,8},{28,12},{1,17},{... | collective-permute-start | bytes 393224 | tf_op jit(solution)/shard_map/ppermute | solution.py:20

commit v2 on v1

--- a/solution.py
+++ b/solution.py
@@ -205,6 +205,52 @@
     out[...] = own[...] + other[...]
 
 
+def outer_rows(leaf, edge, rows, sems):
+    n = rows.shape[0]
+    _, x, _, d = edges()
+    own = pl.ds(pl.multiple_of(edge * n, n), n)
+    return [
+        pltpu.make_async_copy(leaf.at[own, pl.ds(pl.multiple_of(e * n, n), n)], rows.at[:, pl.ds(p * n, n)], sems.at[p])
+        for p, e in enumerate((x, d))
+    ]
+
+
+def side_kernel(base, leaf, data, out, rows, held, sems):
+    n, width = rows.shape[0], held.shape[1]
+    i, _, y, _ = edges()
+    copies = outer_rows(leaf, i, rows, sems)
+    copies.append(pltpu.make_async_copy(data.at[:, pl.ds(base, width)], held, sems.at[2]))
+    for copy in copies:
+        copy.start()
+    if out.shape[1] > width:
+        whole = leaf.at[pl.ds(pl.multiple_of(y * n, n), n), pl.ds(pl.multiple_of(i * n, n), n)]
+        fetch([(whole, out.at[:, pl.ds(width, n)])], sems.at[pl.ds(3, 1)])
+    for copy in copies:
+        copy.wait()
+    out[:, :width] = triple(split(rows[...]), split(held[...]))
+
+
+def blocks_kernel(leaf, joined, middle, sems):
+    n = joined.shape[1]
+    i, _, y, _ = edges()
+    whole = leaf.at[pl.ds(pl.multiple_of(y * n, n), n), pl.ds(pl.multiple_of(i * n, n), n)]
+    fetch([(whole, middle.at[pl.ds(0, n)])] + symmetric(leaf, y, middle, n) + symmetric(leaf, i, joined, 0), sems)
+
+
+def passing_kernel(middle, middle_z, out):
+    n = out.shape[1]
+    out[:n] = middle_z[:n]
+    out[n:] = middle[n:] + middle_z[n:]
+
+
+def relay_kernel(given, out):
+    out[...] = given[...]
+
+
+def sum_kernel(own, other, out):
+    out[...] = own[...] + other[...]
+
+
 def append_kernel(before, own, other, out):
     width = before.shape[1]
     out[:, :width] = before[...]
@@ -374,27 +420,26 @@
     n, width = w_own[0].shape[0], solved.shape[1]
     i, _, y, _ = edges()
     cols = pl.ds(base, width)
-    done = 0
+    tops, rests, done = [], [], 0
+    shift = jnp.concatenate([start[...] for start in starts], 1)
     for own, far in zip(w_own, w_far):
         part = slice(done, done + own.shape[1])
         inner = triple((solve_high[...], solve_low[...]), split(jnp.concatenate([own[...], far[...]], 0)))
-        solved[:, part] = inner
+        tops.append(inner[:n] + shift[:, part])
+        rests.append(inner[n:])
         done = part.stop
-    done = 0
-    for start in starts:
-        part = slice(done, done + start.shape[1])
-        solved[:n, part] += start[...]
-        done = part.stop
-    right = split(solved[...])
+    values = jnp.concatenate([jnp.concatenate(tops, 1), jnp.concatenate(rests, 1)], 0)
+    solved[...] = values
     copies = []
+    for p, e in enumerate((i, y)):
+        rows = pl.ds(pl.multiple_of(e * n, n), n)
+        copies.append(pltpu.make_async_copy(solved.at[pl.ds(p * n, n), :], potential.at[rows, cols], sems.at[4 + p]))
+        copies[-1].start()
+    right = split(values)
     for k in range(4):
         rows = pl.ds(k * n, n)
         made[rows] = known[rows, base : base + width] + triple((high[rows], low[rows]), right)
         copies.append(pltpu.make_async_copy(made.at[rows], flux.at[rows, cols], sems.at[k]))
-        copies[-1].start()
-    for p, e in enumerate((i, y)):
-        rows = pl.ds(pl.multiple_of(e * n, n), n)
-        copies.append(pltpu.make_async_copy(solved.at[pl.ds(p * n, n), :], potential.at[rows, cols], sems.at[4 + p]))
         copies[-1].start()
     for copy in copies:
         copy.wait()
@@ -417,7 +462,7 @@
     "build": 0.7,
     "opening": 1.2,
     "copy": 0.05,
-    "closing": 2.0,
+    "closing": 0.3,
 }
 
 
@@ -460,24 +505,28 @@
     dma = pltpu.SemaphoreType.DMA
     call = Chain()
     unit = count // 8
-    widths = [2 * unit, 2 * unit, 2 * unit, unit, unit]
-    bases = [0, 2 * unit, 4 * unit, 6 * unit, 7 * unit]
-
-    middle = call(
-        "crossing", crossing_kernel, [array(n + packed, n)], leaf, limit=EARLY, ins=[HBM], scratch=[dma((5,))]
+    widths = [2 * unit] * 4
+    bases = [0, 2 * unit, 4 * unit, 6 * unit]
+
+    joined, middle = call(
+        "blocks",
+        blocks_kernel,
+        [array(packed, n), array(n + packed, n)],
+        leaf,
+        limit=EARLY,
+        ins=[HBM],
+        scratch=[dma((9,))],
     )
     middle_z = exchange(middle, "gy")
-    joined = call("joined", joined_kernel, [array(packed, n)], leaf, limit=EARLY, ins=[HBM], scratch=[dma((4,))])
     joined_far = exchange(joined, "gx")
 
-    def sides(base, width, extra=0, limit=24):
+    def sides(base, width, extra=0):
         own = call(
             "side",
             functools.partial(side_kernel, base),
             [array(n, width + extra)],
             leaf,
             data,
-            limit=limit,
             ins=[HBM] * 2,
             scratch=[pltpu.VMEM((n, 2 * n), F32), pltpu.VMEM((2 * n, width), F32), dma((4,))],
         )
@@ -507,21 +556,11 @@
     def copy(given, name="copy"):
         return call(name, relay_kernel, [array(*given.shape)], given)
 
-    own_a, far_a = sides(0, 4 * unit, n, EARLY)
+    own_a, far_a = sides(0, 4 * unit, n)
     inverse1, across, half = call(
         "first", first_kernel, [array(n, n)] * 2 + [array(packed, h)], joined, joined_far, middle
     )
     half_z = exchange(half, "gy")
-    passing = call("passing", passing_kernel, [array(n + packed, n)], middle, middle_z)
-    passed = exchange(passing, "gx")
-    (v0,), start0 = middles([0], 0, own_a, far_a)
-    z0 = exchange(v0, "gy")
-    half_z = copy(half_z, "relay")
-    half_x = exchange(half_z, "gx")
-    (v1,), start1 = middles([1], 0, own_a, far_a)
-    z1 = exchange(v1, "gy")
-    own_b, far_b = sides(bases[2], widths[2])
-    own_c, far_c = sides(bases[3], 2 * unit)
     known, high, low, potential, flux = call(
         "known",
         known_kernel,
@@ -545,6 +584,15 @@
         scratch=[pltpu.VMEM((2 * n, count), BF16), pltpu.VMEM((2 * n, count), BF16), dma((2,))],
         grid=(4,),
     )
+    passing = call("passing", passing_kernel, [array(n + packed, n)], middle, middle_z)
+    passed = exchange(passing, "gx")
+    (v0,), start0 = middles([0], 0, own_a, far_a)
+    z0 = exchange(v0, "gy")
+    half_z = copy(half_z, "relay")
+    half_x = exchange(half_z, "gx")
+    (v1,), start1 = middles([1], 0, own_a, far_a)
+    z1 = exchange(v1, "gy")
+    own_b, far_b = sides(bases[2], widths[2])
     across_far, s_own, s_off, s_far = call(
         "build",
         build_kernel,
@@ -559,24 +607,20 @@
         across,
         scratch=[pltpu.VMEM((n, n), F32)],
     )
+    own_c, far_c = sides(bases[3], 2 * unit)
     head, reach, rest = call("head", head_kernel, [array(h, h)] * 3, s_own)
-    w0 = call("opening", sum_kernel, [array(*v0.shape)], v0, z0)
+    w0, w0_far = total(v0, z0, "opening")
     (v2,), start2 = middles([2], bases[2], own_b, far_b)
     z2 = exchange(v2, "gy")
     done, wide, left = call("turn", turn_kernel, [array(n, n)] * 3, head, reach, rest, s_off, s_far)
-    w1 = call("append", append_kernel, [array(n, 4 * unit)], w0, v1, z1)
-    w1_far = exchange(w1, "gx")
-    (v3, v4), start3 = middles([3, 4], bases[3], own_c, far_c)
+    w1, w1_far = total(v1, z1)
+    (v3,), start3 = middles([3], bases[3], own_c, far_c)
     z3 = exchange(v3, "gy")
     head, reach, rest = call("head", head_kernel, [array(h, h)] * 3, left)
     w2, w2_far = total(v2, z2)
-    v4 = copy(v4)
-    z4 = exchange(v4, "gy")
     inverse2 = call(
         "tail", tail_kernel, [array(2 * n, 2 * n, dtype=BF16)] * 2, head, reach, rest, done, wide, across, across_far
     )
-    w3, w3_far = total(v3, z3)
-    w4, w4_far = total(v4, z4, "closing")
 
     def last(base, own, far, starts, held):
         width = sum(part.shape[1] for part in own)
@@ -600,10 +644,10 @@
             aliases={fixed: 1, fixed + 1: 0},
         )
 
-    held = last(0, [w1], [w1_far], [start0, start1], [flux, potential])
-    held = last(bases[2], [w2], [w2_far], [start2], held)
-    w3_far = copy(w3_far)
-    held = last(bases[3], [w3, w4], [w3_far, w4_far], [start3], held)
+    w3, w3_far = total(v3, z3, "closing")
+    w0_far = copy(w0_far)
+    held = last(0, [w0, w1, w2], [w0_far, w1_far, w2_far], [start0, start1, start2], [flux, potential])
+    held = last(bases[3], [w3], [w3_far], [start3], held)
     return held[1][None, None], held[0][None, None]
 
 

time: 95.8 us -> 94.8 us (0.990)
  Pallas kernels: 62.8 us -> 57.7 us
  waiting for transfers between devices: 6.32 us -> 10.1 us
  local copies, waits for them, and re-layouts: 0.7 us -> 2.29 us
  starting transfers between devices: 24.6 us -> 23.2 us
    pallas_call x28 -> x24, Pallas kernels: 62.8 us -> 57.7 us  [__call__(): pl.pallas_call(body, out_shape=list(outs) + [array(8, LANES)], in_specs=l...]
    ppermute x17 -> x16, waiting for transfers between devices: 6.32 us -> 10.1 us  [exchange(): return lax.ppermute(block, axis, [(i, i ^ half) for i in range(2 * half)])]
    unnamed x12, local copies, waits for them, and re-layouts: 0.7 us -> 2.29 us
    ppermute x17 -> x16, starting transfers between devices: 24.6 us -> 23.2 us  [exchange(): return lax.ppermute(block, axis, [(i, i ^ half) for i in range(2 * half)])]
  transfers between devices with their start and end apart: 17 -> 16, of which waited for: 3 -> 4; matrix products, arithmetic and copies ran while one was open for 0% -> 0% of each run, Pallas kernels for 61% -> 56%
where the time goes in v2:
time: 94.8 us; the launch traced here: 94.4 us
  Pallas kernels  57.7 us (61%)
  starting transfers between devices  23.2 us (24%)
  waiting for transfers between devices  10.1 us (11%)
  local copies, waits for them, and re-layouts  2.29 us (2%)
  between operations  1.06 us (1%)
    pallas_call x24, Pallas kernels, __call__(): pl.pallas_call(body, out_shape=list(outs) + [array(8, LANES)], in_specs=l...  57.7 us
    ppermute x16, starting transfers between devices, exchange(): return lax.ppermute(block, axis, [(i, i ^ half) for i in range(2 * half)])  23.2 us
    ppermute x16, waiting for transfers between devices, exchange(): return lax.ppermute(block, axis, [(i, i ^ half) for i in range(2 * half)])  10.1 us
    unnamed x12, local copies, waits for them, and re-layouts  2.29 us
  transfers between devices with their start and end apart: 16, of which 4 were waited for; matrix products, arithmetic and copies ran while one was open for 0% of the time, Pallas kernels for 56%

profile of v2, /device:TPU:0, one launch (start us, length us, event | category | flops | bytes accessed | tf_op | source)
XLA Modules:
  0.0 94.4 jit_solution(1363869505113933748)
XLA Ops:
  0.6 0.0 copy-start
  0.6 2.1 %blocks.1 = (f32[192,256]{1,0:T(8,128)}, f32[448,256]{1,0:T(8,128)}, f32[8,128]{1,0:T(8,128)}) custom-call(f32[1024,1024]{1,0:T(8,128)} %bitcast.4), custom_call_target="tpu_custom_call" | custom-call | flops 5000000 | bytes 15000 | tf_op jit(solution)/shard_map/blocks/pallas_call | solution.py:483
  2.8 4.1 %collective-permute-start = (f32[448,256]{1,0:T(8,128)}, f32[448,256]{1,0:T(8,128)S(1)}, u32[]{:S(2)}, u32[]{:S(2)}) collective-permute-start(f32[448,256]{1,0:T(8,128)} %get-tuple-element.72.refs_2_.refs_0_), channel_id=1, source_target_pairs={{0,2},{1,3},{2,0},{3,1},{4,6},{5,7},{6,4},{7,5},{8,10},{9,11},{10,... | collective-permute-start | bytes 1376264 | tf_op jit(solution)/shard_map/ppermute | solution.py:20
  6.9 1.5 %collective-permute-start.1 = (f32[192,256]{1,0:T(8,128)}, f32[192,256]{1,0:T(8,128)S(1)}, u32[]{:S(2)}, u32[]{:S(2)}) collective-permute-start(f32[192,256]{1,0:T(8,128)} %get-tuple-element.73.refs_0_), channel_id=1, source_target_pairs={{0,16},{4,20},{8,24},{12,28},{16,0},{20,4},{24,8},{28,12},{1,17},{... | collective-permute-start | bytes 589832 | tf_op jit(solution)/shard_map/ppermute | solution.py:20
  8.4 0.0 copy-done
  8.4 0.0 copy-start.1
  8.4 1.6 %copy-done.1 = f32[1,1,512,1024]{3,2,1,0:T(8,128)S(1)} copy-done((f32[1,1,512,1024]{3,2,1,0:T(8,128)S(1)}, f32[1,1,512,1024]{3,2,1,0:T(8,128)}, u32[]{:S(2)}) %copy-start.1) | copy-done | bytes 2097176
  10.0 0.0 copy-start.5
  10.0 0.7 copy-done.5
  10.7 0.0 copy-start.3
  10.7 0.0 copy-start.4
  10.7 0.0 copy-start.2
  10.7 0.8 side.3
  11.5 0.6 collective-permute-start.3
  12.1 1.4 %collective-permute-done.1.refs_1_ = f32[192,256]{1,0:T(8,128)S(1)} collective-permute-done((f32[192,256]{1,0:T(8,128)}, f32[192,256]{1,0:T(8,128)S(1)}, u32[]{:S(2)}, u32[]{:S(2)}) %collective-permute-start.1) | collective-permute-done | bytes 196640 | tf_op jit(solution)/shard_map/ppermute | solution.py:20
  13.5 0.0 copy-done.3
  13.5 0.0 copy-done.4
  13.5 10.7 %first.1 = (f32[256,256]{1,0:T(8,128)S(1)}, f32[256,256]{1,0:T(8,128)S(1)}, f32[192,128]{1,0:T(8,128)S(1)}, f32[8,128]{1,0:T(8,128)S(1)}) custom-call(f32[192,256]{1,0:T(8,128)S(1)} %copy-done.4, f32[192,256]{1,0:T(8,128)S(1)} %collective-permute-done.1.refs_1_, f32[448,256]{1,0:T(8,128)S(1)} %copy-done.3, f32[8,128]{1,0:T(8,128)S(1)} %get-tuple-element.75.refs_3_), custom_call_target="tpu_custom_call" | custom-call | flops 5000000 | bytes 15000 | tf_op jit(solution)/shard_map/first/pallas_call | solution.py:483
  24.2 0.3 collective-permute-start.4
  24.6 0.0 copy-done.2
  24.6 4.9 %known.1 = (f32[1024,1024]{1,0:T(8,128)S(1)}, bf16[1024,512]{1,0:T(8,128)(2,1)S(1)}, bf16[1024,512]{1,0:T(8,128)(2,1)S(1)}, f32[1024,1024]{1,0:T(8,128)}, f32[1024,1024]{1,0:T(8,128)}, /*index=5*/f32[8,128]{1,0:T(8,128)S(1)}) custom-call(f32[1024,1024]{1,0:T(8,128)S(1)} %bitcast.6, f32[512,1024]{1,0:T(8,128)S(1)} %bitcast.14, ...), custom_call_target="tpu_custom_call" | custom-call | flops 5000000 | bytes 15000 | tf_op jit(solution)/shard_map/known/pallas_call | solution.py:483
  29.5 0.0 collective-permute-done.refs_1_
  29.5 2.4 %collective-permute-start.2 = (f32[448,256]{1,0:T(8,128)S(1)}, f32[448,256]{1,0:T(8,128)S(1)}, u32[]{:S(2)}, u32[]{:S(2)}) collective-permute-start(f32[448,256]{1,0:T(8,128)S(1)} %get-tuple-element.78), channel_id=1, source_target_pairs={{0,16},{4,20},{8,24},{12,28},{16,0},{20,4},{24,8},{28,12},{1,17},{... | collective-permute-start | bytes 1376264 | tf_op jit(solution)/shard_map/ppermute | solution.py:20
  31.9 0.0 collective-permute-done.3.refs_3_
  31.9 1.3 %middle.4 = (f32[256,256]{1,0:T(8,128)S(1)}, f32[256,256]{1,0:T(8,128)S(1)}, f32[8,128]{1,0:T(8,128)S(1)}) custom-call(f32[1024,1024]{1,0:T(8,128)S(1)} %bitcast.7, f32[512,1024]{1,0:T(8,128)S(1)} %bitcast.15, f32[256,768]{1,0:T(8,128)S(1)} %get-tuple-element.79.refs_2_, f32[256,768]{1,0:T(8,128)S(1)} %collective-permute-done.3.refs_3_, ...), custom_call_target="tpu_custom_call" | custom-call | flops 5000000 | bytes 15000 | tf_op jit(solution)/shard_map/middle/pallas_call | solution.py:483
  33.1 0.0 collective-permute-done.4.refs_0_
  33.2 0.1 collective-permute-start.5
  33.3 2.8 %collective-permute-start.7 = (f32[256,256]{1,0:T(8,128)S(1)}, f32[256,256]{1,0:T(8,128)S(1)}, u32[]{:S(2)}, u32[]{:S(2)}) collective-permute-start(f32[256,256]{1,0:T(8,128)S(1)} %get-tuple-element.98.refs_0_), channel_id=1, source_target_pairs={{0,2},{1,3},{2,0},{3,1},{4,6},{5,7},{6,4},{7,5},{8,10},{9,11},{10,... | collective-permute-start | bytes 786440 | tf_op jit(solution)/shard_map/ppermute | solution.py:20
  36.1 1.3 %middle.5 = (f32[256,256]{1,0:T(8,128)S(1)}, f32[256,256]{1,0:T(8,128)S(1)}, f32[8,128]{1,0:T(8,128)S(1)}) custom-call(f32[1024,1024]{1,0:T(8,128)S(1)} %bitcast.8, f32[512,1024]{1,0:T(8,128)S(1)} %bitcast.16, f32[256,768]{1,0:T(8,128)S(1)} %get-tuple-element.79.refs_2_, f32[256,768]{1,0:T(8,128)S(1)} %collective-permute-done.3.refs_3_, ...), custom_call_target="tpu_custom_call" | custom-call | flops 5000000 | bytes 15000 | tf_op jit(solution)/shard_map/middle/pallas_call | solution.py:483
  37.4 0.6 side.4
  37.9 2.0 %collective-permute-start.6 = (f32[256,256]{1,0:T(8,128)S(1)}, f32[256,256]{1,0:T(8,128)S(1)}, u32[]{:S(2)}, u32[]{:S(2)}) collective-permute-start(f32[256,256]{1,0:T(8,128)S(1)} %get-tuple-element.97.refs_2_), channel_id=1, source_target_pairs={{0,16},{4,20},{8,24},{12,28},{16,0},{20,4},{24,8},{28,12},{1,17},{... | collective-permute-start | bytes 786440 | tf_op jit(solution)/shard_map/ppermute | solution.py:20
  40.0 0.2 collective-permute-start.9
  40.1 5.3 %collective-permute-done.5.refs_6_ = f32[192,128]{1,0:T(8,128)S(1)} collective-permute-done((f32[192,128]{1,0:T(8,128)S(1)}, f32[192,128]{1,0:T(8,128)S(1)}, u32[]{:S(2)}, u32[]{:S(2)}) %collective-permute-start.5) | collective-permute-done | bytes 98336 | tf_op jit(solution)/shard_map/ppermute | solution.py:20
  45.4 0.0 collective-permute-done.2.refs_2_
  45.4 1.5 %build.1 = (f32[256,256]{1,0:T(8,128)S(1)}, f32[256,256]{1,0:T(8,128)S(1)}, f32[256,256]{1,0:T(8,128)S(1)}, f32[256,256]{1,0:T(8,128)S(1)}, f32[8,128]{1,0:T(8,128)S(1)}) custom-call(f32[448,256]{1,0:T(8,128)S(1)} %copy-done.3, f32[448,256]{1,0:T(8,128)S(1)} %collective-permute-done.refs_1_, f32[448,256]{1,0:T(8,128)S(1)} %collective-permute-done.2.refs_2_, ...), custom_call_target="tpu_custom_call" | custom-call | flops 700000000 | bytes 2100000 | tf_op jit(solution)/shard_map/build/pallas_call | solution.py:483
  46.9 0.7 side.5
  47.6 2.1 %collective-permute-start.8 = (f32[256,256]{1,0:T(8,128)S(1)}, f32[256,256]{1,0:T(8,128)S(1)}, u32[]{:S(2)}, u32[]{:S(2)}) collective-permute-start(f32[256,256]{1,0:T(8,128)S(1)} %get-tuple-element.103.refs_2_), channel_id=1, source_target_pairs={{0,16},{4,20},{8,24},{12,28},{16,0},{20,4},{24,8},{28,12},{1,17},{... | collective-permute-start | bytes 786440 | tf_op jit(solution)/shard_map/ppermute | solution.py:20
  49.7 5.1 %head.2 = (f32[128,128]{1,0:T(8,128)S(1)}, f32[128,128]{1,0:T(8,128)S(1)}, f32[128,128]{1,0:T(8,128)S(1)}, f32[8,128]{1,0:T(8,128)S(1)}) custom-call(f32[256,256]{1,0:T(8,128)S(1)} %get-tuple-element.89.refs_0_, f32[8,128]{1,0:T(8,128)S(1)} %get-tuple-element.91.refs_1_), custom_call_target="tpu_custom_call" | custom-call | flops 5000000 | bytes 15000 | tf_op jit(solution)/shard_map/head/pallas_call | solution.py:483
  54.8 0.0 collective-permute-done.7.refs_1_
  54.9 0.0 collective-permute-done.6.refs_3_
  54.9 1.3 %middle.6 = (f32[256,256]{1,0:T(8,128)S(1)}, f32[256,256]{1,0:T(8,128)S(1)}, f32[8,128]{1,0:T(8,128)S(1)}) custom-call(f32[1024,1024]{1,0:T(8,128)S(1)} %bitcast.11, f32[512,1024]{1,0:T(8,128)S(1)} %bitcast.19, f32[256,256]{1,0:T(8,128)S(1)} %get-tuple-element.97.refs_2_, f32[256,256]{1,0:T(8,128)S(1)} %collective-permute-done.6.refs_3_, ...), custom_call_target="tpu_custom_call" | custom-call | flops 5000000 | bytes 15000 | tf_op jit(solution)/shard_map/middle/pallas_call | solution.py:483
  56.2 2.9 %collective-permute-start.10 = (f32[256,256]{1,0:T(8,128)S(1)}, f32[256,256]{1,0:T(8,128)S(1)}, u32[]{:S(2)}, u32[]{:S(2)}) collective-permute-start(f32[256,256]{1,0:T(8,128)S(1)} %get-tuple-element.114.refs_0_), channel_id=1, source_target_pairs={{0,2},{1,3},{2,0},{3,1},{4,6},{5,7},{6,4},{7,5},{8,10},{9,11},{10,... | collective-permute-start | bytes 786440 | tf_op jit(solution)/shard_map/ppermute | solution.py:20
  59.1 5.8 %turn.1 = (f32[256,256]{1,0:T(8,128)S(1)}, f32[256,256]{1,0:T(8,128)S(1)}, f32[256,256]{1,0:T(8,128)S(1)}, f32[8,128]{1,0:T(8,128)S(1)}) custom-call(f32[128,128]{1,0:T(8,128)S(1)} %get-tuple-element.92.refs_0_, f32[128,128]{1,0:T(8,128)S(1)} %get-tuple-element.93.refs_1_, f32[128,128]{1,0:T(8,128)S(1)} %get-tuple-element.94.refs_2_, ...), custom_call_target="tpu_custom_call" | custom-call | flops 5000000 | bytes 15000 | tf_op jit(solution)/shard_map/turn/pallas_call | solution.py:483
  64.9 0.7 collective-permute-done.9.refs_1_
  65.6 0.0 collective-permute-done.8.refs_3_
  65.6 1.3 %middle.7 = (f32[256,256]{1,0:T(8,128)S(1)}, f32[256,256]{1,0:T(8,128)S(1)}, f32[8,128]{1,0:T(8,128)S(1)}) custom-call(f32[1024,1024]{1,0:T(8,128)S(1)} %bitcast.12, f32[512,1024]{1,0:T(8,128)S(1)} %bitcast.20, f32[256,256]{1,0:T(8,128)S(1)} %get-tuple-element.103.refs_2_, f32[256,256]{1,0:T(8,128)S(1)} %collective-permute-done.8.refs_3_, ...), custom_call_target="tpu_custom_call" | custom-call | flops 5000000 | bytes 15000 | tf_op jit(solution)/shard_map/middle/pallas_call | solution.py:483
  66.9 0.1 collective-permute-start.11
  67.0 1.1 %collective-permute-start.13 = (f32[256,256]{1,0:T(8,128)S(1)}, f32[256,256]{1,0:T(8,128)S(1)}, u32[]{:S(2)}, u32[]{:S(2)}) collective-permute-start(f32[256,256]{1,0:T(8,128)S(1)} %get-tuple-element.126.refs_5_), channel_id=1, source_target_pairs={{0,16},{4,20},{8,24},{12,28},{16,0},{20,4},{24,8},{28,12},{1,17},{... | collective-permute-start | bytes 786440 | tf_op jit(solution)/shard_map/ppermute | solution.py:20
  68.1 1.0 %collective-permute-start.14 = (f32[256,256]{1,0:T(8,128)S(1)}, f32[256,256]{1,0:T(8,128)S(1)}, u32[]{:S(2)}, u32[]{:S(2)}) collective-permute-start(f32[256,256]{1,0:T(8,128)S(1)} %get-tuple-element.127.refs_6_), channel_id=1, source_target_pairs={{0,16},{4,20},{8,24},{12,28},{16,0},{20,4},{24,8},{28,12},{1,17},{... | collective-permute-start | bytes 786440 | tf_op jit(solution)/shard_map/ppermute | solution.py:20
  69.1 5.1 %head.3 = (f32[128,128]{1,0:T(8,128)S(1)}, f32[128,128]{1,0:T(8,128)S(1)}, f32[128,128]{1,0:T(8,128)S(1)}, f32[8,128]{1,0:T(8,128)S(1)}) custom-call(f32[256,256]{1,0:T(8,128)S(1)} %get-tuple-element.102.refs_0_, f32[8,128]{1,0:T(8,128)S(1)} %get-tuple-element.107.refs_1_), custom_call_target="tpu_custom_call" | custom-call | flops 5000000 | bytes 15000 | tf_op jit(solution)/shard_map/head/pallas_call | solution.py:483
  74.3 2.6 %collective-permute-done.10.refs_1_ = f32[256,256]{1,0:T(8,128)S(1)} collective-permute-done((f32[256,256]{1,0:T(8,128)S(1)}, f32[256,256]{1,0:T(8,128)S(1)}, u32[]{:S(2)}, u32[]{:S(2)}) %collective-permute-start.10) | collective-permute-done | bytes 262176 | tf_op jit(solution)/shard_map/ppermute | solution.py:20
  76.9 1.1 %collective-permute-start.15 = (f32[256,256]{1,0:T(8,128)S(1)}, f32[256,256]{1,0:T(8,128)S(1)}, u32[]{:S(2)}, u32[]{:S(2)}) collective-permute-start(f32[256,256]{1,0:T(8,128)S(1)} %get-tuple-element.128.refs_7_), channel_id=1, source_target_pairs={{0,16},{4,20},{8,24},{12,28},{16,0},{20,4},{24,8},{28,12},{1,17},{... | collective-permute-start | bytes 786440 | tf_op jit(solution)/shard_map/ppermute | solution.py:20
  78.0 6.6 %tail.1 = (bf16[512,512]{1,0:T(8,128)(2,1)S(1)}, bf16[512,512]{1,0:T(8,128)(2,1)S(1)}, f32[8,128]{1,0:T(8,128)S(1)}) custom-call(f32[128,128]{1,0:T(8,128)S(1)} %get-tuple-element.108.refs_0_, f32[128,128]{1,0:T(8,128)S(1)} %get-tuple-element.109.refs_1_, f32[128,128]{1,0:T(8,128)S(1)} %get-tuple-element.110.refs_2_, ...), custom_call_target="tpu_custom_call" | custom-call | flops 5000000 | bytes 15000 | tf_op jit(solution)/shard_map/tail/pallas_call | solution.py:483
  84.7 0.0 collective-permute-done.11.refs_1_
  84.7 1.0 %collective-permute-start.12 = (f32[256,256]{1,0:T(8,128)S(1)}, f32[256,256]{1,0:T(8,128)S(1)}, u32[]{:S(2)}, u32[]{:S(2)}) collective-permute-start(f32[256,256]{1,0:T(8,128)S(1)} %get-tuple-element.124.refs_5_), channel_id=1, source_target_pairs={{0,16},{4,20},{8,24},{12,28},{16,0},{20,4},{24,8},{28,12},{1,17},{... | collective-permute-start | bytes 786440 | tf_op jit(solution)/shard_map/ppermute | solution.py:20
  85.7 0.0 collective-permute-done.13.refs_0_
  85.8 0.0 collective-permute-done.14.refs_9_
  85.8 0.0 collective-permute-done.15.refs_10_
  85.8 5.3 %last.2 = (f32[1024,1024]{1,0:T(8,128)}, f32[1024,1024]{1,0:T(8,128)}, f32[8,128]{1,0:T(8,128)S(1)}) custom-call(bf16[512,512]{1,0:T(8,128)(2,1)S(1)} %get-tuple-element.117.refs_0_, bf16[512,512]{1,0:T(8,128)(2,1)S(1)} %get-tuple-element.118.refs_1_, ...), custom_call_target="tpu_custom_call", output_to_operand_aliasing={{1}: (14, {}), {0}: (15, {})} | custom-call | flops 5000000 | bytes 15000 | tf_op jit(solution)/shard_map/last/pallas_call | solution.py:483
  91.1 0.0 collective-permute-done.12.refs_6_
  91.1 3.0 %last.3 = (f32[1024,1024]{1,0:T(8,128)}, f32[1024,1024]{1,0:T(8,128)}, f32[8,128]{1,0:T(8,128)}) custom-call(bf16[512,512]{1,0:T(8,128)(2,1)S(1)} %get-tuple-element.117.refs_0_, bf16[512,512]{1,0:T(8,128)(2,1)S(1)} %get-tuple-element.118.refs_1_, bf16[1024,512]{1,0:T(8,128)(2,1)S(1)} %get-tuple-element.119.refs_2_, ...), custom_call_target="tpu_custom_call", output_to_operand_aliasing={{1}: (8, {}), {0}: (9, {})} | custom-call | flops 5000000 | bytes 15000 | tf_op jit(solution)/shard_map/last/pallas_call | solution.py:483
  (7 shorter events, 0.2 us)
Async XLA Ops:
  0.6 7.8 %copy-start = (f32[1,1,1024,1024]{3,2,1,0:T(8,128)S(1)}, f32[1,1,1024,1024]{3,2,1,0:T(8,128)}, u32[]{:S(2)}) copy-start(f32[1,1,1024,1024]{3,2,1,0:T(8,128)} %param.2) | copy-start | bytes 12582916
  2.8 26.7 %collective-permute-start = (f32[448,256]{1,0:T(8,128)}, f32[448,256]{1,0:T(8,128)S(1)}, u32[]{:S(2)}, u32[]{:S(2)}) collective-permute-start(f32[448,256]{1,0:T(8,128)} %get-tuple-element.72.refs_2_.refs_0_), channel_id=1, source_target_pairs={{0,2},{1,3},{2,0},{3,1},{4,6},{5,7},{6,4},{7,5},{8,10},{9,11},{10,... | collective-permute-start | bytes 1376264 | tf_op jit(solution)/shard_map/ppermute | solution.py:20
  6.9 6.7 %collective-permute-start.1 = (f32[192,256]{1,0:T(8,128)}, f32[192,256]{1,0:T(8,128)S(1)}, u32[]{:S(2)}, u32[]{:S(2)}) collective-permute-start(f32[192,256]{1,0:T(8,128)} %get-tuple-element.73.refs_0_), channel_id=1, source_target_pairs={{0,16},{4,20},{8,24},{12,28},{16,0},{20,4},{24,8},{28,12},{1,17},{... | collective-permute-start | bytes 589832 | tf_op jit(solution)/shard_map/ppermute | solution.py:20
  8.4 1.6 %copy-start.1 = (f32[1,1,512,1024]{3,2,1,0:T(8,128)S(1)}, f32[1,1,512,1024]{3,2,1,0:T(8,128)}, u32[]{:S(2)}) copy-start(f32[1,1,512,1024]{3,2,1,0:T(8,128)} %param.3) | copy-start | bytes 6291460
  10.0 0.7 copy-start.5
  10.7 2.9 %copy-start.3 = (f32[448,256]{1,0:T(8,128)S(1)}, f32[448,256]{1,0:T(8,128)}, u32[]{:S(2)}) copy-start(f32[448,256]{1,0:T(8,128)} %get-tuple-element.72.refs_2_.refs_0_) | copy-start | bytes 1376260
  10.7 2.9 %copy-start.4 = (f32[192,256]{1,0:T(8,128)S(1)}, f32[192,256]{1,0:T(8,128)}, u32[]{:S(2)}) copy-start(f32[192,256]{1,0:T(8,128)} %get-tuple-element.73.refs_0_) | copy-start | bytes 589828
  10.7 13.9 %copy-start.2 = (f32[1,1,512,1024]{3,2,1,0:T(8,128)S(1)}, f32[1,1,512,1024]{3,2,1,0:T(8,128)}, u32[]{:S(2)}) copy-start(f32[1,1,512,1024]{3,2,1,0:T(8,128)} %param.3) | copy-start | bytes 6291460
  11.5 20.3 %collective-permute-start.3 = (f32[256,768]{1,0:T(8,128)S(1)}, f32[256,768]{1,0:T(8,128)S(1)}, u32[]{:S(2)}, u32[]{:S(2)}) collective-permute-start(f32[256,768]{1,0:T(8,128)S(1)} %get-tuple-element.79.refs_2_), channel_id=1, source_target_pairs={{0,16},{4,20},{8,24},{12,28},{16,0},{20,4},{24,8},{28,12},{1,17},{... | collective-permute-start | bytes 2359304 | tf_op jit(solution)/shard_map/ppermute | solution.py:20
  24.2 8.9 %collective-permute-start.4 = (f32[192,128]{1,0:T(8,128)S(1)}, f32[192,128]{1,0:T(8,128)S(1)}, u32[]{:S(2)}, u32[]{:S(2)}) collective-permute-start(f32[192,128]{1,0:T(8,128)S(1)} %get-tuple-element.81), channel_id=1, source_target_pairs={{0,2},{1,3},{2,0},{3,1},{4,6},{5,7},{6,4},{7,5},{8,10},{9,11},{10,... | collective-permute-start | bytes 294920 | tf_op jit(solution)/shard_map/ppermute | solution.py:20
  29.5 15.9 %collective-permute-start.2 = (f32[448,256]{1,0:T(8,128)S(1)}, f32[448,256]{1,0:T(8,128)S(1)}, u32[]{:S(2)}, u32[]{:S(2)}) collective-permute-start(f32[448,256]{1,0:T(8,128)S(1)} %get-tuple-element.78), channel_id=1, source_target_pairs={{0,16},{4,20},{8,24},{12,28},{16,0},{20,4},{24,8},{28,12},{1,17},{... | collective-permute-start | bytes 1376264 | tf_op jit(solution)/shard_map/ppermute | solution.py:20
  33.2 12.2 %collective-permute-start.5 = (f32[192,128]{1,0:T(8,128)S(1)}, f32[192,128]{1,0:T(8,128)S(1)}, u32[]{:S(2)}, u32[]{:S(2)}) collective-permute-start(f32[192,128]{1,0:T(8,128)S(1)} %get-tuple-element.85.refs_5_), channel_id=1, source_target_pairs={{0,16},{4,20},{8,24},{12,28},{16,0},{20,4},{24,8},{28,12},{1,17},{... | collective-permute-start | bytes 294920 | tf_op jit(solution)/shard_map/ppermute | solution.py:20
  33.3 21.6 %collective-permute-start.7 = (f32[256,256]{1,0:T(8,128)S(1)}, f32[256,256]{1,0:T(8,128)S(1)}, u32[]{:S(2)}, u32[]{:S(2)}) collective-permute-start(f32[256,256]{1,0:T(8,128)S(1)} %get-tuple-element.98.refs_0_), channel_id=1, source_target_pairs={{0,2},{1,3},{2,0},{3,1},{4,6},{5,7},{6,4},{7,5},{8,10},{9,11},{10,... | collective-permute-start | bytes 786440 | tf_op jit(solution)/shard_map/ppermute | solution.py:20
  37.9 16.9 %collective-permute-start.6 = (f32[256,256]{1,0:T(8,128)S(1)}, f32[256,256]{1,0:T(8,128)S(1)}, u32[]{:S(2)}, u32[]{:S(2)}) collective-permute-start(f32[256,256]{1,0:T(8,128)S(1)} %get-tuple-element.97.refs_2_), channel_id=1, source_target_pairs={{0,16},{4,20},{8,24},{12,28},{16,0},{20,4},{24,8},{28,12},{1,17},{... | collective-permute-start | bytes 786440 | tf_op jit(solution)/shard_map/ppermute | solution.py:20
  40.0 25.7 %collective-permute-start.9 = (f32[256,256]{1,0:T(8,128)S(1)}, f32[256,256]{1,0:T(8,128)S(1)}, u32[]{:S(2)}, u32[]{:S(2)}) collective-permute-start(f32[256,256]{1,0:T(8,128)S(1)} %get-tuple-element.104.refs_0_), channel_id=1, source_target_pairs={{0,2},{1,3},{2,0},{3,1},{4,6},{5,7},{6,4},{7,5},{8,10},{9,11},{10,... | collective-permute-start | bytes 786440 | tf_op jit(solution)/shard_map/ppermute | solution.py:20
  47.6 18.0 %collective-permute-start.8 = (f32[256,256]{1,0:T(8,128)S(1)}, f32[256,256]{1,0:T(8,128)S(1)}, u32[]{:S(2)}, u32[]{:S(2)}) collective-permute-start(f32[256,256]{1,0:T(8,128)S(1)} %get-tuple-element.103.refs_2_), channel_id=1, source_target_pairs={{0,16},{4,20},{8,24},{12,28},{16,0},{20,4},{24,8},{28,12},{1,17},{... | collective-permute-start | bytes 786440 | tf_op jit(solution)/shard_map/ppermute | solution.py:20
  56.2 20.6 %collective-permute-start.10 = (f32[256,256]{1,0:T(8,128)S(1)}, f32[256,256]{1,0:T(8,128)S(1)}, u32[]{:S(2)}, u32[]{:S(2)}) collective-permute-start(f32[256,256]{1,0:T(8,128)S(1)} %get-tuple-element.114.refs_0_), channel_id=1, source_target_pairs={{0,2},{1,3},{2,0},{3,1},{4,6},{5,7},{6,4},{7,5},{8,10},{9,11},{10,... | collective-permute-start | bytes 786440 | tf_op jit(solution)/shard_map/ppermute | solution.py:20
  66.9 17.7 %collective-permute-start.11 = (f32[256,256]{1,0:T(8,128)S(1)}, f32[256,256]{1,0:T(8,128)S(1)}, u32[]{:S(2)}, u32[]{:S(2)}) collective-permute-start(f32[256,256]{1,0:T(8,128)S(1)} %get-tuple-element.122.refs_0_), channel_id=1, source_target_pairs={{0,2},{1,3},{2,0},{3,1},{4,6},{5,7},{6,4},{7,5},{8,10},{9,11},{10,... | collective-permute-start | bytes 786440 | tf_op jit(solution)/shard_map/ppermute | solution.py:20
  67.0 18.7 %collective-permute-start.13 = (f32[256,256]{1,0:T(8,128)S(1)}, f32[256,256]{1,0:T(8,128)S(1)}, u32[]{:S(2)}, u32[]{:S(2)}) collective-permute-start(f32[256,256]{1,0:T(8,128)S(1)} %get-tuple-element.126.refs_5_), channel_id=1, source_target_pairs={{0,16},{4,20},{8,24},{12,28},{16,0},{20,4},{24,8},{28,12},{1,17},{... | collective-permute-start | bytes 786440 | tf_op jit(solution)/shard_map/ppermute | solution.py:20
  68.1 17.6 %collective-permute-start.14 = (f32[256,256]{1,0:T(8,128)S(1)}, f32[256,256]{1,0:T(8,128)S(1)}, u32[]{:S(2)}, u32[]{:S(2)}) collective-permute-start(f32[256,256]{1,0:T(8,128)S(1)} %get-tuple-element.127.refs_6_), channel_id=1, source_target_pairs={{0,16},{4,20},{8,24},{12,28},{16,0},{20,4},{24,8},{28,12},{1,17},{... | collective-permute-start | bytes 786440 | tf_op jit(solution)/shard_map/ppermute | solution.py:20
  76.9 8.9 %collective-permute-start.15 = (f32[256,256]{1,0:T(8,128)S(1)}, f32[256,256]{1,0:T(8,128)S(1)}, u32[]{:S(2)}, u32[]{:S(2)}) collective-permute-start(f32[256,256]{1,0:T(8,128)S(1)} %get-tuple-element.128.refs_7_), channel_id=1, source_target_pairs={{0,16},{4,20},{8,24},{12,28},{16,0},{20,4},{24,8},{28,12},{1,17},{... | collective-permute-start | bytes 786440 | tf_op jit(solution)/shard_map/ppermute | solution.py:20
  84.7 6.4 %collective-permute-start.12 = (f32[256,256]{1,0:T(8,128)S(1)}, f32[256,256]{1,0:T(8,128)S(1)}, u32[]{:S(2)}, u32[]{:S(2)}) collective-permute-start(f32[256,256]{1,0:T(8,128)S(1)} %get-tuple-element.124.refs_5_), channel_id=1, source_target_pairs={{0,16},{4,20},{8,24},{12,28},{16,0},{20,4},{24,8},{28,12},{1,17},{... | collective-permute-start | bytes 786440 | tf_op jit(solution)/shard_map/ppermute | solution.py:20

commit v3 on v2

--- a/solution.py
+++ b/solution.py
@@ -162,6 +162,27 @@
     )
 
 
+def fold(square):
+    h = square.shape[0] // 2
+    low = square[h:, :h]
+    top = jnp.concatenate([square[:h, :h], square[h:, h:]], 1)
+    return jnp.concatenate([top, jnp.concatenate([low[: h // 2], low[h // 2 :]], 1)], 0)
+
+
+def fold_twice(square):
+    h = square.shape[0] // 2
+    once = fold(square)
+    top = jnp.concatenate([fold(once[:h, :h]), fold(once[:h, h:])], 1)
+    return jnp.concatenate([top, once[h:]], 0)
+
+
+def unfold_twice(packed):
+    h = packed.shape[1] // 2
+    tall = 3 * h // 4
+    top = jnp.concatenate([unpack(packed[:tall, :h]), unpack(packed[:tall, h:])], 1)
+    return unpack(jnp.concatenate([top, packed[tall:]], 0))
+
+
 def quarters(leaf, n, a, b):
     h = n // 2
 
@@ -189,6 +210,14 @@
         (block(h, h // 2, 0), out.at[pl.ds(base + h, h // 2), pl.ds(0, h)]),
         (block(h + h // 2, h // 2, 0), out.at[pl.ds(base + h, h // 2), pl.ds(h, h)]),
     ]
+
+
+def blocks_kernel(leaf, joined, middle, held, sems):
+    n = joined.shape[1]
+    i, _, y, _ = edges()
+    block = lambda a, b: leaf.at[pl.ds(pl.multiple_of(a * n, n), n), pl.ds(pl.multiple_of(b * n, n), n)]
+    fetch([(block(y, y), held), (block(y, i), middle.at[pl.ds(0, n)])] + symmetric(leaf, i, joined, 0), sems)
+    middle[n:] = fold_twice(held[...])
 
 
 def passing_kernel(middle, middle_z, out):
@@ -230,91 +259,36 @@
     out[:, :width] = triple(split(rows[...]), split(held[...]))
 
 
-def blocks_kernel(leaf, joined, middle, sems):
-    n = joined.shape[1]
-    i, _, y, _ = edges()
-    whole = leaf.at[pl.ds(pl.multiple_of(y * n, n), n), pl.ds(pl.multiple_of(i * n, n), n)]
-    fetch([(whole, middle.at[pl.ds(0, n)])] + symmetric(leaf, y, middle, n) + symmetric(leaf, i, joined, 0), sems)
-
-
-def passing_kernel(middle, middle_z, out):
-    n = out.shape[1]
-    out[:n] = middle_z[:n]
-    out[n:] = middle[n:] + middle_z[n:]
-
-
-def relay_kernel(given, out):
-    out[...] = given[...]
-
-
-def sum_kernel(own, other, out):
-    out[...] = own[...] + other[...]
-
-
-def append_kernel(before, own, other, out):
-    width = before.shape[1]
-    out[:, :width] = before[...]
-    out[:, width:] = own[...] + other[...]
-
-
-def outer_rows(leaf, edge, rows, sems):
-    n = rows.shape[0]
-    _, x, _, d = edges()
-    own = pl.ds(pl.multiple_of(edge * n, n), n)
-    return [
-        pltpu.make_async_copy(leaf.at[own, pl.ds(pl.multiple_of(e * n, n), n)], rows.at[:, pl.ds(p * n, n)], sems.at[p])
-        for p, e in enumerate((x, d))
-    ]
-
-
-def side_kernel(base, leaf, data, out, rows, held, sems):
-    n, width = rows.shape[0], held.shape[1]
-    i, _, y, _ = edges()
-    copies = outer_rows(leaf, i, rows, sems)
-    copies.append(pltpu.make_async_copy(data.at[:, pl.ds(base, width)], held, sems.at[2]))
-    for copy in copies:
-        copy.start()
-    if out.shape[1] > width:
-        whole = leaf.at[pl.ds(pl.multiple_of(y * n, n), n), pl.ds(pl.multiple_of(i * n, n), n)]
-        fetch([(whole, out.at[:, pl.ds(width, n)])], sems.at[pl.ds(3, 1)])
-    for copy in copies:
-        copy.wait()
-    out[:, :width] = triple(split(rows[...]), split(held[...]))
-
-
-def joined_kernel(leaf, out, sems):
-    fetch(symmetric(leaf, edges()[0], out, 0), sems)
-
-
-def crossing_kernel(leaf, out, sems):
-    n = out.shape[1]
-    i, _, y, _ = edges()
-    whole = leaf.at[pl.ds(pl.multiple_of(y * n, n), n), pl.ds(pl.multiple_of(i * n, n), n)]
-    fetch([(whole, out.at[pl.ds(0, n)])] + symmetric(leaf, y, out, n), sems)
-
-
-def known_kernel(leaf, data, flux, high, low, potential, _, data_high, data_low, sems):
-    step = pl.program_id(0)
+def known_kernel(leaf, data, flux, high, low, data_high, data_low):
     n = leaf.shape[0]
     i, x, y, d = edges()
+
+    @pl.when(pl.program_id(0) == 0)
+    def _():
+        data_high[...], data_low[...] = split(data[...])
+
+    cols = lambda e: leaf[:, pl.ds(pl.multiple_of(e * n, n), n)]
+    high[...], low[...] = split(jnp.concatenate([cols(i), cols(y)], 1))
+    outer = split(jnp.concatenate([cols(x), cols(d)], 1))
+    flux[...] = triple(outer, (data_high[...], data_low[...]))
+
+
+def known_and_data_kernel(leaf, data, flux, high, low, potential, _, data_high, data_low, sems):
+    n = leaf.shape[0]
+    _, x, _, d = edges()
     copies = [
         pltpu.make_async_copy(data.at[pl.ds(p * n, n), :], potential.at[pl.ds(pl.multiple_of(e * n, n), n), :], sems.at[p])
         for p, e in enumerate((x, d))
     ]
 
-    @pl.when(step == 0)
+    @pl.when(pl.program_id(0) == 0)
     def _():
         for copy in copies:
             copy.start()
-        data_high[...], data_low[...] = split(data[...])
-
-    cols = lambda e: leaf[:, pl.ds(pl.multiple_of(e * n, n), n)]
-    unknown = split(jnp.concatenate([cols(i), cols(y)], 1))
-    high[...], low[...] = unknown
-    outer = split(jnp.concatenate([cols(x), cols(d)], 1))
-    flux[...] = triple(outer, (data_high[...], data_low[...]))
-
-    @pl.when(step == pl.num_programs(0) - 1)
+
+    known_kernel(leaf, data, flux, high, low, data_high, data_low)
+
+    @pl.when(pl.program_id(0) == pl.num_programs(0) - 1)
     def _():
         for copy in copies:
             copy.wait()
@@ -384,9 +358,9 @@
     across_far[...] = q_far
     p_own = near_nt(other[...], middle_z[:n])
     p_far = near_nt(other[...], passed[:n])
-    own[...] = unpack(middle[n:] + middle_z[n:]) - (near_nn(middle[:n], q_own) + near_nn(middle_z[:n], p_own))
+    own[...] = unfold_twice(middle[n:] + middle_z[n:]) - (near_nn(middle[:n], q_own) + near_nn(middle_z[:n], p_own))
     off[...] = -(near_nn(middle[:n], q_far) + near_nn(middle_z[:n], p_far))
-    far[...] = unpack(passed[n:]) - (near_nn(cross, q_far) + near_nn(passed[:n], p_far))
+    far[...] = unfold_twice(passed[n:]) - (near_nn(cross, q_far) + near_nn(passed[:n], p_far))
 
 
 def open_half(matrix, head, reach, rest):
@@ -414,7 +388,8 @@
     high[...], low[...] = split(jnp.concatenate([inward, -solved[:n]], 0))
 
 
-def last_kernel(count, base, solve_high, solve_low, high, low, known, *rest):
+def last_kernel(count, base, solve_high, solve_low, *rest):
+    halves, rest = (rest[:3], rest[3:6]), rest[6:]
     w_own, w_far, starts = rest[:count], rest[count : 2 * count], rest[2 * count : -7]
     flux, potential, solved, made, sems = rest[-5:]
     n, width = w_own[0].shape[0], solved.shape[1]
@@ -438,7 +413,8 @@
     right = split(values)
     for k in range(4):
         rows = pl.ds(k * n, n)
-        made[rows] = known[rows, base : base + width] + triple((high[rows], low[rows]), right)
+        known, high, low = (ref.at[pl.ds(k % 2 * n, n)] for ref in halves[k // 2])
+        made[rows] = known[:, base : base + width] + triple((high[...], low[...]), right)
         copies.append(pltpu.make_async_copy(made.at[rows], flux.at[rows, cols], sems.at[k]))
         copies[-1].start()
     for copy in copies:
@@ -502,6 +478,7 @@
     n = full // 4
     h = n // 2
     packed = 3 * n // 4
+    tight = 5 * n // 8
     dma = pltpu.SemaphoreType.DMA
     call = Chain()
     unit = count // 8
@@ -511,11 +488,11 @@
     joined, middle = call(
         "blocks",
         blocks_kernel,
-        [array(packed, n), array(n + packed, n)],
+        [array(packed, n), array(n + tight, n)],
         leaf,
         limit=EARLY,
         ins=[HBM],
-        scratch=[dma((9,))],
+        scratch=[pltpu.VMEM((n, n), F32), dma((6,))],
     )
     middle_z = exchange(middle, "gy")
     joined_far = exchange(joined, "gx")
@@ -561,30 +538,28 @@
         "first", first_kernel, [array(n, n)] * 2 + [array(packed, h)], joined, joined_far, middle
     )
     half_z = exchange(half, "gy")
-    known, high, low, potential, flux = call(
-        "known",
-        known_kernel,
-        [
-            array(full, count),
-            array(full, 2 * n, dtype=BF16),
-            array(full, 2 * n, dtype=BF16),
-            array(full, count),
-            array(full, count),
-        ],
-        leaf,
-        data,
-        ins=[pl.BlockSpec((n, full), lambda s: (s, 0)), pl.BlockSpec((2 * n, count), lambda s: (0, 0))],
-        out_specs=[
-            pl.BlockSpec((n, count), lambda s: (s, 0)),
-            pl.BlockSpec((n, 2 * n), lambda s: (s, 0)),
-            pl.BlockSpec((n, 2 * n), lambda s: (s, 0)),
-            ANY,
-            ANY,
-        ],
-        scratch=[pltpu.VMEM((2 * n, count), BF16), pltpu.VMEM((2 * n, count), BF16), dma((2,))],
-        grid=(4,),
+    def known_half(name, kernel, first, outs, out_specs, sems):
+        return call(
+            name,
+            kernel,
+            [array(2 * n, count), array(2 * n, 2 * n, dtype=BF16), array(2 * n, 2 * n, dtype=BF16), *outs],
+            leaf,
+            data,
+            ins=[pl.BlockSpec((n, full), lambda s: (s + first, 0)), pl.BlockSpec((2 * n, count), lambda s: (0, 0))],
+            out_specs=[
+                pl.BlockSpec((n, count), lambda s: (s, 0)),
+                pl.BlockSpec((n, 2 * n), lambda s: (s, 0)),
+                pl.BlockSpec((n, 2 * n), lambda s: (s, 0)),
+                *out_specs,
+            ],
+            scratch=[pltpu.VMEM((2 * n, count), BF16), pltpu.VMEM((2 * n, count), BF16), *sems],
+            grid=(2,),
+        )
+
+    *known_a, potential, flux = known_half(
+        "known_and_data", known_and_data_kernel, 0, [array(full, count)] * 2, [ANY] * 2, [dma((2,))]
     )
-    passing = call("passing", passing_kernel, [array(n + packed, n)], middle, middle_z)
+    passing = call("passing", passing_kernel, [array(n + tight, n)], middle, middle_z)
     passed = exchange(passing, "gx")
     (v0,), start0 = middles([0], 0, own_a, far_a)
     z0 = exchange(v0, "gy")
@@ -593,6 +568,7 @@
     (v1,), start1 = middles([1], 0, own_a, far_a)
     z1 = exchange(v1, "gy")
     own_b, far_b = sides(bases[2], widths[2])
+    known_b = known_half("known", known_kernel, 2, [], [], [])
     across_far, s_own, s_off, s_far = call(
         "build",
         build_kernel,
@@ -624,15 +600,14 @@
 
     def last(base, own, far, starts, held):
         width = sum(part.shape[1] for part in own)
-        fixed = 5 + 2 * len(own) + len(starts)
+        fixed = 8 + 2 * len(own) + len(starts)
         return call(
             "last",
             functools.partial(last_kernel, len(own), base),
             [array(full, count), array(full, count)],
             *inverse2,
-            high,
-            low,
-            known,
+            *known_a,
+            *known_b,
             *own,
             *far,
             *starts,

time: 94.8 us -> 93.7 us (0.988)
  starting transfers between devices: 23.2 us -> 20.2 us
  waiting for transfers between devices: 10.1 us -> 12 us
    ppermute x16, starting transfers between devices: 23.2 us -> 20.2 us  [exchange(): return lax.ppermute(block, axis, [(i, i ^ half) for i in range(2 * half)])]
    ppermute x16, waiting for transfers between devices: 10.1 us -> 12 us  [exchange(): return lax.ppermute(block, axis, [(i, i ^ half) for i in range(2 * half)])]
    pallas_call x24 -> x25, Pallas kernels: 57.7 us -> 58 us  [__call__(): pl.pallas_call(body, out_shape=list(outs) + [array(8, LANES)], in_specs=l...]
  transfers between devices with their start and end apart: 16 -> 16, of which waited for: 4 -> 6; matrix products, arithmetic and copies ran while one was open for 0% -> 0% of each run, Pallas kernels for 56% -> 57%
where the time goes in v3:
time: 93.7 us; the launch traced here: 93.5 us
  Pallas kernels  58 us (62%)
  starting transfers between devices  20.2 us (22%)
  waiting for transfers between devices  12 us (13%)
  local copies, waits for them, and re-layouts  2.29 us (2%)
  between operations  1.07 us (1%)
    pallas_call x25, Pallas kernels, __call__(): pl.pallas_call(body, out_shape=list(outs) + [array(8, LANES)], in_specs=l...  58 us
    ppermute x16, starting transfers between devices, exchange(): return lax.ppermute(block, axis, [(i, i ^ half) for i in range(2 * half)])  20.2 us
    ppermute x16, waiting for transfers between devices, exchange(): return lax.ppermute(block, axis, [(i, i ^ half) for i in range(2 * half)])  12 us
    unnamed x12, local copies, waits for them, and re-layouts  2.29 us
  transfers between devices with their start and end apart: 16, of which 6 were waited for; matrix products, arithmetic and copies ran while one was open for 0% of the time, Pallas kernels for 57%

profile of v3, /device:TPU:0, one launch (start us, length us, event | category | flops | bytes accessed | tf_op | source)
XLA Modules:
  0.0 93.5 jit_solution(822930480612554992)
XLA Ops:
  0.6 0.0 copy-start
  0.6 2.1 %blocks.1 = (f32[192,256]{1,0:T(8,128)}, f32[416,256]{1,0:T(8,128)}, f32[8,128]{1,0:T(8,128)}) custom-call(f32[1024,1024]{1,0:T(8,128)} %bitcast.4), custom_call_target="tpu_custom_call" | custom-call | flops 5000000 | bytes 15000 | tf_op jit(solution)/shard_map/blocks/pallas_call | solution.py:459
  2.7 4.1 %collective-permute-start = (f32[416,256]{1,0:T(8,128)}, f32[416,256]{1,0:T(8,128)S(1)}, u32[]{:S(2)}, u32[]{:S(2)}) collective-permute-start(f32[416,256]{1,0:T(8,128)} %get-tuple-element.76.refs_2_.refs_0_), channel_id=1, source_target_pairs={{0,2},{1,3},{2,0},{3,1},{4,6},{5,7},{6,4},{7,5},{8,10},{9,11},{10,... | collective-permute-start | bytes 1277960 | tf_op jit(solution)/shard_map/ppermute | solution.py:20
  6.8 1.5 %collective-permute-start.1 = (f32[192,256]{1,0:T(8,128)}, f32[192,256]{1,0:T(8,128)S(1)}, u32[]{:S(2)}, u32[]{:S(2)}) collective-permute-start(f32[192,256]{1,0:T(8,128)} %get-tuple-element.77.refs_0_), channel_id=1, source_target_pairs={{0,16},{4,20},{8,24},{12,28},{16,0},{20,4},{24,8},{28,12},{1,17},{... | collective-permute-start | bytes 589832 | tf_op jit(solution)/shard_map/ppermute | solution.py:20
  8.3 0.0 copy-done
  8.3 0.0 copy-start.1
  8.4 1.6 %copy-done.1 = f32[1,1,512,1024]{3,2,1,0:T(8,128)S(1)} copy-done((f32[1,1,512,1024]{3,2,1,0:T(8,128)S(1)}, f32[1,1,512,1024]{3,2,1,0:T(8,128)}, u32[]{:S(2)}) %copy-start.1) | copy-done | bytes 2097176
  9.9 0.0 copy-start.5
  9.9 0.7 copy-done.5
  10.6 0.0 copy-start.3
  10.6 0.0 copy-start.4
  10.6 0.0 copy-start.2
  10.6 0.8 side.3
  11.5 0.6 collective-permute-start.3
  12.0 1.4 %collective-permute-done.1.refs_1_ = f32[192,256]{1,0:T(8,128)S(1)} collective-permute-done((f32[192,256]{1,0:T(8,128)}, f32[192,256]{1,0:T(8,128)S(1)}, u32[]{:S(2)}, u32[]{:S(2)}) %collective-permute-start.1) | collective-permute-done | bytes 196640 | tf_op jit(solution)/shard_map/ppermute | solution.py:20
  13.5 0.0 copy-done.3
  13.5 0.0 copy-done.4
  13.5 10.7 %first.1 = (f32[256,256]{1,0:T(8,128)S(1)}, f32[256,256]{1,0:T(8,128)S(1)}, f32[192,128]{1,0:T(8,128)S(1)}, f32[8,128]{1,0:T(8,128)S(1)}) custom-call(f32[192,256]{1,0:T(8,128)S(1)} %copy-done.4, f32[192,256]{1,0:T(8,128)S(1)} %collective-permute-done.1.refs_1_, f32[416,256]{1,0:T(8,128)S(1)} %copy-done.3, f32[8,128]{1,0:T(8,128)S(1)} %get-tuple-element.79.refs_3_), custom_call_target="tpu_custom_call" | custom-call | flops 5000000 | bytes 15000 | tf_op jit(solution)/shard_map/first/pallas_call | solution.py:459
  24.2 0.3 collective-permute-start.4
  24.5 0.0 copy-done.2
  24.5 2.6 %known_and_data.1 = (f32[512,1024]{1,0:T(8,128)S(1)}, bf16[512,512]{1,0:T(8,128)(2,1)S(1)}, bf16[512,512]{1,0:T(8,128)(2,1)S(1)}, f32[1024,1024]{1,0:T(8,128)}, ...) custom-call(f32[1024,1024]{1,0:T(8,128)S(1)} %bitcast.6, f32[512,1024]{1,0:T(8,128)S(1)} %bitcast.15, ...), custom_call_target="tpu_custom_call" | custom-call | flops 5000000 | bytes 15000 | tf_op jit(solution)/shard_map/known_and_data/pallas_call | solution.py:459
  27.2 0.0 collective-permute-done.refs_1_
  27.2 2.3 %collective-permute-start.2 = (f32[416,256]{1,0:T(8,128)S(1)}, f32[416,256]{1,0:T(8,128)S(1)}, u32[]{:S(2)}, u32[]{:S(2)}) collective-permute-start(f32[416,256]{1,0:T(8,128)S(1)} %get-tuple-element.82), channel_id=1, source_target_pairs={{0,16},{4,20},{8,24},{12,28},{16,0},{20,4},{24,8},{28,12},{1,17},{... | collective-permute-start | bytes 1277960 | tf_op jit(solution)/shard_map/ppermute | solution.py:20
  29.6 2.3 %collective-permute-done.3.refs_3_ = f32[256,768]{1,0:T(8,128)S(1)} collective-permute-done((f32[256,768]{1,0:T(8,128)S(1)}, f32[256,768]{1,0:T(8,128)S(1)}, u32[]{:S(2)}, u32[]{:S(2)}) %collective-permute-start.3) | collective-permute-done | bytes 786464 | tf_op jit(solution)/shard_map/ppermute | solution.py:20
  31.9 1.3 %middle.4 = (f32[256,256]{1,0:T(8,128)S(1)}, f32[256,256]{1,0:T(8,128)S(1)}, f32[8,128]{1,0:T(8,128)S(1)}) custom-call(f32[1024,1024]{1,0:T(8,128)S(1)} %bitcast.7, f32[512,1024]{1,0:T(8,128)S(1)} %bitcast.16, f32[256,768]{1,0:T(8,128)S(1)} %get-tuple-element.83.refs_2_, f32[256,768]{1,0:T(8,128)S(1)} %collective-permute-done.3.refs_3_, ...), custom_call_target="tpu_custom_call" | custom-call | flops 5000000 | bytes 15000 | tf_op jit(solution)/shard_map/middle/pallas_call | solution.py:459
  33.2 0.0 collective-permute-done.4.refs_0_
  33.2 0.9 collective-permute-start.5
  34.1 0.0 collective-permute-start.7
  34.1 1.3 %middle.5 = (f32[256,256]{1,0:T(8,128)S(1)}, f32[256,256]{1,0:T(8,128)S(1)}, f32[8,128]{1,0:T(8,128)S(1)}) custom-call(f32[1024,1024]{1,0:T(8,128)S(1)} %bitcast.8, f32[512,1024]{1,0:T(8,128)S(1)} %bitcast.17, f32[256,768]{1,0:T(8,128)S(1)} %get-tuple-element.83.refs_2_, f32[256,768]{1,0:T(8,128)S(1)} %collective-permute-done.3.refs_3_, ...), custom_call_target="tpu_custom_call" | custom-call | flops 5000000 | bytes 15000 | tf_op jit(solution)/shard_map/middle/pallas_call | solution.py:459
  35.4 0.6 side.4
  35.9 1.7 %collective-permute-start.6 = (f32[256,256]{1,0:T(8,128)S(1)}, f32[256,256]{1,0:T(8,128)S(1)}, u32[]{:S(2)}, u32[]{:S(2)}) collective-permute-start(f32[256,256]{1,0:T(8,128)S(1)} %get-tuple-element.102.refs_2_), channel_id=1, source_target_pairs={{0,16},{4,20},{8,24},{12,28},{16,0},{20,4},{24,8},{28,12},{1,17},{... | collective-permute-start | bytes 786440 | tf_op jit(solution)/shard_map/ppermute | solution.py:20
  37.6 2.5 %collective-permute-start.9 = (f32[256,256]{1,0:T(8,128)S(1)}, f32[256,256]{1,0:T(8,128)S(1)}, u32[]{:S(2)}, u32[]{:S(2)}) collective-permute-start(f32[256,256]{1,0:T(8,128)S(1)} %get-tuple-element.109.refs_0_), channel_id=1, source_target_pairs={{0,2},{1,3},{2,0},{3,1},{4,6},{5,7},{6,4},{7,5},{8,10},{9,11},{10,... | collective-permute-start | bytes 786440 | tf_op jit(solution)/shard_map/ppermute | solution.py:20
  40.1 2.6 %known.1 = (f32[512,1024]{1,0:T(8,128)S(1)}, bf16[512,512]{1,0:T(8,128)(2,1)S(1)}, bf16[512,512]{1,0:T(8,128)(2,1)S(1)}, f32[8,128]{1,0:T(8,128)S(1)}) custom-call(f32[1024,1024]{1,0:T(8,128)S(1)} %bitcast.10, f32[512,1024]{1,0:T(8,128)S(1)} %bitcast.19, f32[8,128]{1,0:T(8,128)S(1)} %get-tuple-element.92.refs_2_), custom_call_target="tpu_custom_call" | custom-call | flops 5000000 | bytes 15000 | tf_op jit(solution)/shard_map/known/pallas_call | solution.py:459
  42.7 0.0 collective-permute-done.2.refs_2_
  42.7 0.4 collective-permute-done.5.refs_6_
  43.1 1.5 %build.1 = (f32[256,256]{1,0:T(8,128)S(1)}, f32[256,256]{1,0:T(8,128)S(1)}, f32[256,256]{1,0:T(8,128)S(1)}, f32[256,256]{1,0:T(8,128)S(1)}, f32[8,128]{1,0:T(8,128)S(1)}) custom-call(f32[416,256]{1,0:T(8,128)S(1)} %copy-done.3, f32[416,256]{1,0:T(8,128)S(1)} %collective-permute-done.refs_1_, f32[416,256]{1,0:T(8,128)S(1)} %collective-permute-done.2.refs_2_, ...), custom_call_target="tpu_custom_call" | custom-call | flops 700000000 | bytes 2100000 | tf_op jit(solution)/shard_map/build/pallas_call | solution.py:459
  44.6 0.7 side.5
  45.3 1.4 %collective-permute-start.8 = (f32[256,256]{1,0:T(8,128)S(1)}, f32[256,256]{1,0:T(8,128)S(1)}, u32[]{:S(2)}, u32[]{:S(2)}) collective-permute-start(f32[256,256]{1,0:T(8,128)S(1)} %get-tuple-element.108.refs_2_), channel_id=1, source_target_pairs={{0,16},{4,20},{8,24},{12,28},{16,0},{20,4},{24,8},{28,12},{1,17},{... | collective-permute-start | bytes 786440 | tf_op jit(solution)/shard_map/ppermute | solution.py:20
  46.7 5.1 %head.2 = (f32[128,128]{1,0:T(8,128)S(1)}, f32[128,128]{1,0:T(8,128)S(1)}, f32[128,128]{1,0:T(8,128)S(1)}, f32[8,128]{1,0:T(8,128)S(1)}) custom-call(f32[256,256]{1,0:T(8,128)S(1)} %get-tuple-element.94.refs_0_, f32[8,128]{1,0:T(8,128)S(1)} %get-tuple-element.96.refs_1_), custom_call_target="tpu_custom_call" | custom-call | flops 5000000 | bytes 15000 | tf_op jit(solution)/shard_map/head/pallas_call | solution.py:459
  51.8 1.7 %collective-permute-done.7.refs_1_ = f32[256,256]{1,0:T(8,128)S(1)} collective-permute-done((f32[256,256]{1,0:T(8,128)S(1)}, f32[256,256]{1,0:T(8,128)S(1)}, u32[]{:S(2)}, u32[]{:S(2)}) %collective-permute-start.7) | collective-permute-done | bytes 262176 | tf_op jit(solution)/shard_map/ppermute | solution.py:20
  53.6 0.0 collective-permute-done.6.refs_3_
  53.6 1.3 %middle.6 = (f32[256,256]{1,0:T(8,128)S(1)}, f32[256,256]{1,0:T(8,128)S(1)}, f32[8,128]{1,0:T(8,128)S(1)}) custom-call(f32[1024,1024]{1,0:T(8,128)S(1)} %bitcast.12, f32[512,1024]{1,0:T(8,128)S(1)} %bitcast.21, f32[256,256]{1,0:T(8,128)S(1)} %get-tuple-element.102.refs_2_, f32[256,256]{1,0:T(8,128)S(1)} %collective-permute-done.6.refs_3_, ...), custom_call_target="tpu_custom_call" | custom-call | flops 5000000 | bytes 15000 | tf_op jit(solution)/shard_map/middle/pallas_call | solution.py:459
  54.9 0.5 collective-permute-start.10
  55.4 5.8 %turn.1 = (f32[256,256]{1,0:T(8,128)S(1)}, f32[256,256]{1,0:T(8,128)S(1)}, f32[256,256]{1,0:T(8,128)S(1)}, f32[8,128]{1,0:T(8,128)S(1)}) custom-call(f32[128,128]{1,0:T(8,128)S(1)} %get-tuple-element.97.refs_0_, f32[128,128]{1,0:T(8,128)S(1)} %get-tuple-element.98.refs_1_, f32[128,128]{1,0:T(8,128)S(1)} %get-tuple-element.99.refs_2_, ...), custom_call_target="tpu_custom_call" | custom-call | flops 5000000 | bytes 15000 | tf_op jit(solution)/shard_map/turn/pallas_call | solution.py:459
  61.2 3.6 %collective-permute-done.9.refs_1_ = f32[256,256]{1,0:T(8,128)S(1)} collective-permute-done((f32[256,256]{1,0:T(8,128)S(1)}, f32[256,256]{1,0:T(8,128)S(1)}, u32[]{:S(2)}, u32[]{:S(2)}) %collective-permute-start.9) | collective-permute-done | bytes 262176 | tf_op jit(solution)/shard_map/ppermute | solution.py:20
  64.8 0.0 collective-permute-done.8.refs_3_
  64.8 1.3 %middle.7 = (f32[256,256]{1,0:T(8,128)S(1)}, f32[256,256]{1,0:T(8,128)S(1)}, f32[8,128]{1,0:T(8,128)S(1)}) custom-call(f32[1024,1024]{1,0:T(8,128)S(1)} %bitcast.13, f32[512,1024]{1,0:T(8,128)S(1)} %bitcast.22, f32[256,256]{1,0:T(8,128)S(1)} %get-tuple-element.108.refs_2_, f32[256,256]{1,0:T(8,128)S(1)} %collective-permute-done.8.refs_3_, ...), custom_call_target="tpu_custom_call" | custom-call | flops 5000000 | bytes 15000 | tf_op jit(solution)/shard_map/middle/pallas_call | solution.py:459
  66.1 0.1 collective-permute-start.11
  66.2 0.4 collective-permute-start.14
  66.6 1.7 %collective-permute-start.13 = (f32[256,256]{1,0:T(8,128)S(1)}, f32[256,256]{1,0:T(8,128)S(1)}, u32[]{:S(2)}, u32[]{:S(2)}) collective-permute-start(f32[256,256]{1,0:T(8,128)S(1)} %get-tuple-element.134.refs_8_), channel_id=1, source_target_pairs={{0,16},{4,20},{8,24},{12,28},{16,0},{20,4},{24,8},{28,12},{1,17},{... | collective-permute-start | bytes 786440 | tf_op jit(solution)/shard_map/ppermute | solution.py:20
  68.3 5.1 %head.3 = (f32[128,128]{1,0:T(8,128)S(1)}, f32[128,128]{1,0:T(8,128)S(1)}, f32[128,128]{1,0:T(8,128)S(1)}, f32[8,128]{1,0:T(8,128)S(1)}) custom-call(f32[256,256]{1,0:T(8,128)S(1)} %get-tuple-element.107.refs_0_, f32[8,128]{1,0:T(8,128)S(1)} %get-tuple-element.112.refs_1_), custom_call_target="tpu_custom_call" | custom-call | flops 5000000 | bytes 15000 | tf_op jit(solution)/shard_map/head/pallas_call | solution.py:459
  73.4 2.6 %collective-permute-done.10.refs_1_ = f32[256,256]{1,0:T(8,128)S(1)} collective-permute-done((f32[256,256]{1,0:T(8,128)S(1)}, f32[256,256]{1,0:T(8,128)S(1)}, u32[]{:S(2)}, u32[]{:S(2)}) %collective-permute-start.10) | collective-permute-done | bytes 262176 | tf_op jit(solution)/shard_map/ppermute | solution.py:20
  76.1 0.4 collective-permute-start.15
  76.5 6.6 %tail.1 = (bf16[512,512]{1,0:T(8,128)(2,1)S(1)}, bf16[512,512]{1,0:T(8,128)(2,1)S(1)}, f32[8,128]{1,0:T(8,128)S(1)}) custom-call(f32[128,128]{1,0:T(8,128)S(1)} %get-tuple-element.113.refs_0_, f32[128,128]{1,0:T(8,128)S(1)} %get-tuple-element.114.refs_1_, f32[128,128]{1,0:T(8,128)S(1)} %get-tuple-element.115.refs_2_, ...), custom_call_target="tpu_custom_call" | custom-call | flops 5000000 | bytes 15000 | tf_op jit(solution)/shard_map/tail/pallas_call | solution.py:459
  83.1 0.0 collective-permute-done.11.refs_1_
  83.2 1.7 %collective-permute-start.12 = (f32[256,256]{1,0:T(8,128)S(1)}, f32[256,256]{1,0:T(8,128)S(1)}, u32[]{:S(2)}, u32[]{:S(2)}) collective-permute-start(f32[256,256]{1,0:T(8,128)S(1)} %get-tuple-element.132.refs_8_), channel_id=1, source_target_pairs={{0,16},{4,20},{8,24},{12,28},{16,0},{20,4},{24,8},{28,12},{1,17},{... | collective-permute-start | bytes 786440 | tf_op jit(solution)/shard_map/ppermute | solution.py:20
  84.9 0.0 collective-permute-done.13.refs_0_
  85.0 0.0 collective-permute-done.14.refs_12_
  85.0 0.0 collective-permute-done.15.refs_13_
  85.0 5.3 %last.2 = (f32[1024,1024]{1,0:T(8,128)}, f32[1024,1024]{1,0:T(8,128)}, f32[8,128]{1,0:T(8,128)S(1)}) custom-call(bf16[512,512]{1,0:T(8,128)(2,1)S(1)} %get-tuple-element.122.refs_0_, bf16[512,512]{1,0:T(8,128)(2,1)S(1)} %get-tuple-element.123.refs_1_, f32[512,1024]{1,0:T(8,128)S(1)} %get-tuple-element.124.refs_2_, ...), custom_call_target="tpu_custom_call", output_to_operand_aliasing={{1}: (17, {}), {0}: (18, {})} | custom-call | flops 5000000 | bytes 15000 | tf_op jit(solution)/shard_map/last/pallas_call | solution.py:459
  90.3 0.0 collective-permute-done.12.refs_9_
  90.3 3.0 %last.3 = (f32[1024,1024]{1,0:T(8,128)}, f32[1024,1024]{1,0:T(8,128)}, f32[8,128]{1,0:T(8,128)}) custom-call(bf16[512,512]{1,0:T(8,128)(2,1)S(1)} %get-tuple-element.122.refs_0_, bf16[512,512]{1,0:T(8,128)(2,1)S(1)} %get-tuple-element.123.refs_1_, f32[512,1024]{1,0:T(8,128)S(1)} %get-tuple-element.124.refs_2_, ...), custom_call_target="tpu_custom_call", output_to_operand_aliasing={{1}: (11, {}), {0}: (12, {})} | custom-call | flops 5000000 | bytes 15000 | tf_op jit(solution)/shard_map/last/pallas_call | solution.py:459
  (7 shorter events, 0.2 us)
Async XLA Ops:
  0.6 7.7 %copy-start = (f32[1,1,1024,1024]{3,2,1,0:T(8,128)S(1)}, f32[1,1,1024,1024]{3,2,1,0:T(8,128)}, u32[]{:S(2)}) copy-start(f32[1,1,1024,1024]{3,2,1,0:T(8,128)} %param.2) | copy-start | bytes 12582916
  2.7 24.4 %collective-permute-start = (f32[416,256]{1,0:T(8,128)}, f32[416,256]{1,0:T(8,128)S(1)}, u32[]{:S(2)}, u32[]{:S(2)}) collective-permute-start(f32[416,256]{1,0:T(8,128)} %get-tuple-element.76.refs_2_.refs_0_), channel_id=1, source_target_pairs={{0,2},{1,3},{2,0},{3,1},{4,6},{5,7},{6,4},{7,5},{8,10},{9,11},{10,... | collective-permute-start | bytes 1277960 | tf_op jit(solution)/shard_map/ppermute | solution.py:20
  6.8 6.7 %collective-permute-start.1 = (f32[192,256]{1,0:T(8,128)}, f32[192,256]{1,0:T(8,128)S(1)}, u32[]{:S(2)}, u32[]{:S(2)}) collective-permute-start(f32[192,256]{1,0:T(8,128)} %get-tuple-element.77.refs_0_), channel_id=1, source_target_pairs={{0,16},{4,20},{8,24},{12,28},{16,0},{20,4},{24,8},{28,12},{1,17},{... | collective-permute-start | bytes 589832 | tf_op jit(solution)/shard_map/ppermute | solution.py:20
  8.3 1.6 %copy-start.1 = (f32[1,1,512,1024]{3,2,1,0:T(8,128)S(1)}, f32[1,1,512,1024]{3,2,1,0:T(8,128)}, u32[]{:S(2)}) copy-start(f32[1,1,512,1024]{3,2,1,0:T(8,128)} %param.3) | copy-start | bytes 6291460
  9.9 0.7 copy-start.5
  10.6 2.9 %copy-start.3 = (f32[416,256]{1,0:T(8,128)S(1)}, f32[416,256]{1,0:T(8,128)}, u32[]{:S(2)}) copy-start(f32[416,256]{1,0:T(8,128)} %get-tuple-element.76.refs_2_.refs_0_) | copy-start | bytes 1277956
  10.6 2.9 %copy-start.4 = (f32[192,256]{1,0:T(8,128)S(1)}, f32[192,256]{1,0:T(8,128)}, u32[]{:S(2)}) copy-start(f32[192,256]{1,0:T(8,128)} %get-tuple-element.77.refs_0_) | copy-start | bytes 589828
  10.6 13.9 %copy-start.2 = (f32[1,1,512,1024]{3,2,1,0:T(8,128)S(1)}, f32[1,1,512,1024]{3,2,1,0:T(8,128)}, u32[]{:S(2)}) copy-start(f32[1,1,512,1024]{3,2,1,0:T(8,128)} %param.3) | copy-start | bytes 6291460
  11.5 20.4 %collective-permute-start.3 = (f32[256,768]{1,0:T(8,128)S(1)}, f32[256,768]{1,0:T(8,128)S(1)}, u32[]{:S(2)}, u32[]{:S(2)}) collective-permute-start(f32[256,768]{1,0:T(8,128)S(1)} %get-tuple-element.83.refs_2_), channel_id=1, source_target_pairs={{0,16},{4,20},{8,24},{12,28},{16,0},{20,4},{24,8},{28,12},{1,17},{... | collective-permute-start | bytes 2359304 | tf_op jit(solution)/shard_map/ppermute | solution.py:20
  24.2 9.0 %collective-permute-start.4 = (f32[192,128]{1,0:T(8,128)S(1)}, f32[192,128]{1,0:T(8,128)S(1)}, u32[]{:S(2)}, u32[]{:S(2)}) collective-permute-start(f32[192,128]{1,0:T(8,128)S(1)} %get-tuple-element.85), channel_id=1, source_target_pairs={{0,2},{1,3},{2,0},{3,1},{4,6},{5,7},{6,4},{7,5},{8,10},{9,11},{10,... | collective-permute-start | bytes 294920 | tf_op jit(solution)/shard_map/ppermute | solution.py:20
  27.2 15.5 %collective-permute-start.2 = (f32[416,256]{1,0:T(8,128)S(1)}, f32[416,256]{1,0:T(8,128)S(1)}, u32[]{:S(2)}, u32[]{:S(2)}) collective-permute-start(f32[416,256]{1,0:T(8,128)S(1)} %get-tuple-element.82), channel_id=1, source_target_pairs={{0,16},{4,20},{8,24},{12,28},{16,0},{20,4},{24,8},{28,12},{1,17},{... | collective-permute-start | bytes 1277960 | tf_op jit(solution)/shard_map/ppermute | solution.py:20
  33.2 9.9 %collective-permute-start.5 = (f32[192,128]{1,0:T(8,128)S(1)}, f32[192,128]{1,0:T(8,128)S(1)}, u32[]{:S(2)}, u32[]{:S(2)}) collective-permute-start(f32[192,128]{1,0:T(8,128)S(1)} %get-tuple-element.89.refs_5_), channel_id=1, source_target_pairs={{0,16},{4,20},{8,24},{12,28},{16,0},{20,4},{24,8},{28,12},{1,17},{... | collective-permute-start | bytes 294920 | tf_op jit(solution)/shard_map/ppermute | solution.py:20
  34.1 19.5 %collective-permute-start.7 = (f32[256,256]{1,0:T(8,128)S(1)}, f32[256,256]{1,0:T(8,128)S(1)}, u32[]{:S(2)}, u32[]{:S(2)}) collective-permute-start(f32[256,256]{1,0:T(8,128)S(1)} %get-tuple-element.103.refs_0_), channel_id=1, source_target_pairs={{0,2},{1,3},{2,0},{3,1},{4,6},{5,7},{6,4},{7,5},{8,10},{9,11},{10,... | collective-permute-start | bytes 786440 | tf_op jit(solution)/shard_map/ppermute | solution.py:20
  35.9 17.7 %collective-permute-start.6 = (f32[256,256]{1,0:T(8,128)S(1)}, f32[256,256]{1,0:T(8,128)S(1)}, u32[]{:S(2)}, u32[]{:S(2)}) collective-permute-start(f32[256,256]{1,0:T(8,128)S(1)} %get-tuple-element.102.refs_2_), channel_id=1, source_target_pairs={{0,16},{4,20},{8,24},{12,28},{16,0},{20,4},{24,8},{28,12},{1,17},{... | collective-permute-start | bytes 786440 | tf_op jit(solution)/shard_map/ppermute | solution.py:20
  37.6 27.1 %collective-permute-start.9 = (f32[256,256]{1,0:T(8,128)S(1)}, f32[256,256]{1,0:T(8,128)S(1)}, u32[]{:S(2)}, u32[]{:S(2)}) collective-permute-start(f32[256,256]{1,0:T(8,128)S(1)} %get-tuple-element.109.refs_0_), channel_id=1, source_target_pairs={{0,2},{1,3},{2,0},{3,1},{4,6},{5,7},{6,4},{7,5},{8,10},{9,11},{10,... | collective-permute-start | bytes 786440 | tf_op jit(solution)/shard_map/ppermute | solution.py:20
  45.3 19.5 %collective-permute-start.8 = (f32[256,256]{1,0:T(8,128)S(1)}, f32[256,256]{1,0:T(8,128)S(1)}, u32[]{:S(2)}, u32[]{:S(2)}) collective-permute-start(f32[256,256]{1,0:T(8,128)S(1)} %get-tuple-element.108.refs_2_), channel_id=1, source_target_pairs={{0,16},{4,20},{8,24},{12,28},{16,0},{20,4},{24,8},{28,12},{1,17},{... | collective-permute-start | bytes 786440 | tf_op jit(solution)/shard_map/ppermute | solution.py:20
  54.9 21.1 %collective-permute-start.10 = (f32[256,256]{1,0:T(8,128)S(1)}, f32[256,256]{1,0:T(8,128)S(1)}, u32[]{:S(2)}, u32[]{:S(2)}) collective-permute-start(f32[256,256]{1,0:T(8,128)S(1)} %get-tuple-element.119.refs_0_), channel_id=1, source_target_pairs={{0,2},{1,3},{2,0},{3,1},{4,6},{5,7},{6,4},{7,5},{8,10},{9,11},{10,... | collective-permute-start | bytes 786440 | tf_op jit(solution)/shard_map/ppermute | solution.py:20
  66.1 17.0 %collective-permute-start.11 = (f32[256,256]{1,0:T(8,128)S(1)}, f32[256,256]{1,0:T(8,128)S(1)}, u32[]{:S(2)}, u32[]{:S(2)}) collective-permute-start(f32[256,256]{1,0:T(8,128)S(1)} %get-tuple-element.130.refs_0_), channel_id=1, source_target_pairs={{0,2},{1,3},{2,0},{3,1},{4,6},{5,7},{6,4},{7,5},{8,10},{9,11},{10,... | collective-permute-start | bytes 786440 | tf_op jit(solution)/shard_map/ppermute | solution.py:20
  66.2 18.8 %collective-permute-start.14 = (f32[256,256]{1,0:T(8,128)S(1)}, f32[256,256]{1,0:T(8,128)S(1)}, u32[]{:S(2)}, u32[]{:S(2)}) collective-permute-start(f32[256,256]{1,0:T(8,128)S(1)} %get-tuple-element.135.refs_9_), channel_id=1, source_target_pairs={{0,16},{4,20},{8,24},{12,28},{16,0},{20,4},{24,8},{28,12},{1,17},{... | collective-permute-start | bytes 786440 | tf_op jit(solution)/shard_map/ppermute | solution.py:20
  66.6 18.3 %collective-permute-start.13 = (f32[256,256]{1,0:T(8,128)S(1)}, f32[256,256]{1,0:T(8,128)S(1)}, u32[]{:S(2)}, u32[]{:S(2)}) collective-permute-start(f32[256,256]{1,0:T(8,128)S(1)} %get-tuple-element.134.refs_8_), channel_id=1, source_target_pairs={{0,16},{4,20},{8,24},{12,28},{16,0},{20,4},{24,8},{28,12},{1,17},{... | collective-permute-start | bytes 786440 | tf_op jit(solution)/shard_map/ppermute | solution.py:20
  76.1 8.9 %collective-permute-start.15 = (f32[256,256]{1,0:T(8,128)S(1)}, f32[256,256]{1,0:T(8,128)S(1)}, u32[]{:S(2)}, u32[]{:S(2)}) collective-permute-start(f32[256,256]{1,0:T(8,128)S(1)} %get-tuple-element.136.refs_10_), channel_id=1, source_target_pairs={{0,16},{4,20},{8,24},{12,28},{16,0},{20,4},{24,8},{28,12},{1,17},{... | collective-permute-start | bytes 786440 | tf_op jit(solution)/shard_map/ppermute | solution.py:20
  83.2 7.1 %collective-permute-start.12 = (f32[256,256]{1,0:T(8,128)S(1)}, f32[256,256]{1,0:T(8,128)S(1)}, u32[]{:S(2)}, u32[]{:S(2)}) collective-permute-start(f32[256,256]{1,0:T(8,128)S(1)} %get-tuple-element.132.refs_8_), channel_id=1, source_target_pairs={{0,16},{4,20},{8,24},{12,28},{16,0},{20,4},{24,8},{28,12},{1,17},{... | collective-permute-start | bytes 786440 | tf_op jit(solution)/shard_map/ppermute | solution.py:20

commit v4 on v3

--- a/solution.py
+++ b/solution.py
@@ -568,6 +568,7 @@
     (v1,), start1 = middles([1], 0, own_a, far_a)
     z1 = exchange(v1, "gy")
     own_b, far_b = sides(bases[2], widths[2])
+    own_c, far_c = sides(bases[3], 2 * unit)
     known_b = known_half("known", known_kernel, 2, [], [], [])
     across_far, s_own, s_off, s_far = call(
         "build",
@@ -583,7 +584,6 @@
         across,
         scratch=[pltpu.VMEM((n, n), F32)],
     )
-    own_c, far_c = sides(bases[3], 2 * unit)
     head, reach, rest = call("head", head_kernel, [array(h, h)] * 3, s_own)
     w0, w0_far = total(v0, z0, "opening")
     (v2,), start2 = middles([2], bases[2], own_b, far_b)

time: 93.7 us -> 92.9 us (level)
  waiting for transfers between devices: 12 us -> 8.26 us
  starting transfers between devices: 20.2 us -> 23.2 us
    ppermute x16, waiting for transfers between devices: 12 us -> 8.26 us  [exchange(): return lax.ppermute(block, axis, [(i, i ^ half) for i in range(2 * half)])]
    ppermute x16, starting transfers between devices: 20.2 us -> 23.2 us  [exchange(): return lax.ppermute(block, axis, [(i, i ^ half) for i in range(2 * half)])]
where the time goes in v4:
time: 92.9 us; the launch traced here: 92.7 us
  Pallas kernels  57.9 us (62%)
  starting transfers between devices  23.2 us (25%)
  waiting for transfers between devices  8.26 us (9%)
  local copies, waits for them, and re-layouts  2.29 us (2%)
  between operations  1.08 us (1%)
    pallas_call x25, Pallas kernels, __call__(): pl.pallas_call(body, out_shape=list(outs) + [array(8, LANES)], in_specs=l...  57.9 us
    ppermute x16, starting transfers between devices, exchange(): return lax.ppermute(block, axis, [(i, i ^ half) for i in range(2 * half)])  23.2 us
    ppermute x16, waiting for transfers between devices, exchange(): return lax.ppermute(block, axis, [(i, i ^ half) for i in range(2 * half)])  8.26 us
    unnamed x12, local copies, waits for them, and re-layouts  2.29 us
  transfers between devices with their start and end apart: 16, of which 6 were waited for; matrix products, arithmetic and copies ran while one was open for 0% of the time, Pallas kernels for 57%

profile of v4, /device:TPU:0, one launch (start us, length us, event | category | flops | bytes accessed | tf_op | source)
XLA Modules:
  0.0 92.7 jit_solution(7157467131538776880)
XLA Ops:
  0.6 0.0 copy-start
  0.6 2.1 %blocks.1 = (f32[192,256]{1,0:T(8,128)}, f32[416,256]{1,0:T(8,128)}, f32[8,128]{1,0:T(8,128)}) custom-call(f32[1024,1024]{1,0:T(8,128)} %bitcast.4), custom_call_target="tpu_custom_call" | custom-call | flops 5000000 | bytes 15000 | tf_op jit(solution)/shard_map/blocks/pallas_call | solution.py:459
  2.7 4.1 %collective-permute-start = (f32[416,256]{1,0:T(8,128)}, f32[416,256]{1,0:T(8,128)S(1)}, u32[]{:S(2)}, u32[]{:S(2)}) collective-permute-start(f32[416,256]{1,0:T(8,128)} %get-tuple-element.76.refs_2_.refs_0_), channel_id=1, source_target_pairs={{0,2},{1,3},{2,0},{3,1},{4,6},{5,7},{6,4},{7,5},{8,10},{9,11},{10,... | collective-permute-start | bytes 1277960 | tf_op jit(solution)/shard_map/ppermute | solution.py:20
  6.8 1.5 %collective-permute-start.1 = (f32[192,256]{1,0:T(8,128)}, f32[192,256]{1,0:T(8,128)S(1)}, u32[]{:S(2)}, u32[]{:S(2)}) collective-permute-start(f32[192,256]{1,0:T(8,128)} %get-tuple-element.77.refs_0_), channel_id=1, source_target_pairs={{0,16},{4,20},{8,24},{12,28},{16,0},{20,4},{24,8},{28,12},{1,17},{... | collective-permute-start | bytes 589832 | tf_op jit(solution)/shard_map/ppermute | solution.py:20
  8.3 0.0 copy-done
  8.3 0.0 copy-start.1
  8.4 1.6 %copy-done.1 = f32[1,1,512,1024]{3,2,1,0:T(8,128)S(1)} copy-done((f32[1,1,512,1024]{3,2,1,0:T(8,128)S(1)}, f32[1,1,512,1024]{3,2,1,0:T(8,128)}, u32[]{:S(2)}) %copy-start.1) | copy-done | bytes 2097176
  9.9 0.0 copy-start.5
  9.9 0.7 copy-done.5
  10.6 0.0 copy-start.3
  10.6 0.0 copy-start.4
  10.6 0.0 copy-start.2
  10.6 0.8 side.3
  11.5 0.6 collective-permute-start.3
  12.0 1.4 %collective-permute-done.1.refs_1_ = f32[192,256]{1,0:T(8,128)S(1)} collective-permute-done((f32[192,256]{1,0:T(8,128)}, f32[192,256]{1,0:T(8,128)S(1)}, u32[]{:S(2)}, u32[]{:S(2)}) %collective-permute-start.1) | collective-permute-done | bytes 196640 | tf_op jit(solution)/shard_map/ppermute | solution.py:20
  13.5 0.0 copy-done.3
  13.5 0.0 copy-done.4
  13.5 10.7 %first.1 = (f32[256,256]{1,0:T(8,128)S(1)}, f32[256,256]{1,0:T(8,128)S(1)}, f32[192,128]{1,0:T(8,128)S(1)}, f32[8,128]{1,0:T(8,128)S(1)}) custom-call(f32[192,256]{1,0:T(8,128)S(1)} %copy-done.4, f32[192,256]{1,0:T(8,128)S(1)} %collective-permute-done.1.refs_1_, f32[416,256]{1,0:T(8,128)S(1)} %copy-done.3, f32[8,128]{1,0:T(8,128)S(1)} %get-tuple-element.79.refs_3_), custom_call_target="tpu_custom_call" | custom-call | flops 5000000 | bytes 15000 | tf_op jit(solution)/shard_map/first/pallas_call | solution.py:459
  24.2 0.3 collective-permute-start.4
  24.5 0.0 copy-done.2
  24.5 2.6 %known_and_data.1 = (f32[512,1024]{1,0:T(8,128)S(1)}, bf16[512,512]{1,0:T(8,128)(2,1)S(1)}, bf16[512,512]{1,0:T(8,128)(2,1)S(1)}, f32[1024,1024]{1,0:T(8,128)}, ...) custom-call(f32[1024,1024]{1,0:T(8,128)S(1)} %bitcast.6, f32[512,1024]{1,0:T(8,128)S(1)} %bitcast.15, ...), custom_call_target="tpu_custom_call" | custom-call | flops 5000000 | bytes 15000 | tf_op jit(solution)/shard_map/known_and_data/pallas_call | solution.py:459
  27.2 0.0 collective-permute-done.refs_1_
  27.2 2.3 %collective-permute-start.2 = (f32[416,256]{1,0:T(8,128)S(1)}, f32[416,256]{1,0:T(8,128)S(1)}, u32[]{:S(2)}, u32[]{:S(2)}) collective-permute-start(f32[416,256]{1,0:T(8,128)S(1)} %get-tuple-element.82), channel_id=1, source_target_pairs={{0,16},{4,20},{8,24},{12,28},{16,0},{20,4},{24,8},{28,12},{1,17},{... | collective-permute-start | bytes 1277960 | tf_op jit(solution)/shard_map/ppermute | solution.py:20
  29.6 2.3 %collective-permute-done.3.refs_3_ = f32[256,768]{1,0:T(8,128)S(1)} collective-permute-done((f32[256,768]{1,0:T(8,128)S(1)}, f32[256,768]{1,0:T(8,128)S(1)}, u32[]{:S(2)}, u32[]{:S(2)}) %collective-permute-start.3) | collective-permute-done | bytes 786464 | tf_op jit(solution)/shard_map/ppermute | solution.py:20
  31.9 1.3 %middle.4 = (f32[256,256]{1,0:T(8,128)S(1)}, f32[256,256]{1,0:T(8,128)S(1)}, f32[8,128]{1,0:T(8,128)S(1)}) custom-call(f32[1024,1024]{1,0:T(8,128)S(1)} %bitcast.7, f32[512,1024]{1,0:T(8,128)S(1)} %bitcast.16, f32[256,768]{1,0:T(8,128)S(1)} %get-tuple-element.83.refs_2_, f32[256,768]{1,0:T(8,128)S(1)} %collective-permute-done.3.refs_3_, ...), custom_call_target="tpu_custom_call" | custom-call | flops 5000000 | bytes 15000 | tf_op jit(solution)/shard_map/middle/pallas_call | solution.py:459
  33.2 0.5 collective-permute-start.7
  33.7 0.0 collective-permute-done.4.refs_0_
  33.7 0.5 collective-permute-start.5
  34.2 1.3 %middle.5 = (f32[256,256]{1,0:T(8,128)S(1)}, f32[256,256]{1,0:T(8,128)S(1)}, f32[8,128]{1,0:T(8,128)S(1)}) custom-call(f32[1024,1024]{1,0:T(8,128)S(1)} %bitcast.8, f32[512,1024]{1,0:T(8,128)S(1)} %bitcast.17, f32[256,768]{1,0:T(8,128)S(1)} %get-tuple-element.83.refs_2_, f32[256,768]{1,0:T(8,128)S(1)} %collective-permute-done.3.refs_3_, ...), custom_call_target="tpu_custom_call" | custom-call | flops 5000000 | bytes 15000 | tf_op jit(solution)/shard_map/middle/pallas_call | solution.py:459
  35.4 0.6 side.4
  36.0 1.7 %collective-permute-start.6 = (f32[256,256]{1,0:T(8,128)S(1)}, f32[256,256]{1,0:T(8,128)S(1)}, u32[]{:S(2)}, u32[]{:S(2)}) collective-permute-start(f32[256,256]{1,0:T(8,128)S(1)} %get-tuple-element.102.refs_2_), channel_id=1, source_target_pairs={{0,16},{4,20},{8,24},{12,28},{16,0},{20,4},{24,8},{28,12},{1,17},{... | collective-permute-start | bytes 786440 | tf_op jit(solution)/shard_map/ppermute | solution.py:20
  37.7 2.5 %collective-permute-start.9 = (f32[256,256]{1,0:T(8,128)S(1)}, f32[256,256]{1,0:T(8,128)S(1)}, u32[]{:S(2)}, u32[]{:S(2)}) collective-permute-start(f32[256,256]{1,0:T(8,128)S(1)} %get-tuple-element.109.refs_0_), channel_id=1, source_target_pairs={{0,2},{1,3},{2,0},{3,1},{4,6},{5,7},{6,4},{7,5},{8,10},{9,11},{10,... | collective-permute-start | bytes 786440 | tf_op jit(solution)/shard_map/ppermute | solution.py:20
  40.2 0.5 side.5
  40.7 0.3 collective-permute-done.2.refs_2_
  41.0 1.3 %collective-permute-start.8 = (f32[256,256]{1,0:T(8,128)S(1)}, f32[256,256]{1,0:T(8,128)S(1)}, u32[]{:S(2)}, u32[]{:S(2)}) collective-permute-start(f32[256,256]{1,0:T(8,128)S(1)} %get-tuple-element.108.refs_2_), channel_id=1, source_target_pairs={{0,16},{4,20},{8,24},{12,28},{16,0},{20,4},{24,8},{28,12},{1,17},{... | collective-permute-start | bytes 786440 | tf_op jit(solution)/shard_map/ppermute | solution.py:20
  42.3 2.6 %known.1 = (f32[512,1024]{1,0:T(8,128)S(1)}, bf16[512,512]{1,0:T(8,128)(2,1)S(1)}, bf16[512,512]{1,0:T(8,128)(2,1)S(1)}, f32[8,128]{1,0:T(8,128)S(1)}) custom-call(f32[1024,1024]{1,0:T(8,128)S(1)} %bitcast.11, f32[512,1024]{1,0:T(8,128)S(1)} %bitcast.20, f32[8,128]{1,0:T(8,128)S(1)} %get-tuple-element.93.refs_2_), custom_call_target="tpu_custom_call" | custom-call | flops 5000000 | bytes 15000 | tf_op jit(solution)/shard_map/known/pallas_call | solution.py:459
  44.9 0.0 collective-permute-done.5.refs_6_
  44.9 1.6 %build.1 = (f32[256,256]{1,0:T(8,128)S(1)}, f32[256,256]{1,0:T(8,128)S(1)}, f32[256,256]{1,0:T(8,128)S(1)}, f32[256,256]{1,0:T(8,128)S(1)}, f32[8,128]{1,0:T(8,128)S(1)}) custom-call(f32[416,256]{1,0:T(8,128)S(1)} %copy-done.3, f32[416,256]{1,0:T(8,128)S(1)} %collective-permute-done.refs_1_, f32[416,256]{1,0:T(8,128)S(1)} %collective-permute-done.2.refs_2_, ...), custom_call_target="tpu_custom_call" | custom-call | flops 700000000 | bytes 2100000 | tf_op jit(solution)/shard_map/build/pallas_call | solution.py:459
  46.6 5.1 %head.2 = (f32[128,128]{1,0:T(8,128)S(1)}, f32[128,128]{1,0:T(8,128)S(1)}, f32[128,128]{1,0:T(8,128)S(1)}, f32[8,128]{1,0:T(8,128)S(1)}) custom-call(f32[256,256]{1,0:T(8,128)S(1)} %get-tuple-element.95.refs_0_, f32[8,128]{1,0:T(8,128)S(1)} %get-tuple-element.96.refs_1_), custom_call_target="tpu_custom_call" | custom-call | flops 5000000 | bytes 15000 | tf_op jit(solution)/shard_map/head/pallas_call | solution.py:459
  51.7 0.0 collective-permute-done.7.refs_1_
  51.8 0.0 collective-permute-done.6.refs_3_
  51.8 1.3 %middle.6 = (f32[256,256]{1,0:T(8,128)S(1)}, f32[256,256]{1,0:T(8,128)S(1)}, f32[8,128]{1,0:T(8,128)S(1)}) custom-call(f32[1024,1024]{1,0:T(8,128)S(1)} %bitcast.12, f32[512,1024]{1,0:T(8,128)S(1)} %bitcast.21, f32[256,256]{1,0:T(8,128)S(1)} %get-tuple-element.102.refs_2_, f32[256,256]{1,0:T(8,128)S(1)} %collective-permute-done.6.refs_3_, ...), custom_call_target="tpu_custom_call" | custom-call | flops 5000000 | bytes 15000 | tf_op jit(solution)/shard_map/middle/pallas_call | solution.py:459
  53.1 2.8 %collective-permute-start.10 = (f32[256,256]{1,0:T(8,128)S(1)}, f32[256,256]{1,0:T(8,128)S(1)}, u32[]{:S(2)}, u32[]{:S(2)}) collective-permute-start(f32[256,256]{1,0:T(8,128)S(1)} %get-tuple-element.119.refs_0_), channel_id=1, source_target_pairs={{0,2},{1,3},{2,0},{3,1},{4,6},{5,7},{6,4},{7,5},{8,10},{9,11},{10,... | collective-permute-start | bytes 786440 | tf_op jit(solution)/shard_map/ppermute | solution.py:20
  55.9 5.8 %turn.1 = (f32[256,256]{1,0:T(8,128)S(1)}, f32[256,256]{1,0:T(8,128)S(1)}, f32[256,256]{1,0:T(8,128)S(1)}, f32[8,128]{1,0:T(8,128)S(1)}) custom-call(f32[128,128]{1,0:T(8,128)S(1)} %get-tuple-element.97.refs_0_, f32[128,128]{1,0:T(8,128)S(1)} %get-tuple-element.98.refs_1_, f32[128,128]{1,0:T(8,128)S(1)} %get-tuple-element.99.refs_2_, ...), custom_call_target="tpu_custom_call" | custom-call | flops 5000000 | bytes 15000 | tf_op jit(solution)/shard_map/turn/pallas_call | solution.py:459
  61.7 1.0 %collective-permute-done.9.refs_1_ = f32[256,256]{1,0:T(8,128)S(1)} collective-permute-done((f32[256,256]{1,0:T(8,128)S(1)}, f32[256,256]{1,0:T(8,128)S(1)}, u32[]{:S(2)}, u32[]{:S(2)}) %collective-permute-start.9) | collective-permute-done | bytes 262176 | tf_op jit(solution)/shard_map/ppermute | solution.py:20
  62.8 0.0 collective-permute-done.8.refs_3_
  62.8 1.3 %middle.7 = (f32[256,256]{1,0:T(8,128)S(1)}, f32[256,256]{1,0:T(8,128)S(1)}, f32[8,128]{1,0:T(8,128)S(1)}) custom-call(f32[1024,1024]{1,0:T(8,128)S(1)} %bitcast.13, f32[512,1024]{1,0:T(8,128)S(1)} %bitcast.22, f32[256,256]{1,0:T(8,128)S(1)} %get-tuple-element.108.refs_2_, f32[256,256]{1,0:T(8,128)S(1)} %collective-permute-done.8.refs_3_, ...), custom_call_target="tpu_custom_call" | custom-call | flops 5000000 | bytes 15000 | tf_op jit(solution)/shard_map/middle/pallas_call | solution.py:459
  64.1 0.1 collective-permute-start.11
  64.2 2.4 %collective-permute-start.13 = (f32[256,256]{1,0:T(8,128)S(1)}, f32[256,256]{1,0:T(8,128)S(1)}, u32[]{:S(2)}, u32[]{:S(2)}) collective-permute-start(f32[256,256]{1,0:T(8,128)S(1)} %get-tuple-element.134.refs_8_), channel_id=1, source_target_pairs={{0,16},{4,20},{8,24},{12,28},{16,0},{20,4},{24,8},{28,12},{1,17},{... | collective-permute-start | bytes 786440 | tf_op jit(solution)/shard_map/ppermute | solution.py:20
  66.5 0.1 collective-permute-start.14
  66.6 5.1 %head.3 = (f32[128,128]{1,0:T(8,128)S(1)}, f32[128,128]{1,0:T(8,128)S(1)}, f32[128,128]{1,0:T(8,128)S(1)}, f32[8,128]{1,0:T(8,128)S(1)}) custom-call(f32[256,256]{1,0:T(8,128)S(1)} %get-tuple-element.107.refs_0_, f32[8,128]{1,0:T(8,128)S(1)} %get-tuple-element.112.refs_1_), custom_call_target="tpu_custom_call" | custom-call | flops 5000000 | bytes 15000 | tf_op jit(solution)/shard_map/head/pallas_call | solution.py:459
  71.7 2.2 %collective-permute-done.10.refs_1_ = f32[256,256]{1,0:T(8,128)S(1)} collective-permute-done((f32[256,256]{1,0:T(8,128)S(1)}, f32[256,256]{1,0:T(8,128)S(1)}, u32[]{:S(2)}, u32[]{:S(2)}) %collective-permute-start.10) | collective-permute-done | bytes 262176 | tf_op jit(solution)/shard_map/ppermute | solution.py:20
  74.0 2.4 %collective-permute-start.15 = (f32[256,256]{1,0:T(8,128)S(1)}, f32[256,256]{1,0:T(8,128)S(1)}, u32[]{:S(2)}, u32[]{:S(2)}) collective-permute-start(f32[256,256]{1,0:T(8,128)S(1)} %get-tuple-element.136.refs_10_), channel_id=1, source_target_pairs={{0,16},{4,20},{8,24},{12,28},{16,0},{20,4},{24,8},{28,12},{1,17},{... | collective-permute-start | bytes 786440 | tf_op jit(solution)/shard_map/ppermute | solution.py:20
  76.4 6.6 %tail.1 = (bf16[512,512]{1,0:T(8,128)(2,1)S(1)}, bf16[512,512]{1,0:T(8,128)(2,1)S(1)}, f32[8,128]{1,0:T(8,128)S(1)}) custom-call(f32[128,128]{1,0:T(8,128)S(1)} %get-tuple-element.113.refs_0_, f32[128,128]{1,0:T(8,128)S(1)} %get-tuple-element.114.refs_1_, f32[128,128]{1,0:T(8,128)S(1)} %get-tuple-element.115.refs_2_, ...), custom_call_target="tpu_custom_call" | custom-call | flops 5000000 | bytes 15000 | tf_op jit(solution)/shard_map/tail/pallas_call | solution.py:459
  83.0 0.0 collective-permute-done.11.refs_1_
  83.1 0.1 collective-permute-start.12
  83.2 0.0 collective-permute-done.13.refs_0_
  83.2 0.0 collective-permute-done.14.refs_12_
  83.2 0.0 collective-permute-done.15.refs_13_
  83.2 5.3 %last.2 = (f32[1024,1024]{1,0:T(8,128)}, f32[1024,1024]{1,0:T(8,128)}, f32[8,128]{1,0:T(8,128)S(1)}) custom-call(bf16[512,512]{1,0:T(8,128)(2,1)S(1)} %get-tuple-element.122.refs_0_, bf16[512,512]{1,0:T(8,128)(2,1)S(1)} %get-tuple-element.123.refs_1_, f32[512,1024]{1,0:T(8,128)S(1)} %get-tuple-element.124.refs_2_, ...), custom_call_target="tpu_custom_call", output_to_operand_aliasing={{1}: (17, {}), {0}: (18, {})} | custom-call | flops 5000000 | bytes 15000 | tf_op jit(solution)/shard_map/last/pallas_call | solution.py:459
  88.5 1.0 %collective-permute-done.12.refs_9_ = f32[256,256]{1,0:T(8,128)S(1)} collective-permute-done((f32[256,256]{1,0:T(8,128)S(1)}, f32[256,256]{1,0:T(8,128)S(1)}, u32[]{:S(2)}, u32[]{:S(2)}) %collective-permute-start.12) | collective-permute-done | bytes 262176 | tf_op jit(solution)/shard_map/ppermute | solution.py:20
  89.5 3.0 %last.3 = (f32[1024,1024]{1,0:T(8,128)}, f32[1024,1024]{1,0:T(8,128)}, f32[8,128]{1,0:T(8,128)}) custom-call(bf16[512,512]{1,0:T(8,128)(2,1)S(1)} %get-tuple-element.122.refs_0_, bf16[512,512]{1,0:T(8,128)(2,1)S(1)} %get-tuple-element.123.refs_1_, f32[512,1024]{1,0:T(8,128)S(1)} %get-tuple-element.124.refs_2_, ...), custom_call_target="tpu_custom_call", output_to_operand_aliasing={{1}: (11, {}), {0}: (12, {})} | custom-call | flops 5000000 | bytes 15000 | tf_op jit(solution)/shard_map/last/pallas_call | solution.py:459
  (7 shorter events, 0.2 us)
Async XLA Ops:
  0.6 7.7 %copy-start = (f32[1,1,1024,1024]{3,2,1,0:T(8,128)S(1)}, f32[1,1,1024,1024]{3,2,1,0:T(8,128)}, u32[]{:S(2)}) copy-start(f32[1,1,1024,1024]{3,2,1,0:T(8,128)} %param.2) | copy-start | bytes 12582916
  2.7 24.4 %collective-permute-start = (f32[416,256]{1,0:T(8,128)}, f32[416,256]{1,0:T(8,128)S(1)}, u32[]{:S(2)}, u32[]{:S(2)}) collective-permute-start(f32[416,256]{1,0:T(8,128)} %get-tuple-element.76.refs_2_.refs_0_), channel_id=1, source_target_pairs={{0,2},{1,3},{2,0},{3,1},{4,6},{5,7},{6,4},{7,5},{8,10},{9,11},{10,... | collective-permute-start | bytes 1277960 | tf_op jit(solution)/shard_map/ppermute | solution.py:20
  6.8 6.7 %collective-permute-start.1 = (f32[192,256]{1,0:T(8,128)}, f32[192,256]{1,0:T(8,128)S(1)}, u32[]{:S(2)}, u32[]{:S(2)}) collective-permute-start(f32[192,256]{1,0:T(8,128)} %get-tuple-element.77.refs_0_), channel_id=1, source_target_pairs={{0,16},{4,20},{8,24},{12,28},{16,0},{20,4},{24,8},{28,12},{1,17},{... | collective-permute-start | bytes 589832 | tf_op jit(solution)/shard_map/ppermute | solution.py:20
  8.3 1.6 %copy-start.1 = (f32[1,1,512,1024]{3,2,1,0:T(8,128)S(1)}, f32[1,1,512,1024]{3,2,1,0:T(8,128)}, u32[]{:S(2)}) copy-start(f32[1,1,512,1024]{3,2,1,0:T(8,128)} %param.3) | copy-start | bytes 6291460
  9.9 0.7 copy-start.5
  10.6 2.9 %copy-start.3 = (f32[416,256]{1,0:T(8,128)S(1)}, f32[416,256]{1,0:T(8,128)}, u32[]{:S(2)}) copy-start(f32[416,256]{1,0:T(8,128)} %get-tuple-element.76.refs_2_.refs_0_) | copy-start | bytes 1277956
  10.6 2.9 %copy-start.4 = (f32[192,256]{1,0:T(8,128)S(1)}, f32[192,256]{1,0:T(8,128)}, u32[]{:S(2)}) copy-start(f32[192,256]{1,0:T(8,128)} %get-tuple-element.77.refs_0_) | copy-start | bytes 589828
  10.6 13.9 %copy-start.2 = (f32[1,1,512,1024]{3,2,1,0:T(8,128)S(1)}, f32[1,1,512,1024]{3,2,1,0:T(8,128)}, u32[]{:S(2)}) copy-start(f32[1,1,512,1024]{3,2,1,0:T(8,128)} %param.3) | copy-start | bytes 6291460
  11.5 20.4 %collective-permute-start.3 = (f32[256,768]{1,0:T(8,128)S(1)}, f32[256,768]{1,0:T(8,128)S(1)}, u32[]{:S(2)}, u32[]{:S(2)}) collective-permute-start(f32[256,768]{1,0:T(8,128)S(1)} %get-tuple-element.83.refs_2_), channel_id=1, source_target_pairs={{0,16},{4,20},{8,24},{12,28},{16,0},{20,4},{24,8},{28,12},{1,17},{... | collective-permute-start | bytes 2359304 | tf_op jit(solution)/shard_map/ppermute | solution.py:20
  24.2 9.5 %collective-permute-start.4 = (f32[192,128]{1,0:T(8,128)S(1)}, f32[192,128]{1,0:T(8,128)S(1)}, u32[]{:S(2)}, u32[]{:S(2)}) collective-permute-start(f32[192,128]{1,0:T(8,128)S(1)} %get-tuple-element.85), channel_id=1, source_target_pairs={{0,2},{1,3},{2,0},{3,1},{4,6},{5,7},{6,4},{7,5},{8,10},{9,11},{10,... | collective-permute-start | bytes 294920 | tf_op jit(solution)/shard_map/ppermute | solution.py:20
  27.2 13.8 %collective-permute-start.2 = (f32[416,256]{1,0:T(8,128)S(1)}, f32[416,256]{1,0:T(8,128)S(1)}, u32[]{:S(2)}, u32[]{:S(2)}) collective-permute-start(f32[416,256]{1,0:T(8,128)S(1)} %get-tuple-element.82), channel_id=1, source_target_pairs={{0,16},{4,20},{8,24},{12,28},{16,0},{20,4},{24,8},{28,12},{1,17},{... | collective-permute-start | bytes 1277960 | tf_op jit(solution)/shard_map/ppermute | solution.py:20
  33.2 18.5 %collective-permute-start.7 = (f32[256,256]{1,0:T(8,128)S(1)}, f32[256,256]{1,0:T(8,128)S(1)}, u32[]{:S(2)}, u32[]{:S(2)}) collective-permute-start(f32[256,256]{1,0:T(8,128)S(1)} %get-tuple-element.103.refs_0_), channel_id=1, source_target_pairs={{0,2},{1,3},{2,0},{3,1},{4,6},{5,7},{6,4},{7,5},{8,10},{9,11},{10,... | collective-permute-start | bytes 786440 | tf_op jit(solution)/shard_map/ppermute | solution.py:20
  33.7 11.2 %collective-permute-start.5 = (f32[192,128]{1,0:T(8,128)S(1)}, f32[192,128]{1,0:T(8,128)S(1)}, u32[]{:S(2)}, u32[]{:S(2)}) collective-permute-start(f32[192,128]{1,0:T(8,128)S(1)} %get-tuple-element.89.refs_5_), channel_id=1, source_target_pairs={{0,16},{4,20},{8,24},{12,28},{16,0},{20,4},{24,8},{28,12},{1,17},{... | collective-permute-start | bytes 294920 | tf_op jit(solution)/shard_map/ppermute | solution.py:20
  36.0 15.8 %collective-permute-start.6 = (f32[256,256]{1,0:T(8,128)S(1)}, f32[256,256]{1,0:T(8,128)S(1)}, u32[]{:S(2)}, u32[]{:S(2)}) collective-permute-start(f32[256,256]{1,0:T(8,128)S(1)} %get-tuple-element.102.refs_2_), channel_id=1, source_target_pairs={{0,16},{4,20},{8,24},{12,28},{16,0},{20,4},{24,8},{28,12},{1,17},{... | collective-permute-start | bytes 786440 | tf_op jit(solution)/shard_map/ppermute | solution.py:20
  37.7 25.0 %collective-permute-start.9 = (f32[256,256]{1,0:T(8,128)S(1)}, f32[256,256]{1,0:T(8,128)S(1)}, u32[]{:S(2)}, u32[]{:S(2)}) collective-permute-start(f32[256,256]{1,0:T(8,128)S(1)} %get-tuple-element.109.refs_0_), channel_id=1, source_target_pairs={{0,2},{1,3},{2,0},{3,1},{4,6},{5,7},{6,4},{7,5},{8,10},{9,11},{10,... | collective-permute-start | bytes 786440 | tf_op jit(solution)/shard_map/ppermute | solution.py:20
  41.0 21.7 %collective-permute-start.8 = (f32[256,256]{1,0:T(8,128)S(1)}, f32[256,256]{1,0:T(8,128)S(1)}, u32[]{:S(2)}, u32[]{:S(2)}) collective-permute-start(f32[256,256]{1,0:T(8,128)S(1)} %get-tuple-element.108.refs_2_), channel_id=1, source_target_pairs={{0,16},{4,20},{8,24},{12,28},{16,0},{20,4},{24,8},{28,12},{1,17},{... | collective-permute-start | bytes 786440 | tf_op jit(solution)/shard_map/ppermute | solution.py:20
  53.1 20.9 %collective-permute-start.10 = (f32[256,256]{1,0:T(8,128)S(1)}, f32[256,256]{1,0:T(8,128)S(1)}, u32[]{:S(2)}, u32[]{:S(2)}) collective-permute-start(f32[256,256]{1,0:T(8,128)S(1)} %get-tuple-element.119.refs_0_), channel_id=1, source_target_pairs={{0,2},{1,3},{2,0},{3,1},{4,6},{5,7},{6,4},{7,5},{8,10},{9,11},{10,... | collective-permute-start | bytes 786440 | tf_op jit(solution)/shard_map/ppermute | solution.py:20
  64.1 18.9 %collective-permute-start.11 = (f32[256,256]{1,0:T(8,128)S(1)}, f32[256,256]{1,0:T(8,128)S(1)}, u32[]{:S(2)}, u32[]{:S(2)}) collective-permute-start(f32[256,256]{1,0:T(8,128)S(1)} %get-tuple-element.130.refs_0_), channel_id=1, source_target_pairs={{0,2},{1,3},{2,0},{3,1},{4,6},{5,7},{6,4},{7,5},{8,10},{9,11},{10,... | collective-permute-start | bytes 786440 | tf_op jit(solution)/shard_map/ppermute | solution.py:20
  64.2 19.0 %collective-permute-start.13 = (f32[256,256]{1,0:T(8,128)S(1)}, f32[256,256]{1,0:T(8,128)S(1)}, u32[]{:S(2)}, u32[]{:S(2)}) collective-permute-start(f32[256,256]{1,0:T(8,128)S(1)} %get-tuple-element.134.refs_8_), channel_id=1, source_target_pairs={{0,16},{4,20},{8,24},{12,28},{16,0},{20,4},{24,8},{28,12},{1,17},{... | collective-permute-start | bytes 786440 | tf_op jit(solution)/shard_map/ppermute | solution.py:20
  66.5 16.7 %collective-permute-start.14 = (f32[256,256]{1,0:T(8,128)S(1)}, f32[256,256]{1,0:T(8,128)S(1)}, u32[]{:S(2)}, u32[]{:S(2)}) collective-permute-start(f32[256,256]{1,0:T(8,128)S(1)} %get-tuple-element.135.refs_9_), channel_id=1, source_target_pairs={{0,16},{4,20},{8,24},{12,28},{16,0},{20,4},{24,8},{28,12},{1,17},{... | collective-permute-start | bytes 786440 | tf_op jit(solution)/shard_map/ppermute | solution.py:20
  74.0 9.2 %collective-permute-start.15 = (f32[256,256]{1,0:T(8,128)S(1)}, f32[256,256]{1,0:T(8,128)S(1)}, u32[]{:S(2)}, u32[]{:S(2)}) collective-permute-start(f32[256,256]{1,0:T(8,128)S(1)} %get-tuple-element.136.refs_10_), channel_id=1, source_target_pairs={{0,16},{4,20},{8,24},{12,28},{16,0},{20,4},{24,8},{28,12},{1,17},{... | collective-permute-start | bytes 786440 | tf_op jit(solution)/shard_map/ppermute | solution.py:20
  83.1 6.4 %collective-permute-start.12 = (f32[256,256]{1,0:T(8,128)S(1)}, f32[256,256]{1,0:T(8,128)S(1)}, u32[]{:S(2)}, u32[]{:S(2)}) collective-permute-start(f32[256,256]{1,0:T(8,128)S(1)} %get-tuple-element.132.refs_8_), channel_id=1, source_target_pairs={{0,16},{4,20},{8,24},{12,28},{16,0},{20,4},{24,8},{28,12},{1,17},{... | collective-permute-start | bytes 786440 | tf_op jit(solution)/shard_map/ppermute | solution.py:20
